TPU v7x, 256 devices: a whole 4x4x8 slice. The times are simulated.
256 devices in a mesh: grp: 2 (over core), img: 16 (over x_hi, z), tp: 8 (over x_lo, y).
Axes of the slice: x: 4 (x_hi: 2, x_lo: 2; x = x_hi * 2 + x_lo), y: 4, z: 8, core: 2. Of those that a mesh axis runs over, the one named last changes fastest.
Arguments:
- features: bfloat16 [2, 8192, 256], P('grp', 'img'), may hold values from -7 to 7
- masters: float32 [2, 65536, 256], P('grp', ('img', 'tp')), may hold values from -7 to 7
- patch_mask: int32 [8192], P('img'), may hold values from 0 to 1, as said below
Outputs:
- updated: float32 [2, 65536, 256], P('grp', ('img', 'tp'))
Inputs may be any that keep to these rules, and one draw needn't show every extreme that they name: `patch_mask`: 1 marks a masked student patch; some crops have no masked patch.
All inputs are finite; a program needn't handle non-finite values.
Results may differ from a plain program's by a relative error of at most 0.0045.
Values may be sent and summed in bfloat16 or wider, within the bound.
No kernel may reach another device: no remote copies, remote signals or barrier semaphores. Data moves between devices by JAX's collectives and lax.ppermute only.
A program may use at most 128 MiB of HBM per device.

v0:
```python
import jax
import jax.numpy as jnp
from jax import lax
from jax.sharding import PartitionSpec as P

PROTOS = 65536
PATCHES = 256
BALANCE_STEPS = 3


MOMENTUM = 0.994
TEACHER_TEMP = 0.07
STUDENT_TEMP = 0.1
EPS = 1e-06


def shifted(block, axis, distance):
    devices = range(lax.axis_size(axis))
    route = [(i - distance, i) for i in devices if i - distance in devices]
    return lax.ppermute(block, axis, route)


def unit_rows(values):
    values = values.astype(jnp.float32)
    return (values / jnp.sqrt(jnp.sum(values * values, -1, keepdims=True) + EPS)).astype(
        jnp.bfloat16
    )


def per_device(features, masters, patch_mask):
    teacher = lax.axis_index("grp") == 1
    own_master = masters[0]
    partner = shifted(own_master, "grp", 1)
    blended = MOMENTUM * partner + (1.0 - MOMENTUM) * own_master
    teacher_blend = jnp.where(teacher, MOMENTUM * own_master + (1.0 - MOMENTUM) * partner, blended)
    blended = jnp.where(teacher, teacher_blend, own_master)
    proto_unit = unit_rows(blended)
    token_unit = unit_rows(features[0])
    inverse_temp = jnp.where(teacher, 1.0 / TEACHER_TEMP, 1.0 / STUDENT_TEMP)
    masked = patch_mask.astype(jnp.float32).reshape(-1, PATCHES)
    counts = jnp.sum(masked, 1, keepdims=True)
    row_weight = (
        (masked / (STUDENT_TEMP * jnp.maximum(counts, 1.0))).reshape(-1).astype(jnp.bfloat16)
    )
    logits = jnp.einsum(
        "rk,pk->rp",
        token_unit,
        lax.all_gather(proto_unit, "img", axis=0, tiled=True),
        preferred_element_type=jnp.float32,
    )
    exponent = jnp.exp(logits * inverse_temp)
    row_scale = jnp.ones((exponent.shape[0],), jnp.float32)
    col_scale = jnp.ones((exponent.shape[1],), jnp.float32)
    row_sum = row_scale
    for balance_sweep in range(BALANCE_STEPS):
        col_mass = lax.psum(jnp.dot(row_scale, exponent, precision=lax.Precision.HIGHEST), "img")
        col_scale = jnp.where(teacher, 1.0 / col_mass, jnp.ones_like(col_mass))
        row_sum = lax.psum(jnp.dot(exponent, col_scale, precision=lax.Precision.HIGHEST), "tp")
        row_scale = 1.0 / row_sum
    normed = exponent * col_scale[None, :] / row_sum[:, None]
    received = shifted(normed.astype(jnp.bfloat16), "grp", -1).astype(jnp.float32)
    weight_rows = row_weight.astype(jnp.float32)
    error_rows = (PROTOS * (normed - received) * weight_rows[:, None]).astype(jnp.bfloat16)
    loss_gradient = lax.psum_scatter(
        jnp.einsum("rp,rk->pk", error_rows, token_unit, preferred_element_type=jnp.float32),
        "img",
        scatter_dimension=0,
        tiled=True,
    )
    return jnp.where(teacher, blended, loss_gradient)[None]


def solution(mesh):
    in_specs = (P("grp", "img", None), P("grp", ("img", "tp"), None), P("img"))
    out_specs = P("grp", ("img", "tp"), None)
    return jax.shard_map(
        per_device, mesh=mesh, in_specs=in_specs, out_specs=out_specs, check_vma=False
    )
```

profile of v0, /device:TPU:2, one launch (start us, length us, event | category | flops | bytes accessed | tf_op | source)
XLA Modules:
  0.0 750.9 jit_solution(3962045471696456151)
XLA Ops:
  6.5 0.0 all-gather.2.cloned.1.call-start
  6.5 1.8 collective-permute-start
  8.3 1.7 collective-permute-done
  10.0 1.3 multiply_reduce_fusion
  11.3 0.9 divide_convert_fusion
  12.2 0.0 all-gather.2.cloned.1.call-update
  12.2 0.0 reduce-scatter.2.cloned.1.call-start
  12.2 1.1 fusion.3
  13.3 101.1 %all-gather.2.cloned.1.call-done = bf16[8192,256]{1,0:T(8,128)(2,1)} async-done(((bf16[512,256]{1,0:T(8,128)(2,1)}), bf16[8192,256]{1,0:T(8,128)(2,1)}) %all-gather.2.cloned.1.call-update) | async-done | bytes 4194320 | tf_op jit(solution)/shard_map/all_gather | solution.py:48
  114.4 4.2 multiply_exponential_fusion
  118.7 0.0 copy-start
  118.7 5.7 copy-done
  124.4 7.9 %fusion.5 = f32[1,8192]{1,0:T(1,128)S(1)} fusion(f32[512,8192]{1,0:T(8,128)S(1)} %multiply_exponential_fusion), kind=kOutput, calls=%fused_computation.21 | convolution fusion | flops 50331648 | bytes 16809984 | tf_op jit(solution)/shard_map/dot_general | solution.py:56
  132.3 75.2 %psum.42 = f32[8192]{0:T(1024)S(1)} all-reduce(f32[8192]{0:T(1024)S(1)} %bitcast.43), channel_id=1, replica_groups=mesh['grp'=2,'img'=16,'tp'=8] {'img'}, use_global_device_ids=true, to_apply=%region_2.3 | all-reduce | flops 8192 | bytes 65536 | tf_op jit(solution)/shard_map/psum | solution.py:56
  207.6 17.6 %fusion.10 = f32[1,512]{1,0:T(1,128)S(1)} fusion(f32[512,8192]{1,0:T(8,128)} %copy-done, f32[8192,1]{0,1:T(1,128)S(1)} %bitcast.39), kind=kOutput, calls=%fused_computation.28 | convolution fusion | flops 50331648 | bytes 16812032 | tf_op jit(solution)/shard_map/dot_general | solution.py:58
  225.2 18.7 %psum.43 = f32[512]{0:T(512)S(1)} all-reduce(f32[512]{0:T(512)S(1)} %bitcast.44), channel_id=1, replica_groups=mesh['grp'=2,'img'=16,'tp'=8] {'tp'}, use_global_device_ids=true, to_apply=%region_3.4 | all-reduce | flops 512 | bytes 4096 | tf_op jit(solution)/shard_map/psum | solution.py:58
  243.9 11.5 %fusion.11 = f32[1,8192]{1,0:T(1,128)S(1)} fusion(f32[512,1]{0,1:T(1,128)S(1)} %bitcast.47, f32[512,8192]{1,0:T(8,128)} %copy-done), kind=kOutput, calls=%fused_computation.29 | convolution fusion | flops 50331648 | bytes 16812032 | tf_op jit(solution)/shard_map/dot_general | solution.py:56
  255.3 72.1 %psum.44 = f32[8192]{0:T(1024)S(1)} all-reduce(f32[8192]{0:T(1024)S(1)} %bitcast.40), channel_id=1, replica_groups=mesh['grp'=2,'img'=16,'tp'=8] {'img'}, use_global_device_ids=true, to_apply=%region_4.5 | all-reduce | flops 8192 | bytes 65536 | tf_op jit(solution)/shard_map/psum | solution.py:56
  327.4 17.6 %fusion.12 = f32[1,512]{1,0:T(1,128)S(1)} fusion(f32[512,8192]{1,0:T(8,128)} %copy-done, f32[8192,1]{0,1:T(1,128)S(1)} %bitcast.41), kind=kOutput, calls=%fused_computation.30 | convolution fusion | flops 50331648 | bytes 16812032 | tf_op jit(solution)/shard_map/dot_general | solution.py:58
  345.0 16.0 %psum.45 = f32[512]{0:T(512)S(1)} all-reduce(f32[512]{0:T(512)S(1)} %bitcast.45), channel_id=1, replica_groups=mesh['grp'=2,'img'=16,'tp'=8] {'tp'}, use_global_device_ids=true, to_apply=%region_5.6 | all-reduce | flops 512 | bytes 4096 | tf_op jit(solution)/shard_map/psum | solution.py:58
  361.0 11.5 %fusion.13 = f32[1,8192]{1,0:T(1,128)S(1)} fusion(f32[512,1]{0,1:T(1,128)S(1)} %bitcast.48, f32[512,8192]{1,0:T(8,128)} %copy-done), kind=kOutput, calls=%fused_computation.31 | convolution fusion | flops 50331648 | bytes 16812032 | tf_op jit(solution)/shard_map/dot_general | solution.py:56
  372.5 72.1 %psum.46 = f32[8192]{0:T(1024)S(1)} all-reduce(f32[8192]{0:T(1024)S(1)} %bitcast.42), channel_id=1, replica_groups=mesh['grp'=2,'img'=16,'tp'=8] {'img'}, use_global_device_ids=true, to_apply=%region_6.7 | all-reduce | flops 8192 | bytes 65536 | tf_op jit(solution)/shard_map/psum | solution.py:56
  444.6 17.6 %fusion.14 = f32[1,512]{1,0:T(1,128)S(1)} fusion(f32[512,8192]{1,0:T(8,128)} %copy-done, f32[8192,1]{0,1:T(1,128)S(1)} %bitcast.38), kind=kOutput, calls=%fused_computation.32 | convolution fusion | flops 50331648 | bytes 16812032 | tf_op jit(solution)/shard_map/dot_general | solution.py:58
  462.2 0.0 copy-start.2
  462.2 0.0 copy-start.1
  462.2 18.4 %psum.47 = f32[512]{0:T(512)S(1)} all-reduce(f32[512]{0:T(512)S(1)} %bitcast.46), channel_id=1, replica_groups=mesh['grp'=2,'img'=16,'tp'=8] {'tp'}, use_global_device_ids=true, to_apply=%region_7.8 | all-reduce | flops 512 | bytes 4096 | tf_op jit(solution)/shard_map/psum | solution.py:58
  480.6 9.4 %fusion.2 = bf16[512,8192]{1,0:T(8,128)(2,1)} fusion(f32[512]{0:T(512)S(1)} %psum.47, f32[512,8192]{1,0:T(8,128)} %copy-done, f32[8192]{0:T(1024)S(1)} %divide_select_fusion), kind=kLoop, calls=%fused_computation.5 | loop fusion | flops 12582912 | bytes 25200640 | tf_op jit(solution)/shard_map/convert_element_type | solution.py:61
  490.0 1.3 collective-permute-start.1
  491.3 0.0 copy-done.2
  491.3 0.1 reduce_sum.29
  491.5 0.1 broadcast_bitcast_fusion
  491.5 13.8 %collective-permute-done.1 = bf16[512,8192]{1,0:T(8,128)(2,1)} collective-permute-done((bf16[512,8192]{1,0:T(8,128)(2,1)}, bf16[512,8192]{1,0:T(8,128)(2,1)}, u32[]{:S(2)}, u32[]{:S(2)}) %collective-permute-start.1) | collective-permute-done | bytes 8388640 | tf_op jit(solution)/shard_map/ppermute | solution.py:20
  505.4 0.0 copy-done.1
  505.4 15.9 %fusion = f32[8192,256]{1,0:T(8,128)} fusion(bf16[512,8192]{1,0:T(8,128)(2,1)} %collective-permute-done.1, f32[512]{0:T(512)S(1)} %convert_multiply_fusion.1, f32[512,8192]{1,0:T(8,128)} %copy-done, f32[512]{0:T(512)S(1)} %psum.47, f32[8192]{0:T(1024)S(1)} %divide_select_fusion, bf16[1,512,256]{2,1,0:T(8,128)(2,1)S(1)} %copy-done.1, f32[512]{0:T(512)S(1)} %add_sqrt_fusion.1), kind=kOutput, calls=%fused_computation.3 | convolution fusion | flops 2173042688 | bytes 33855488 | tf_op jit(solution)/shard_map/rp,rk->pk/dot_general | solution.py:65
  521.3 0.0 reduce-scatter.2.cloned.1.call-update
  521.3 220.6 %reduce-scatter.2.cloned.1.call-done = f32[512,256]{1,0:T(8,128)} async-done(((f32[8192,256]{1,0:T(8,128)}), f32[512,256]{1,0:T(8,128)}) %reduce-scatter.2.cloned.1.call-update) | async-done | bytes 524304 | tf_op jit(solution)/shard_map/reduce_scatter | solution.py:64
  741.9 1.9 select_bitcast_fusion
  (12 shorter events, 0.1 us)
Async XLA Ops:
  6.5 107.9 %all-gather.2.cloned.1.call-start = ((), (), s32[]{:S(2)}) async-start(), calls=%async_computation.1 | async-start | bytes 4456448 | tf_op jit(solution)/shard_map/all_gather | solution.py:48
  6.5 3.5 collective-permute-start
  12.2 729.8 %reduce-scatter.2.cloned.1.call-start = ((), (), s32[]{:S(2)}) async-start(), calls=%async_computation.2 | async-start | bytes 8912896 | tf_op jit(solution)/shard_map/reduce_scatter | solution.py:64
  118.7 5.7 copy-start
  462.2 29.1 %copy-start.2 = (s32[512]{0:T(512)S(1)}, s32[512]{0:T(512)}, u32[]{:S(2)}) copy-start(s32[512]{0:T(512)} %param.5) | copy-start | bytes 6148
  462.2 43.2 %copy-start.1 = (bf16[1,512,256]{2,1,0:T(8,128)(2,1)S(1)}, bf16[1,512,256]{2,1,0:T(8,128)(2,1)}, u32[]{:S(2)}) copy-start(bf16[1,512,256]{2,1,0:T(8,128)(2,1)} %param.3) | copy-start | bytes 786436
  490.0 15.4 %collective-permute-start.1 = (bf16[512,8192]{1,0:T(8,128)(2,1)}, bf16[512,8192]{1,0:T(8,128)(2,1)}, u32[]{:S(2)}, u32[]{:S(2)}) collective-permute-start(bf16[512,8192]{1,0:T(8,128)(2,1)} %fusion.2), channel_id=1, source_target_pairs={{128,0},{129,1},{130,2},{131,3},{132,4},{133,5},{134,6},{135,7},{1... | collective-permute-start | bytes 25165832 | tf_op jit(solution)/shard_map/ppermute | solution.py:20
Sparse Core Ops, SparseCore 0:
  12.3 102.0 all-gather.1
  521.4 220.4 reduce-scatter.1
where the time goes:
time: 760 us; the launch traced here: 751 us
  waiting for transfers between devices  337 us (44%)
  blocking collectives  272 us (36%)
  matrix products  104 us (14%)
  other arithmetic  14.7 us (2%)
  between operations  13.7 us (2%)
    reduce_scatter x1, waiting for transfers between devices, per_device(): lax.psum_scatter(jnp.einsum('rp,rk->pk', error_rows, token_unit, preferre...  221 us
    psum x3, blocking collectives, per_device(): lax.psum(jnp.dot(row_scale, exponent, precision=lax.Precision.HIGHEST), '...  219 us
    all_gather x1, waiting for transfers between devices, per_device(): lax.all_gather(proto_unit, 'img', axis=0, tiled=True)  101 us
    psum x3, blocking collectives, per_device(): lax.psum(jnp.dot(exponent, col_scale, precision=lax.Precision.HIGHEST), '...  53 us
    dot_general x3, matrix products, per_device(): jnp.dot(exponent, col_scale, precision=lax.Precision.HIGHEST)  52.9 us
    dot_general x3, matrix products, per_device(): jnp.dot(row_scale, exponent, precision=lax.Precision.HIGHEST)  30.8 us
    dot_general x1, matrix products, per_device(): jnp.einsum('rp,rk->pk', error_rows, token_unit, preferred_element_type=jn...  15.9 us
    ppermute x2, waiting for transfers between devices, shifted(): return lax.ppermute(block, axis, route)  15.5 us
  transfers between devices with their start and end apart: 4, of which 4 were waited for; matrix products, arithmetic and copies ran while one was open for 0% of the time, Pallas kernels for 0%

commit v1 on v0

v1 whole, which is shorter than its diff:
```python
import functools

import jax
import jax.numpy as jnp
from jax import lax
from jax.experimental import pallas as pl
from jax.experimental.pallas import tpu as pltpu
from jax.sharding import PartitionSpec as P

PROTOS = 65536
PATCHES = 256
MOMENTUM = 0.994
TEACHER_TEMP = 0.07
STUDENT_TEMP = 0.1
EPS = 1e-06

AXES = ("grp", "img", "tp")
N_GRP, N_IMG, N_TP = 2, 16, 8
N_Y = 4
HALF = 256
OWN_ROWS = 64
ROWS = N_IMG * OWN_ROWS
OWN = N_Y * HALF
COLS = 2 * OWN
N_ROWGRP = 32
N_COLGRP = 8
VMEM_LIMIT = 40 * 1024 * 1024


def coordinates(device):
    grp, rest = divmod(device, N_IMG * N_TP)
    img, tp = divmod(rest, N_TP)
    x_lo, y = divmod(tp, N_Y)
    return grp, img, x_lo, y


def groups_of(key):
    found = {}
    for device in range(N_GRP * N_IMG * N_TP):
        found.setdefault(key(*coordinates(device)), []).append(device)
    return list(found.values())


Y_GROUPS = groups_of(lambda grp, img, x_lo, y: (grp, img, x_lo))
COL_GROUPS = groups_of(lambda grp, img, x_lo, y: (img, x_lo))
ROW_GROUPS = groups_of(lambda grp, img, x_lo, y: (grp, y))


def exchange(blocks, groups):
    return lax.all_to_all(blocks, AXES, 0, 0, axis_index_groups=groups, tiled=True)


def swapped(block):
    return lax.ppermute(block, "grp", [(0, 1), (1, 0)])


def unit_rows(values):
    values = values.astype(jnp.float32)
    return (values / jnp.sqrt(jnp.sum(values * values, -1, keepdims=True) + EPS)).astype(
        jnp.bfloat16
    )


def diagonal():
    return lax.broadcasted_iota(jnp.int32, (128, 128), 0) == lax.broadcasted_iota(
        jnp.int32, (128, 128), 1
    )


def to_row(column):
    return jnp.sum(jnp.where(diagonal(), column, 0.0), axis=0, keepdims=True)


def to_column(row):
    return jnp.sum(jnp.where(diagonal(), row, 0.0), axis=1, keepdims=True)


def lanes(pieces):
    return jnp.concatenate([pieces[k : k + 1, :] for k in range(pieces.shape[0])], axis=1)


def pieces_of(row):
    return jnp.concatenate([row[:, k * 128 : (k + 1) * 128] for k in range(8)], axis=0)


def send_columns(grp_ref, vector_ref, out_ref):
    top, bottom = vector_ref[0:8, :], vector_ref[8:16, :]
    for target in range(2):
        same = grp_ref[0] == target
        first = jnp.where(same, top, bottom)
        second = jnp.where(same, bottom, top)
        for y in range(N_Y):
            out_ref[target * N_Y + y, 0:8, :] = first
            out_ref[target * N_Y + y, 8:16, :] = second


def teacher_exp_kernel(grp_ref, own_ref, other_ref, token_ref, exp_ref, out_ref, vector_ref):
    for part, proto_ref in enumerate((own_ref, other_ref)):

        @pl.loop(0, OWN // 256)
        def _(i):
            protos = proto_ref[pl.ds(i * 256, 256), :]
            logits = lax.dot_general(
                protos,
                token_ref[...],
                (((1,), (1,)), ((), ())),
                preferred_element_type=jnp.float32,
            )
            values = jnp.exp(logits * (1.0 / TEACHER_TEMP))
            exp_ref[pl.ds(part * OWN + i * 256, 256), :] = values
            folded = sum(values[:, k * 128 : (k + 1) * 128] for k in range(8))
            column = jnp.sum(folded, axis=1, keepdims=True)
            for h in range(2):
                vector_ref[pl.ds(part * 8 + i * 2 + h, 1), :] = to_row(
                    column[h * 128 : (h + 1) * 128]
                )

    send_columns(grp_ref, vector_ref, out_ref)


def student_exp_kernel(own_ref, other_ref, token_ref, exp_ref, out_ref, total_ref):
    total_ref[...] = jnp.zeros_like(total_ref)
    for part, proto_ref in enumerate((own_ref, other_ref)):

        @pl.loop(0, OWN // 256)
        def _(i):
            protos = proto_ref[pl.ds(i * 256, 256), :]
            logits = lax.dot_general(
                protos,
                token_ref[...],
                (((1,), (1,)), ((), ())),
                preferred_element_type=jnp.float32,
            )
            values = jnp.exp(logits * (1.0 / STUDENT_TEMP))
            exp_ref[pl.ds(part * OWN + i * 256, 256), :] = values
            total_ref[...] += jnp.sum(values.reshape(32, 8, ROWS), axis=0)

    out_ref[...] = pieces_of(jnp.sum(total_ref[...], axis=0, keepdims=True))


def row_kernel(with_student, *refs):
    if with_student:
        parts_ref, exp_ref, student_ref, out_ref, scale_ref, total_ref = refs
    else:
        parts_ref, exp_ref, out_ref, scale_ref, total_ref = refs
    scale_ref[...] = 1.0 / jnp.sum(parts_ref[...], axis=0)
    total_ref[...] = jnp.zeros_like(total_ref)

    @pl.loop(0, COLS // 128)
    def _(j):
        column = to_column(scale_ref[pl.ds(j, 1), :])
        weighted = exp_ref[pl.ds(j * 128, 128), :] * column
        total_ref[...] += jnp.sum(weighted.reshape(16, 8, ROWS), axis=0)

    mine = pieces_of(jnp.sum(total_ref[...], axis=0, keepdims=True))
    for k in range(N_ROWGRP):
        out_ref[k, 0:8, :] = mine
        if with_student:
            out_ref[k, 8:16, :] = student_ref[...]


def col_kernel(with_student, *refs):
    if with_student:
        grp_ref, parts_ref, exp_ref, out_ref, student_ref, vector_ref = refs
    else:
        grp_ref, parts_ref, exp_ref, out_ref, vector_ref = refs
    total = jnp.sum(parts_ref[...], axis=0)
    inverse = 1.0 / total
    row = lanes(inverse[0:8, :])
    if with_student:
        student_ref[...] = inverse[8:16, :]

    @pl.loop(0, COLS // 128)
    def _(j):
        weighted = exp_ref[pl.ds(j * 128, 128), :] * row
        folded = sum(weighted[:, k * 128 : (k + 1) * 128] for k in range(8))
        vector_ref[pl.ds(j, 1), :] = to_row(jnp.sum(folded, axis=1, keepdims=True))

    send_columns(grp_ref, vector_ref, out_ref)


def grad_kernel(
    parts_ref,
    scale_ref,
    student_ref,
    weight_ref,
    teacher_exp_ref,
    student_exp_ref,
    token_ref,
    own_ref,
    other_ref,
):
    row_inverse = lanes(1.0 / jnp.sum(parts_ref[...], axis=0))
    student_inverse = lanes(student_ref[...])
    weight = lanes(weight_ref[...])

    for part, out_ref in enumerate((own_ref, other_ref)):

        @pl.loop(0, OWN // 256)
        def _(i):
            errors = []
            for h in range(2):
                j = part * 8 + i * 2 + h
                column = to_column(scale_ref[pl.ds(j, 1), :])
                rows = pl.ds(j * 128, 128)
                targets = (teacher_exp_ref[rows, :] * column * row_inverse).astype(jnp.bfloat16)
                probs = student_exp_ref[rows, :] * student_inverse
                errors.append(
                    (PROTOS * (probs - targets.astype(jnp.float32)) * weight).astype(jnp.bfloat16)
                )
            out_ref[pl.ds(i * 256, 256), :] = jnp.dot(
                jnp.concatenate(errors, axis=0),
                token_ref[...],
                preferred_element_type=jnp.float32,
            ).astype(out_ref.dtype)


def call(kernel, outs, scratch, *args, flops=0, transcendentals=0):
    vmem = pl.BlockSpec(memory_space=pltpu.VMEM)
    smem = pl.BlockSpec(memory_space=pltpu.SMEM)
    return pl.pallas_call(
        kernel,
        out_shape=outs,
        in_specs=[smem if a.dtype == jnp.int32 else vmem for a in args],
        out_specs=[vmem] * len(outs),
        scratch_shapes=scratch,
        compiler_params=pltpu.CompilerParams(vmem_limit_bytes=VMEM_LIMIT),
        cost_estimate=pl.CostEstimate(
            flops=flops, transcendentals=transcendentals, bytes_accessed=COLS * ROWS * 4
        ),
    )(*args)


def shape(dims, dtype=jnp.float32):
    return jax.ShapeDtypeStruct(dims, dtype)


def per_device(features, masters, patch_mask):
    grp = lax.axis_index("grp")
    y = lax.axis_index("tp") % N_Y
    teacher = grp == 1
    grp_word = grp.astype(jnp.int32).reshape(1)
    vec = pltpu.VMEM((16, 128), jnp.float32)
    wide = pltpu.VMEM((8, ROWS), jnp.float32)

    own_master = masters[0]
    other_master = swapped(own_master)
    start = y * (2 * OWN_ROWS)
    own_rows = lax.dynamic_slice_in_dim(features[0], start + grp * OWN_ROWS, OWN_ROWS)
    lent_rows = lax.dynamic_slice_in_dim(features[0], start + (1 - grp) * OWN_ROWS, OWN_ROWS)
    other_rows = swapped(lent_rows)

    student_master = jnp.where(teacher, other_master, own_master)
    teacher_master = jnp.where(teacher, own_master, other_master)
    blended = MOMENTUM * teacher_master + (1.0 - MOMENTUM) * student_master
    teacher_half = unit_rows(lax.dynamic_slice_in_dim(blended, grp * HALF, HALF))
    student_half = unit_rows(lax.dynamic_slice_in_dim(student_master, grp * HALF, HALF))
    teacher_rows = unit_rows(jnp.where(teacher, own_rows, other_rows))
    student_rows = unit_rows(jnp.where(teacher, other_rows, own_rows))

    masked = patch_mask.astype(jnp.float32).reshape(-1, PATCHES)
    counts = jnp.sum(masked, 1, keepdims=True)
    row_weight = (
        (masked / (STUDENT_TEMP * jnp.maximum(counts, 1.0))).reshape(-1).astype(jnp.bfloat16)
    )
    own_weight = lax.dynamic_slice_in_dim(row_weight, start + grp * OWN_ROWS, OWN_ROWS)
    student_pack = jnp.concatenate(
        [student_rows, jnp.pad(own_weight.reshape(1, OWN_ROWS), ((0, 15), (0, 256 - OWN_ROWS)))]
    )

    teacher_own = exchange(
        jnp.broadcast_to(teacher_half[None], (N_Y, HALF, 256)), Y_GROUPS
    ).reshape(OWN, 256)
    teacher_other = swapped(teacher_own)
    teacher_tokens = lax.all_to_all(
        jnp.broadcast_to(teacher_rows[None], (N_IMG, OWN_ROWS, 256)), "img", 0, 0, tiled=True
    ).reshape(ROWS, 256)

    student_own = lax.all_gather(
        student_half, AXES, axis_index_groups=Y_GROUPS, axis=0, tiled=True
    )
    student_other = swapped(student_own)
    packs = lax.all_gather(student_pack, "img", axis=0)
    student_tokens = packs[:, :OWN_ROWS].reshape(ROWS, 256)
    weights = packs[:, OWN_ROWS, :OWN_ROWS].astype(jnp.float32).reshape(8, 128)

    work = COLS * ROWS
    teacher_exp, col_parts = call(
        teacher_exp_kernel,
        [shape((COLS, ROWS)), shape((N_COLGRP, 16, 128))],
        [vec],
        grp_word,
        teacher_own,
        teacher_other,
        teacher_tokens,
        flops=2 * work * 256,
        transcendentals=work,
    )
    student_exp, student_part = call(
        student_exp_kernel,
        [shape((COLS, ROWS)), shape((8, 128))],
        [wide],
        student_own,
        student_other,
        student_tokens,
        flops=2 * work * 256,
        transcendentals=work,
    )

    for sweep in range(3):
        last = sweep == 2
        col_parts = exchange(col_parts, COL_GROUPS)
        row_parts, col_scale = call(
            functools.partial(row_kernel, sweep == 1),
            [shape((N_ROWGRP, 16 if sweep == 1 else 8, 128)), shape((16, 128))],
            [wide],
            col_parts,
            teacher_exp,
            *((student_part,) if sweep == 1 else ()),
            flops=2 * work,
        )
        row_parts = exchange(row_parts, ROW_GROUPS)
        if not last:
            results = call(
                functools.partial(col_kernel, sweep == 1),
                [shape((N_COLGRP, 16, 128))] + ([shape((8, 128))] if sweep == 1 else []),
                [vec],
                grp_word,
                row_parts,
                teacher_exp,
                flops=2 * work,
            )
            col_parts = results[0]
            if sweep == 1:
                student_inverse = results[1]

    own_grad, other_grad = call(
        grad_kernel,
        [shape((OWN, 256)), shape((OWN, 256), jnp.bfloat16)],
        [],
        row_parts,
        col_scale,
        student_inverse,
        weights,
        teacher_exp,
        student_exp,
        student_tokens,
        flops=2 * work * 256,
    )
    chip_grad = own_grad + swapped(other_grad).astype(jnp.float32)
    received = exchange(chip_grad.astype(jnp.bfloat16).reshape(N_Y, HALF, 256), Y_GROUPS)
    half_grad = jnp.sum(received.astype(jnp.float32), axis=0)
    second = lax.ppermute(half_grad, "grp", [(1, 0)])
    gradient = jnp.concatenate([half_grad, second])
    return jnp.where(teacher, blended, gradient)[None]


def solution(mesh):
    in_specs = (P("grp", "img", None), P("grp", ("img", "tp"), None), P("img"))
    out_specs = P("grp", ("img", "tp"), None)
    return jax.shard_map(
        per_device, mesh=mesh, in_specs=in_specs, out_specs=out_specs, check_vma=False
    )
```

time: 760 us -> 223 us (0.29)
  waiting for transfers between devices: 337 us -> 29.6 us
  blocking collectives: 272 us -> 95.9 us
  matrix products: 104 us -> 0 us
  starting transfers between devices: 3.08 us -> 37.8 us
  Pallas kernels: 0 us -> 26.2 us
  local copies, waits for them, and re-layouts: 5.81 us -> 23.5 us
  between operations: 13.7 us -> 0.23 us
  other arithmetic: 14.7 us -> 6.68 us
    psum x6 -> x0, blocking collectives: 272 us -> none  [the longest x3 219 us: per_device(): lax.psum(jnp.dot(row_scale, exponent, precision=lax.Precision.HIGHEST), '...]
    reduce_scatter x1 -> x0, waiting for transfers between devices: 221 us -> none  [per_device(): lax.psum_scatter(jnp.einsum('rp,rk->pk', error_rows, token_unit, preferre...]
    dot_general x8 -> x0, matrix products: 104 us -> none  [the longest x3 52.9 us: per_device(): jnp.dot(exponent, col_scale, precision=lax.Precision.HIGHEST)]
    all_gather x1 -> x0, waiting for transfers between devices: 101 us -> none  [per_device(): lax.all_gather(proto_unit, 'img', axis=0, tiled=True)]
    all_gather x0 -> x2, blocking collectives: none -> 56.5 us  [the longest x1 43.5 us: per_device(): packs = lax.all_gather(student_pack, 'img', axis=0)]
    all_to_all x0 -> x3, blocking collectives: none -> 39.4 us  [exchange(): lax.all_to_all(blocks, AXES, 0, 0, axis_index_groups=groups, tiled=True)]
    all_to_all x0 -> x6, starting transfers between devices: none -> 35.8 us  [the longest x5 25.7 us: exchange(): lax.all_to_all(blocks, AXES, 0, 0, axis_index_groups=groups, tiled=True)]
    pallas_call x0 -> x8, Pallas kernels: none -> 26.2 us  [call(): pl.pallas_call(kernel, out_shape=outs, in_specs=[smem if a.dtype == jnp.i...]
  transfers between devices with their start and end apart: 4 -> 12, of which waited for: 4 -> 6; matrix products, arithmetic and copies ran while one was open for 0% -> 2% of each run, Pallas kernels for 0% -> 5%
where the time goes in v1:
time: 223 us; the launch traced here: 220 us
  blocking collectives  95.9 us (43%)
  starting transfers between devices  37.8 us (17%)
  waiting for transfers between devices  29.6 us (13%)
  Pallas kernels  26.2 us (12%)
  local copies, waits for them, and re-layouts  23.5 us (11%)
  other arithmetic  6.68 us (3%)
    all_gather x1, blocking collectives, per_device(): packs = lax.all_gather(student_pack, 'img', axis=0)  43.5 us
    all_to_all x3, blocking collectives, exchange(): lax.all_to_all(blocks, AXES, 0, 0, axis_index_groups=groups, tiled=True)  39.4 us
    pallas_call x8, Pallas kernels, call(): pl.pallas_call(kernel, out_shape=outs, in_specs=[smem if a.dtype == jnp.i...  26.2 us
    all_to_all x5, starting transfers between devices, exchange(): lax.all_to_all(blocks, AXES, 0, 0, axis_index_groups=groups, tiled=True)  25.7 us
    all_to_all x5, waiting for transfers between devices, exchange(): lax.all_to_all(blocks, AXES, 0, 0, axis_index_groups=groups, tiled=True)  23.8 us
    unnamed x18, local copies, waits for them, and re-layouts  20.9 us
    all_gather x1, blocking collectives, per_device(): lax.all_gather(student_half, AXES, axis_index_groups=Y_GROUPS, axis=0, ti...  13 us
    all_to_all x1, starting transfers between devices, per_device(): lax.all_to_all(jnp.broadcast_to(teacher_rows[None], (N_IMG, OWN_ROWS, 256...  10.1 us
  transfers between devices with their start and end apart: 12, of which 6 were waited for; matrix products, arithmetic and copies ran while one was open for 2% of the time, Pallas kernels for 5%

profile of v1, /device:TPU:2, one launch (start us, length us, event | category | flops | bytes accessed | tf_op | source)
XLA Modules:
  0.0 219.9 jit_solution(9578095810471674424)
XLA Ops:
  0.0 0.8 dynamic-slice_bitcast_fusion
  0.8 0.5 collective-permute-start
  1.3 0.7 convert_element_type.48
  2.0 0.1 reduce_sum.58
  2.2 0.9 fusion.4
  3.1 1.1 broadcast_select_fusion
  4.2 0.1 multiply_reduce_fusion.1
  4.5 0.8 broadcast_in_dim.6
  5.3 4.5 %all-to-all-start = ((bf16[4,256,256]{2,1,0:T(8,128)(2,1)}), bf16[4,256,256]{2,1,0:T(8,128)(2,1)S(1)}, u32[]{:S(2)}, u32[]{:S(2)}) async-start(bf16[4,256,256]{2,1,0:T(8,128)(2,1)} %broadcast_in_dim.6), calls=%async_computation | async-start | bytes 1048576 | tf_op jit(solution)/shard_map/all_to_all | solution.py:50
  9.8 0.9 fusion.5
  10.6 9.1 %all-to-all-done = bf16[4,256,256]{2,1,0:T(8,128)(2,1)S(1)} async-done(((bf16[4,256,256]{2,1,0:T(8,128)(2,1)}), bf16[4,256,256]{2,1,0:T(8,128)(2,1)S(1)}, u32[]{:S(2)}, u32[]{:S(2)}) %all-to-all-start) | async-done | bytes 524320 | tf_op jit(solution)/shard_map/all_to_all | solution.py:50
  19.7 0.8 broadcast_in_dim.7
  20.6 10.1 %all-to-all-start.1 = ((bf16[16,64,256]{2,1,0:T(8,128)(2,1)}), bf16[16,64,256]{2,1,0:T(8,128)(2,1)S(1)}, u32[]{:S(2)}, u32[]{:S(2)}) async-start(bf16[16,64,256]{2,1,0:T(8,128)(2,1)} %broadcast_in_dim.7), calls=%async_computation.1 | async-start | bytes 1048576 | tf_op jit(solution)/shard_map/all_to_all | solution.py:275
  30.7 0.7 divide_convert_fusion.2
  31.4 0.1 multiply_reduce_fusion
  31.7 13.0 %all_gather.9.own_ref = bf16[1024,256]{1,0:T(8,128)(2,1)S(1)} all-gather(bf16[256,256]{1,0:T(8,128)(2,1)S(1)} %divide_convert_fusion), channel_id=1, replica_groups={{0,1,2,3},{4,5,6,7},{8,9,10,11},{12,13,14,15},{16,17,18,19},{20,21,22,2..., dimensions={0}, use_global_device_ids=true | all-gather | bytes 655360 | tf_op jit(solution)/shard_map/all_gather | solution.py:279
  44.8 1.8 all-to-all-done.1
  46.7 4.1 %shard_map.37 = (f32[2048,1024]{1,0:T(8,128)S(1)}, f32[8,16,128]{2,1,0:T(8,128)}) custom-call(s32[1]{0:T(128)} %bitcast.1.grp_ref.refs_0_, bf16[1024,256]{1,0:T(8,128)(2,1)S(1)} %bitcast.32, bf16[1024,256]{1,0:T(8,128)(2,1)S(1)} %collective-permute-done.1.other_ref, bf16[1024,256]{1,0:T(8,128)(2,1)S(1)} %bitcast.33), custom_call_target="tpu_custom_call" | custom-call | flops 1073741824 | bytes 8388608 | tf_op jit(solution)/shard_map/pallas_call | solution.py:221
  50.7 3.2 %copy-done = f32[2048,1024]{1,0:T(8,128)} copy-done((f32[2048,1024]{1,0:T(8,128)}, f32[2048,1024]{1,0:T(8,128)S(1)}, u32[]{:S(2)}) %copy-start) | copy-done | bytes 8388632
  54.0 3.4 %all-to-all-start.2 = ((f32[8,16,128]{2,1,0:T(8,128)}), f32[8,16,128]{2,1,0:T(8,128)S(1)}, u32[]{:S(2)}, u32[]{:S(2)}) async-start(f32[8,16,128]{2,1,0:T(8,128)} %get-tuple-element.17), calls=%async_computation.2 | async-start | bytes 131072 | tf_op jit(solution)/shard_map/all_to_all | solution.py:50
  57.3 5.2 %all-to-all-done.2.refs_0_ = f32[8,16,128]{2,1,0:T(8,128)S(1)} async-done(((f32[8,16,128]{2,1,0:T(8,128)}), f32[8,16,128]{2,1,0:T(8,128)S(1)}, u32[]{:S(2)}, u32[]{:S(2)}) %all-to-all-start.2) | async-done | bytes 65568 | tf_op jit(solution)/shard_map/all_to_all | solution.py:50
  62.6 3.4 %copy-done.1 = f32[2048,1024]{1,0:T(8,128)S(1)} copy-done((f32[2048,1024]{1,0:T(8,128)S(1)}, f32[2048,1024]{1,0:T(8,128)}, u32[]{:S(2)}) %copy-start.1) | copy-done | bytes 8388632
  66.0 2.5 %shard_map.38 = (f32[32,8,128]{2,1,0:T(8,128)}, f32[16,128]{1,0:T(8,128)}) custom-call(f32[8,16,128]{2,1,0:T(8,128)S(1)} %all-to-all-done.2.refs_0_, f32[2048,1024]{1,0:T(8,128)S(1)} %copy-done.1), custom_call_target="tpu_custom_call" | custom-call | flops 4194304 | bytes 8388608 | tf_op jit(solution)/shard_map/pallas_call | solution.py:221
  68.5 9.3 %all-to-all-start.3 = ((f32[32,8,128]{2,1,0:T(8,128)}), f32[32,8,128]{2,1,0:T(8,128)S(1)}, u32[]{:S(2)}, u32[]{:S(2)}) async-start(f32[32,8,128]{2,1,0:T(8,128)} %get-tuple-element.19), calls=%async_computation.3 | async-start | bytes 262144 | tf_op jit(solution)/shard_map/all_to_all | solution.py:50
  77.8 43.5 %all-gather = bf16[1280,256]{1,0:T(8,128)(2,1)S(1)} all-gather(bf16[80,256]{1,0:T(8,128)(2,1)S(1)} %fusion.6), channel_id=2, replica_groups=mesh['grp'=2,'img'=16,'tp'=8] {'img'}, dimensions={0}, use_global_device_ids=true | all-gather | bytes 696320 | tf_op jit(solution)/shard_map/all_gather | solution.py:283
  121.3 0.8 copy-done.7
  122.2 3.4 %copy-done.2 = f32[2048,1024]{1,0:T(8,128)S(1)} copy-done((f32[2048,1024]{1,0:T(8,128)S(1)}, f32[2048,1024]{1,0:T(8,128)}, u32[]{:S(2)}) %copy-start.2) | copy-done | bytes 8388632
  125.6 2.6 %shard_map.39 = f32[8,16,128]{2,1,0:T(8,128)} custom-call(s32[1]{0:T(128)} %bitcast.1.grp_ref.refs_0_, f32[32,8,128]{2,1,0:T(8,128)S(1)} %all-to-all-done.3.refs_1_, f32[2048,1024]{1,0:T(8,128)S(1)} %copy-done.2), custom_call_target="tpu_custom_call" | custom-call | flops 4194304 | bytes 8388608 | tf_op jit(solution)/shard_map/pallas_call | solution.py:221
  128.2 3.4 %all-to-all-start.4 = ((f32[8,16,128]{2,1,0:T(8,128)}), f32[8,16,128]{2,1,0:T(8,128)S(1)}, u32[]{:S(2)}, u32[]{:S(2)}) async-start(f32[8,16,128]{2,1,0:T(8,128)} %shard_map.39), calls=%async_computation.4 | async-start | bytes 131072 | tf_op jit(solution)/shard_map/all_to_all | solution.py:50
  131.6 2.8 %shard_map.40 = (f32[2048,1024]{1,0:T(8,128)S(1)}, f32[8,128]{1,0:T(8,128)S(1)}) custom-call(bf16[1024,256]{1,0:T(8,128)(2,1)S(1)} %all_gather.9.own_ref, bf16[1024,256]{1,0:T(8,128)(2,1)S(1)} %collective-permute-done.3.other_ref, bf16[1024,256]{1,0:T(8,128)(2,1)S(1)} %bitcast.29), custom_call_target="tpu_custom_call" | custom-call | flops 1073741824 | bytes 8388608 | tf_op jit(solution)/shard_map/pallas_call | solution.py:221
  134.4 3.2 %copy-done.6 = f32[2048,1024]{1,0:T(8,128)} copy-done((f32[2048,1024]{1,0:T(8,128)}, f32[2048,1024]{1,0:T(8,128)S(1)}, u32[]{:S(2)}) %copy-start.6) | copy-done | bytes 8388632
  137.6 3.4 %copy-done.3 = f32[2048,1024]{1,0:T(8,128)S(1)} copy-done((f32[2048,1024]{1,0:T(8,128)S(1)}, f32[2048,1024]{1,0:T(8,128)}, u32[]{:S(2)}) %copy-start.3) | copy-done | bytes 8388632
  141.0 2.5 %shard_map.41 = (f32[32,16,128]{2,1,0:T(8,128)S(1)}, f32[16,128]{1,0:T(8,128)}) custom-call(f32[8,16,128]{2,1,0:T(8,128)S(1)} %all-to-all-done.4.refs_0_, f32[2048,1024]{1,0:T(8,128)S(1)} %copy-done.3, f32[8,128]{1,0:T(8,128)S(1)} %get-tuple-element.20.refs_2_), custom_call_target="tpu_custom_call" | custom-call | flops 4194304 | bytes 8388608 | tf_op jit(solution)/shard_map/pallas_call | solution.py:221
  143.4 17.5 %all_to_all.45.refs_1_ = f32[32,16,128]{2,1,0:T(8,128)S(1)} all-to-all(f32[32,16,128]{2,1,0:T(8,128)S(1)} %get-tuple-element.21), channel_id=1, replica_groups={{0,4,8,12,16,20,24,28,32,36,40,44,48,52,56,60,64,68,72,76,80,84,88,92,9..., dimensions={0} | all-to-all | bytes 524288 | tf_op jit(solution)/shard_map/all_to_all | solution.py:50
  160.9 2.0 shard_map.42
  162.9 9.5 %all_to_all.46.refs_0_ = f32[8,16,128]{2,1,0:T(8,128)S(1)} all-to-all(f32[8,16,128]{2,1,0:T(8,128)S(1)} %get-tuple-element.22), channel_id=1, replica_groups={{0,1,2,3,128,129,130,131},{4,5,6,7,132,133,134,135},{8,9,10,11,136,137,..., dimensions={0} | all-to-all | bytes 131072 | tf_op jit(solution)/shard_map/all_to_all | solution.py:50
  172.4 2.5 %shard_map.43 = (f32[32,8,128]{2,1,0:T(8,128)}, f32[16,128]{1,0:T(8,128)S(1)}) custom-call(f32[8,16,128]{2,1,0:T(8,128)S(1)} %all_to_all.46.refs_0_, f32[2048,1024]{1,0:T(8,128)S(1)} %copy-done.4), custom_call_target="tpu_custom_call" | custom-call | flops 4194304 | bytes 8388608 | tf_op jit(solution)/shard_map/pallas_call | solution.py:221
  174.9 5.2 %all-to-all-start.7 = ((f32[32,8,128]{2,1,0:T(8,128)}), f32[32,8,128]{2,1,0:T(8,128)S(1)}, u32[]{:S(2)}, u32[]{:S(2)}) async-start(f32[32,8,128]{2,1,0:T(8,128)} %get-tuple-element.23), calls=%async_computation.7 | async-start | bytes 262144 | tf_op jit(solution)/shard_map/all_to_all | solution.py:50
  180.1 0.8 fusion.7
  181.0 9.4 %all-to-all-done.7.parts_ref = f32[32,8,128]{2,1,0:T(8,128)S(1)} async-done(((f32[32,8,128]{2,1,0:T(8,128)}), f32[32,8,128]{2,1,0:T(8,128)S(1)}, u32[]{:S(2)}, u32[]{:S(2)}) %all-to-all-start.7) | async-done | bytes 131104 | tf_op jit(solution)/shard_map/all_to_all | solution.py:50
  190.4 3.4 %copy-done.5 = f32[2048,1024]{1,0:T(8,128)S(1)} copy-done((f32[2048,1024]{1,0:T(8,128)S(1)}, f32[2048,1024]{1,0:T(8,128)}, u32[]{:S(2)}) %copy-start.5) | copy-done | bytes 8388632
  193.8 7.2 %shard_map.44 = (f32[1024,256]{1,0:T(8,128)S(1)}, bf16[1024,256]{1,0:T(8,128)(2,1)S(1)}) custom-call(f32[32,8,128]{2,1,0:T(8,128)S(1)} %all-to-all-done.7.parts_ref, f32[16,128]{1,0:T(8,128)S(1)} %get-tuple-element.24.scale_ref, f32[8,128]{1,0:T(8,128)S(1)} %get-tuple-element.25.student_ref, f32[8,128]{1,0:T(8,128)S(1)} %reshape.68.weight_ref, ...), custom_call_target="tpu_custom_call" | custom-call | flops 1073741824 | bytes 8388608 | tf_op jit(solution)/shard_map/pallas_call | solution.py:221
  201.1 1.9 collective-permute-done.4
  203.0 0.1 add_convert_fusion
  203.1 12.5 %all_to_all.47 = bf16[4,256,256]{2,1,0:T(8,128)(2,1)S(1)} all-to-all(bf16[4,256,256]{2,1,0:T(8,128)(2,1)S(1)} %bitcast.36), channel_id=1, replica_groups={{0,1,2,3},{4,5,6,7},{8,9,10,11},{12,13,14,15},{16,17,18,19},{20,21,22,2..., dimensions={0} | all-to-all | bytes 1048576 | tf_op jit(solution)/shard_map/all_to_all | solution.py:50
  215.6 1.3 collective-permute-start.5
  216.9 2.1 collective-permute-done.5
  219.1 0.9 fusion
  (33 shorter events, 0.8 us)
Async XLA Ops:
  0.8 1.4 collective-permute-start.2
  0.8 2.3 %collective-permute-start = (f32[512,256]{1,0:T(8,128)}, f32[512,256]{1,0:T(8,128)S(1)}, u32[]{:S(2)}, u32[]{:S(2)}) collective-permute-start(f32[512,256]{1,0:T(8,128)} %bitcast.37), channel_id=1, source_target_pairs={{0,128},{128,0},{1,129},{129,1},{2,130},{130,2},{3,131},{131,3},{4... | collective-permute-start | bytes 1572872 | tf_op jit(solution)/shard_map/ppermute | solution.py:54
  5.3 14.4 %all-to-all-start = ((bf16[4,256,256]{2,1,0:T(8,128)(2,1)}), bf16[4,256,256]{2,1,0:T(8,128)(2,1)S(1)}, u32[]{:S(2)}, u32[]{:S(2)}) async-start(bf16[4,256,256]{2,1,0:T(8,128)(2,1)} %broadcast_in_dim.6), calls=%async_computation | async-start | bytes 1048576 | tf_op jit(solution)/shard_map/all_to_all | solution.py:50
  20.6 26.1 %all-to-all-start.1 = ((bf16[16,64,256]{2,1,0:T(8,128)(2,1)}), bf16[16,64,256]{2,1,0:T(8,128)(2,1)S(1)}, u32[]{:S(2)}, u32[]{:S(2)}) async-start(bf16[16,64,256]{2,1,0:T(8,128)(2,1)} %broadcast_in_dim.7), calls=%async_computation.1 | async-start | bytes 1048576 | tf_op jit(solution)/shard_map/all_to_all | solution.py:275
  31.5 15.1 %collective-permute-start.1 = (bf16[1024,256]{1,0:T(8,128)(2,1)S(1)}, bf16[1024,256]{1,0:T(8,128)(2,1)S(1)}, u32[]{:S(2)}, u32[]{:S(2)}) collective-permute-start(bf16[1024,256]{1,0:T(8,128)(2,1)S(1)} %bitcast.31), channel_id=1, source_target_pairs={{0,128},{128,0},{1,129},{129,1},{2,130},{130,2},{3,131},{131,3},{4... | collective-permute-start | bytes 1572872 | tf_op jit(solution)/shard_map/ppermute | solution.py:54
  44.8 86.8 %collective-permute-start.3 = (bf16[1024,256]{1,0:T(8,128)(2,1)S(1)}, bf16[1024,256]{1,0:T(8,128)(2,1)S(1)}, u32[]{:S(2)}, u32[]{:S(2)}) collective-permute-start(bf16[1024,256]{1,0:T(8,128)(2,1)S(1)} %all_gather.9.own_ref), channel_id=1, source_target_pairs={{0,128},{128,0},{1,129},{129,1},{2,130},{130,2},{3,131},{131,3},{4... | collective-permute-start | bytes 1572872 | tf_op jit(solution)/shard_map/ppermute | solution.py:54
  50.7 3.2 %copy-start = (f32[2048,1024]{1,0:T(8,128)}, f32[2048,1024]{1,0:T(8,128)S(1)}, u32[]{:S(2)}) copy-start(f32[2048,1024]{1,0:T(8,128)S(1)} %get-tuple-element.18.refs_1_.refs_2_.teacher_exp_ref) | copy-start | bytes 25165828
  54.0 8.6 %all-to-all-start.2 = ((f32[8,16,128]{2,1,0:T(8,128)}), f32[8,16,128]{2,1,0:T(8,128)S(1)}, u32[]{:S(2)}, u32[]{:S(2)}) async-start(f32[8,16,128]{2,1,0:T(8,128)} %get-tuple-element.17), calls=%async_computation.2 | async-start | bytes 131072 | tf_op jit(solution)/shard_map/all_to_all | solution.py:50
  62.6 3.4 %copy-start.1 = (f32[2048,1024]{1,0:T(8,128)S(1)}, f32[2048,1024]{1,0:T(8,128)}, u32[]{:S(2)}) copy-start(f32[2048,1024]{1,0:T(8,128)} %copy-done) | copy-start | bytes 25165828
  68.5 53.7 %all-to-all-start.3 = ((f32[32,8,128]{2,1,0:T(8,128)}), f32[32,8,128]{2,1,0:T(8,128)S(1)}, u32[]{:S(2)}, u32[]{:S(2)}) async-start(f32[32,8,128]{2,1,0:T(8,128)} %get-tuple-element.19), calls=%async_computation.3 | async-start | bytes 262144 | tf_op jit(solution)/shard_map/all_to_all | solution.py:50
  121.3 0.8 copy-start.7
  122.2 3.4 %copy-start.2 = (f32[2048,1024]{1,0:T(8,128)S(1)}, f32[2048,1024]{1,0:T(8,128)}, u32[]{:S(2)}) copy-start(f32[2048,1024]{1,0:T(8,128)} %copy-done) | copy-start | bytes 25165828
  128.2 9.4 %all-to-all-start.4 = ((f32[8,16,128]{2,1,0:T(8,128)}), f32[8,16,128]{2,1,0:T(8,128)S(1)}, u32[]{:S(2)}, u32[]{:S(2)}) async-start(f32[8,16,128]{2,1,0:T(8,128)} %shard_map.39), calls=%async_computation.4 | async-start | bytes 131072 | tf_op jit(solution)/shard_map/all_to_all | solution.py:50
  134.4 3.2 %copy-start.6 = (f32[2048,1024]{1,0:T(8,128)}, f32[2048,1024]{1,0:T(8,128)S(1)}, u32[]{:S(2)}) copy-start(f32[2048,1024]{1,0:T(8,128)S(1)} %get-tuple-element.26.student_exp_ref) | copy-start | bytes 25165828
  137.6 3.4 %copy-start.3 = (f32[2048,1024]{1,0:T(8,128)S(1)}, f32[2048,1024]{1,0:T(8,128)}, u32[]{:S(2)}) copy-start(f32[2048,1024]{1,0:T(8,128)} %copy-done) | copy-start | bytes 25165828
  141.0 19.9 %copy-start.4 = (f32[2048,1024]{1,0:T(8,128)S(1)}, f32[2048,1024]{1,0:T(8,128)}, u32[]{:S(2)}) copy-start(f32[2048,1024]{1,0:T(8,128)} %copy-done) | copy-start | bytes 25165828
  174.9 15.5 %all-to-all-start.7 = ((f32[32,8,128]{2,1,0:T(8,128)}), f32[32,8,128]{2,1,0:T(8,128)S(1)}, u32[]{:S(2)}, u32[]{:S(2)}) async-start(f32[32,8,128]{2,1,0:T(8,128)} %get-tuple-element.23), calls=%async_computation.7 | async-start | bytes 262144 | tf_op jit(solution)/shard_map/all_to_all | solution.py:50
  190.4 3.4 %copy-start.5 = (f32[2048,1024]{1,0:T(8,128)S(1)}, f32[2048,1024]{1,0:T(8,128)}, u32[]{:S(2)}) copy-start(f32[2048,1024]{1,0:T(8,128)} %copy-done) | copy-start | bytes 25165828
  201.0 2.0 collective-permute-start.4
  215.6 3.4 %collective-permute-start.5 = (f32[256,256]{1,0:T(8,128)S(1)}, f32[256,256]{1,0:T(8,128)S(1)}, u32[]{:S(2)}, u32[]{:S(2)}) collective-permute-start(f32[256,256]{1,0:T(8,128)S(1)} %convert_reduce_fusion), channel_id=1, source_target_pairs={{128,0},{129,1},{130,2},{131,3},{132,4},{133,5},{134,6},{135,7},{1... | collective-permute-start | bytes 786440 | tf_op jit(solution)/shard_map/ppermute | solution.py:353

commit v2 on v0

v2 whole, which is shorter than its diff:
```python
import functools

import jax
import jax.numpy as jnp
from jax import lax
from jax.experimental import pallas as pl
from jax.experimental.pallas import tpu as pltpu
from jax.sharding import PartitionSpec as P

PROTOS = 65536
PATCHES = 256
MOMENTUM = 0.994
TEACHER_TEMP = 0.07
STUDENT_TEMP = 0.1
EPS = 1e-06

AXES = ("grp", "img", "tp")
N_GRP, N_IMG, N_TP = 2, 16, 8
N_Y = 4
BLOCK = 512
OWN_ROWS = 64
PACK = 2 * OWN_ROWS + 16
ROWS = N_IMG * OWN_ROWS
COLS = N_Y * BLOCK
N_ROWGRP = 32
N_COLGRP = 8
VMEM_LIMIT = 16 * 1024 * 1024


def coordinates(device):
    grp, rest = divmod(device, N_IMG * N_TP)
    img, tp = divmod(rest, N_TP)
    x_lo, y = divmod(tp, N_Y)
    return grp, img, x_lo, y


def groups_of(key):
    found = {}
    for device in range(N_GRP * N_IMG * N_TP):
        found.setdefault(key(*coordinates(device)), []).append(device)
    return list(found.values())


COL_GROUPS = groups_of(lambda grp, img, x_lo, y: (img, x_lo))
ROW_GROUPS = groups_of(lambda grp, img, x_lo, y: (grp, y))


def exchange(blocks, groups):
    return lax.all_to_all(blocks, AXES, 0, 0, axis_index_groups=groups, tiled=True)


def swapped(block):
    return lax.ppermute(block, "grp", [(0, 1), (1, 0)])


def from_y(block, distance, only_student=False):
    route = []
    for grp in range(1 if only_student else N_GRP):
        for rest in range(N_IMG * N_TP):
            base = grp * N_IMG * N_TP + rest // N_Y * N_Y
            y = rest % N_Y
            route.append((base + (y + distance) % N_Y, base + y))
    return lax.ppermute(block, AXES, route)


def unit_rows(values):
    return (values / jnp.sqrt(jnp.sum(values * values, -1, keepdims=True) + EPS)).astype(
        jnp.bfloat16
    )


def diagonal():
    return lax.broadcasted_iota(jnp.int32, (128, 128), 0) == lax.broadcasted_iota(
        jnp.int32, (128, 128), 1
    )


def to_row(column):
    return jnp.sum(jnp.where(diagonal(), column, 0.0), axis=0, keepdims=True)


def to_column(row):
    return jnp.sum(jnp.where(diagonal(), row, 0.0), axis=1, keepdims=True)


def lanes(pieces):
    return jnp.concatenate([pieces[k : k + 1, :] for k in range(pieces.shape[0])], axis=1)


def pieces_of(row):
    return jnp.concatenate([row[:, k * 128 : (k + 1) * 128] for k in range(8)], axis=0)


def token_kernel(place_ref, features_ref, other_ref, mask_ref, out_ref):
    grp, y = place_ref[0], place_ref[1]
    start = pl.multiple_of(y * (2 * OWN_ROWS) + grp * OWN_ROWS, OWN_ROWS)
    own = unit_rows(features_ref[pl.ds(start, OWN_ROWS), :].astype(jnp.float32))
    other = unit_rows(other_ref[...].astype(jnp.float32))
    student = jnp.where(grp == 0, own, other)
    teacher = jnp.where(grp == 0, other, own)
    crop = mask_ref[pl.ds(y // 2 * 2, 2), :].astype(jnp.float32)
    count = jnp.maximum(jnp.sum(crop), 1.0)
    weight = mask_ref[pl.ds(y, 1), :].astype(jnp.float32) / (STUDENT_TEMP * count)
    weight = jnp.where(grp == 0, weight, pltpu.roll(weight, 64, 1))
    weight = jnp.broadcast_to(jnp.concatenate([weight, weight], axis=1), (16, 256))
    weight = weight.astype(jnp.bfloat16)
    for k in range(N_IMG):
        out_ref[k, 0:OWN_ROWS, :] = teacher
        out_ref[k, OWN_ROWS : 2 * OWN_ROWS, :] = student
        out_ref[k, 2 * OWN_ROWS : PACK, :] = weight


def proto_kernel(place_ref, own_ref, other_ref, master_ref, unit_ref):
    own = own_ref[...]
    blended = MOMENTUM * own + (1.0 - MOMENTUM) * other_ref[...]
    master = jnp.where(place_ref[0] == 1, blended, own)
    master_ref[...] = master
    unit_ref[...] = unit_rows(master)


def exp_kernel(*refs):
    place_ref, pack_ref = refs[:2]
    own_refs, other_refs = refs[2:6], refs[6:10]
    teacher_ref, student_ref, parts_ref, total_ref, token_ref, weight_ref = refs[10:16]
    scratch_ref, vector_ref, wide_ref = refs[16:]
    grp, y = place_ref[0], place_ref[1]
    left = lax.broadcasted_iota(jnp.int32, (1, 128), 1) < OWN_ROWS
    for k in range(N_IMG):
        rows = slice(k * OWN_ROWS, (k + 1) * OWN_ROWS)
        scratch_ref[rows, :] = pack_ref[k, 0:OWN_ROWS, :]
        token_ref[rows, :] = pack_ref[k, OWN_ROWS : 2 * OWN_ROWS, :]
    for k in range(N_IMG // 2):
        first, second = (
            pack_ref[2 * k + j, 2 * OWN_ROWS : PACK, 0:128].astype(jnp.float32)[0:1, :]
            for j in range(2)
        )
        weight_ref[k : k + 1, :] = jnp.where(left, first, pltpu.roll(second, 64, 1))

    def logits_of(protos, tokens):
        return lax.dot_general(
            protos, tokens, (((1,), (1,)), ((), ())), preferred_element_type=jnp.float32
        )

    wide_ref[...] = jnp.zeros_like(wide_ref)
    for k in range(N_Y):
        base = (y + k) % N_Y * BLOCK

        @pl.loop(0, BLOCK // 256)
        def _(i):
            own = own_refs[k][pl.ds(i * 256, 256), :]
            other = other_refs[k][pl.ds(i * 256, 256), :]
            student = jnp.where(grp == 0, own, other)
            teacher = jnp.where(grp == 0, other, own)
            rows = pl.ds(pl.multiple_of(base + i * 256, 256), 256)

            values = jnp.exp(logits_of(teacher, scratch_ref[...]) * (1.0 / TEACHER_TEMP))
            teacher_ref[rows, :] = values
            folded = sum(values[:, k * 128 : (k + 1) * 128] for k in range(8))
            column = jnp.sum(folded, axis=1, keepdims=True)
            for h in range(2):
                vector_ref[pl.ds(base // 128 + i * 2 + h, 1), :] = to_row(
                    column[h * 128 : (h + 1) * 128]
                )

            values = jnp.exp(logits_of(student, token_ref[...]) * (1.0 / STUDENT_TEMP))
            student_ref[rows, :] = values
            wide_ref[...] += jnp.sum(values.reshape(32, 8, ROWS), axis=0)

    total_ref[...] = pieces_of(jnp.sum(wide_ref[...], axis=0, keepdims=True))
    for k in range(N_COLGRP):
        parts_ref[k] = vector_ref[...]


def row_kernel(with_student, *refs):
    if with_student:
        parts_ref, exp_ref, student_ref, out_ref, scale_ref = refs
    else:
        parts_ref, exp_ref, out_ref, scale_ref = refs
    scale = 1.0 / jnp.sum(parts_ref[...], axis=0)
    scale_ref[...] = scale
    total = jnp.zeros((8, ROWS), jnp.float32)
    for j in range(COLS // 128):
        weighted = exp_ref[j * 128 : (j + 1) * 128, :] * to_column(scale[j : j + 1, :])
        total += jnp.sum(weighted.reshape(16, 8, ROWS), axis=0)
    mine = pieces_of(jnp.sum(total, axis=0, keepdims=True))
    for k in range(N_ROWGRP):
        out_ref[k, 0:8, :] = mine
        if with_student:
            out_ref[k, 8:16, :] = student_ref[...]


def col_kernel(with_student, *refs):
    if with_student:
        parts_ref, exp_ref, out_ref, student_ref, vector_ref = refs
    else:
        parts_ref, exp_ref, out_ref, vector_ref = refs
    inverse = 1.0 / jnp.sum(parts_ref[...], axis=0)
    row = lanes(inverse[0:8, :])
    if with_student:
        student_ref[...] = inverse[8:16, :]
    for j in range(COLS // 128):
        weighted = exp_ref[j * 128 : (j + 1) * 128, :] * row
        folded = sum(weighted[:, k * 128 : (k + 1) * 128] for k in range(8))
        vector_ref[j : j + 1, :] = to_row(jnp.sum(folded, axis=1, keepdims=True))
    for k in range(N_COLGRP):
        out_ref[k] = vector_ref[...]


def grad_kernel(
    parts_ref,
    scale_ref,
    student_ref,
    weight_ref,
    teacher_exp_ref,
    student_exp_ref,
    token_ref,
    own_ref,
    sent_ref,
):
    row_inverse = lanes(1.0 / jnp.sum(parts_ref[...], axis=0))
    student_inverse = lanes(student_ref[...])
    weight = lanes(weight_ref[...])

    @pl.loop(0, COLS // 256)
    def _(i):
        errors = []
        for h in range(2):
            j = i * 2 + h
            column = to_column(scale_ref[pl.ds(j, 1), :])
            rows = pl.ds(j * 128, 128)
            targets = (teacher_exp_ref[rows, :] * column * row_inverse).astype(jnp.bfloat16)
            probs = student_exp_ref[rows, :] * student_inverse
            errors.append(
                (PROTOS * (probs - targets.astype(jnp.float32)) * weight).astype(jnp.bfloat16)
            )
        gradient = jnp.dot(
            jnp.concatenate(errors, axis=0), token_ref[...], preferred_element_type=jnp.float32
        )
        own_ref[pl.ds(i * 256, 256), :] = gradient
        sent_ref[pl.ds(i * 256, 256), :] = gradient.astype(jnp.bfloat16)


def split_kernel(place_ref, own_ref, received_ref, mine_ref, *out_refs):
    y = place_ref[1]
    for k in range(N_Y):
        rows = pl.ds(pl.multiple_of((y + k) % N_Y * BLOCK, BLOCK), BLOCK)
        block = own_ref[rows, :] + received_ref[rows, :].astype(jnp.float32)
        if k == 0:
            mine_ref[...] = block
        else:
            out_refs[k - 1][...] = block.astype(jnp.bfloat16)


def call(kernel, outs, scratch, *args, flops=0, transcendentals=0):
    vmem = pl.BlockSpec(memory_space=pltpu.VMEM)
    smem = pl.BlockSpec(memory_space=pltpu.SMEM)
    return pl.pallas_call(
        kernel,
        out_shape=outs,
        in_specs=[smem if a.ndim == 1 else vmem for a in args],
        out_specs=[vmem] * len(outs),
        scratch_shapes=scratch,
        compiler_params=pltpu.CompilerParams(vmem_limit_bytes=VMEM_LIMIT),
        cost_estimate=pl.CostEstimate(
            flops=flops, transcendentals=transcendentals, bytes_accessed=COLS * ROWS * 4
        ),
    )(*args)


def shape(dims, dtype=jnp.float32):
    return jax.ShapeDtypeStruct(dims, dtype)


def per_device(features, masters, patch_mask):
    grp = lax.axis_index("grp")
    y = lax.axis_index("tp") % N_Y
    teacher = grp == 1
    place = jnp.stack([grp, y]).astype(jnp.int32)
    work = COLS * ROWS

    own_master = masters[0]
    other_master = lax.ppermute(own_master, "grp", [(0, 1)])
    start = y * (2 * OWN_ROWS)
    lent_rows = lax.dynamic_slice_in_dim(features[0], start + (1 - grp) * OWN_ROWS, OWN_ROWS)
    other_rows = swapped(lent_rows)

    (pack,) = call(
        token_kernel,
        [shape((N_IMG, PACK, 256), jnp.bfloat16)],
        [],
        place,
        features[0],
        other_rows,
        patch_mask.reshape(4, 128),
    )
    packs = lax.all_to_all(pack, "img", 0, 0, tiled=True)

    master, unit = call(
        proto_kernel,
        [shape((BLOCK, 256)), shape((BLOCK, 256), jnp.bfloat16)],
        [],
        place,
        own_master,
        other_master,
    )
    own_units = [unit] + [from_y(unit, k) for k in range(1, N_Y)]
    other_units = [swapped(block) for block in own_units]

    teacher_exp, student_exp, col_parts, student_part, student_tokens, weights = call(
        exp_kernel,
        [
            shape((COLS, ROWS)),
            shape((COLS, ROWS)),
            shape((N_COLGRP, 16, 128)),
            shape((8, 128)),
            shape((ROWS, 256), jnp.bfloat16),
            shape((8, 128)),
        ],
        [
            pltpu.VMEM((ROWS, 256), jnp.bfloat16),
            pltpu.VMEM((16, 128), jnp.float32),
            pltpu.VMEM((8, ROWS), jnp.float32),
        ],
        place,
        packs,
        *own_units,
        *other_units,
        flops=4 * work * 256,
        transcendentals=2 * work,
    )

    for sweep in range(3):
        with_student = sweep == 0
        col_parts = exchange(col_parts, COL_GROUPS)
        row_parts, col_scale = call(
            functools.partial(row_kernel, with_student),
            [shape((N_ROWGRP, 16 if with_student else 8, 128)), shape((16, 128))],
            [],
            col_parts,
            teacher_exp,
            *((student_part,) if with_student else ()),
            flops=2 * work,
        )
        row_parts = exchange(row_parts, ROW_GROUPS)
        if sweep < 2:
            col_parts, *rest = call(
                functools.partial(col_kernel, with_student),
                [shape((N_COLGRP, 16, 128))] + [shape((8, 128))] * with_student,
                [pltpu.VMEM((16, 128), jnp.float32)],
                row_parts,
                teacher_exp,
                flops=2 * work,
            )
            if with_student:
                (student_inverse,) = rest

    own_grad, sent_grad = call(
        grad_kernel,
        [shape((COLS, 256)), shape((COLS, 256), jnp.bfloat16)],
        [],
        row_parts,
        col_scale,
        student_inverse,
        weights,
        teacher_exp,
        student_exp,
        student_tokens,
        flops=2 * work * 256,
    )
    received = lax.ppermute(sent_grad, "grp", [(1, 0)])
    mine, *outgoing = call(
        split_kernel,
        [shape((BLOCK, 256))] + [shape((BLOCK, 256), jnp.bfloat16)] * 3,
        [],
        place,
        own_grad,
        received,
    )
    gradient = mine
    for k, block in enumerate(outgoing, 1):
        gradient = gradient + from_y(block, -k, True).astype(jnp.float32)
    return jnp.where(teacher, master, gradient)[None]


def solution(mesh):
    in_specs = (P("grp", "img", None), P("grp", ("img", "tp"), None), P("img"))
    out_specs = P("grp", ("img", "tp"), None)
    return jax.shard_map(
        per_device, mesh=mesh, in_specs=in_specs, out_specs=out_specs, check_vma=False
    )
```

time: 760 us -> 156 us (0.21); the launches traced: 751 us -> 155 us
  waiting for transfers between devices: 337 us -> 31.8 us
  blocking collectives: 272 us -> 72.7 us
  matrix products: 104 us -> 0 us
  starting transfers between devices: 3.08 us -> 29.2 us
  Pallas kernels: 0 us -> 15.8 us
  other arithmetic: 14.7 us -> 0.99 us
  between operations: 13.7 us -> 0.12 us
    psum x6 -> x0, blocking collectives: 272 us -> none  [the longest x3 219 us: per_device(): lax.psum(jnp.dot(row_scale, exponent, precision=lax.Precision.HIGHEST), '...]
    reduce_scatter x1 -> x0, waiting for transfers between devices: 221 us -> none  [per_device(): lax.psum_scatter(jnp.einsum('rp,rk->pk', error_rows, token_unit, preferre...]
    dot_general x8 -> x0, matrix products: 104 us -> none  [the longest x3 52.9 us: per_device(): jnp.dot(exponent, col_scale, precision=lax.Precision.HIGHEST)]
    all_gather x1 -> x0, waiting for transfers between devices: 101 us -> none  [per_device(): lax.all_gather(proto_unit, 'img', axis=0, tiled=True)]
    all_to_all x0 -> x6, blocking collectives: none -> 72.7 us  [exchange(): lax.all_to_all(blocks, AXES, 0, 0, axis_index_groups=groups, tiled=True)]
    ppermute x2 -> x13, starting transfers between devices: 3.04 us -> 19.1 us  [the longest x6 15.4 us: from_y(): return lax.ppermute(block, AXES, route)]
    pallas_call x0 -> x10, Pallas kernels: none -> 15.8 us  [call(): pl.pallas_call(kernel, out_shape=outs, in_specs=[smem if a.ndim == 1 else...]
    convert_element_type x3 -> x0, other arithmetic: 10.2 us -> none  [the longest x1 9.38 us: per_device(): normed.astype(jnp.bfloat16)]
  transfers between devices with their start and end apart: 4 -> 14, of which waited for: 4 -> 10; matrix products, arithmetic and copies ran while one was open for 0% -> 0% of each run, Pallas kernels for 0% -> 0%
where the time goes in v2:
time: 156 us; the launch traced here: 155 us
  blocking collectives  72.7 us (47%)
  waiting for transfers between devices  31.8 us (20%)
  starting transfers between devices  29.2 us (19%)
  Pallas kernels  15.8 us (10%)
  local copies, waits for them, and re-layouts  4.11 us (3%)
    all_to_all x6, blocking collectives, exchange(): lax.all_to_all(blocks, AXES, 0, 0, axis_index_groups=groups, tiled=True)  72.7 us
    ppermute x6, waiting for transfers between devices, from_y(): return lax.ppermute(block, AXES, route)  16.3 us
    pallas_call x10, Pallas kernels, call(): pl.pallas_call(kernel, out_shape=outs, in_specs=[smem if a.ndim == 1 else...  15.8 us
    ppermute x6, starting transfers between devices, from_y(): return lax.ppermute(block, AXES, route)  15.4 us
    all_to_all x1, starting transfers between devices, per_device(): packs = lax.all_to_all(pack, 'img', 0, 0, tiled=True)  10.1 us
    all_to_all x1, waiting for transfers between devices, per_device(): packs = lax.all_to_all(pack, 'img', 0, 0, tiled=True)  8.21 us
    unnamed x10, local copies, waits for them, and re-layouts  3.29 us
    ppermute x1, waiting for transfers between devices, per_device(): received = lax.ppermute(sent_grad, 'grp', [(1, 0)])  3.25 us
  transfers between devices with their start and end apart: 14, of which 10 were waited for; matrix products, arithmetic and copies ran while one was open for 0% of the time, Pallas kernels for 0%

profile of v2, /device:TPU:2, one launch (start us, length us, event | category | flops | bytes accessed | tf_op | source)
XLA Modules:
  0.0 154.7 jit_solution(2187883869712345953)
XLA Ops:
  0.0 0.8 dynamic-slice_bitcast_fusion
  0.8 0.0 collective-permute-start.1
  0.8 0.1 pad_add_fusion.place_ref.refs_0_
  0.9 1.1 collective-permute-done.1.other_ref
  2.0 0.9 copy-done.1
  3.0 0.7 copy-done.2
  3.7 1.8 %shard_map.38 = bf16[16,144,256]{2,1,0:T(8,128)(2,1)} custom-call(s32[2]{0:T(128)S(1)} %pad_add_fusion.place_ref.refs_0_, bf16[512,256]{1,0:T(8,128)(2,1)S(1)} %bitcast.11, bf16[64,256]{1,0:T(8,128)(2,1)S(1)} %collective-permute-done.1.other_ref, s32[4,128]{1,0:T(4,128)S(1)} %bitcast.12), custom_call_target="tpu_custom_call" | custom-call | bytes 8388608 | tf_op jit(solution)/shard_map/pallas_call | solution.py:257
  5.5 10.1 %all-to-all-start = ((bf16[16,144,256]{2,1,0:T(8,128)(2,1)}), bf16[16,144,256]{2,1,0:T(8,128)(2,1)S(1)}, u32[]{:S(2)}, u32[]{:S(2)}) async-start(bf16[16,144,256]{2,1,0:T(8,128)(2,1)} %shard_map.38), calls=%async_computation | async-start | bytes 2359296 | tf_op jit(solution)/shard_map/all_to_all | solution.py:296
  15.6 1.8 %collective-permute-start = (f32[512,256]{1,0:T(8,128)S(1)}, f32[512,256]{1,0:T(8,128)S(1)}, u32[]{:S(2)}, u32[]{:S(2)}) collective-permute-start(f32[512,256]{1,0:T(8,128)S(1)} %bitcast.9), channel_id=1, source_target_pairs={{0,128},{1,129},{2,130},{3,131},{4,132},{5,133},{6,134},{7,135},{8... | collective-permute-start | bytes 1572872 | tf_op jit(solution)/shard_map/ppermute | solution.py:282
  17.4 1.5 collective-permute-done.other_ref
  18.9 0.8 shard_map.37
  19.7 1.7 %collective-permute-start.4 = (bf16[512,256]{1,0:T(8,128)(2,1)S(1)}, bf16[512,256]{1,0:T(8,128)(2,1)S(1)}, u32[]{:S(2)}, u32[]{:S(2)}) collective-permute-start(bf16[512,256]{1,0:T(8,128)(2,1)S(1)} %get-tuple-element.26.refs_2_), channel_id=1, source_target_pairs={{3,0},{0,1},{1,2},{2,3},{7,4},{4,5},{5,6},{6,7},{11,8},{8,9},{9,10... | collective-permute-start | bytes 786440 | tf_op jit(solution)/shard_map/ppermute | solution.py:63
  21.4 2.9 %collective-permute-start.3 = (bf16[512,256]{1,0:T(8,128)(2,1)S(1)}, bf16[512,256]{1,0:T(8,128)(2,1)S(1)}, u32[]{:S(2)}, u32[]{:S(2)}) collective-permute-start(bf16[512,256]{1,0:T(8,128)(2,1)S(1)} %get-tuple-element.26.refs_2_), channel_id=1, source_target_pairs={{2,0},{3,1},{0,2},{1,3},{6,4},{7,5},{4,6},{5,7},{10,8},{11,9},{8,1... | collective-permute-start | bytes 786440 | tf_op jit(solution)/shard_map/ppermute | solution.py:63
  24.3 1.3 collective-permute-start.2
  25.6 0.0 collective-permute-start.5
  25.6 4.0 %collective-permute-done.4.refs_5_ = bf16[512,256]{1,0:T(8,128)(2,1)S(1)} collective-permute-done((bf16[512,256]{1,0:T(8,128)(2,1)S(1)}, bf16[512,256]{1,0:T(8,128)(2,1)S(1)}, u32[]{:S(2)}, u32[]{:S(2)}) %collective-permute-start.4) | collective-permute-done | bytes 262176 | tf_op jit(solution)/shard_map/ppermute | solution.py:63
  29.6 0.0 collective-permute-start.8
  29.6 6.8 %collective-permute-done.3.refs_4_ = bf16[512,256]{1,0:T(8,128)(2,1)S(1)} collective-permute-done((bf16[512,256]{1,0:T(8,128)(2,1)S(1)}, bf16[512,256]{1,0:T(8,128)(2,1)S(1)}, u32[]{:S(2)}, u32[]{:S(2)}) %collective-permute-start.3) | collective-permute-done | bytes 262176 | tf_op jit(solution)/shard_map/ppermute | solution.py:63
  36.4 0.0 collective-permute-start.7
  36.4 0.0 collective-permute-done.2.refs_3_
  36.4 0.5 collective-permute-start.6
  36.9 1.0 collective-permute-done.7.refs_8_
  38.0 0.4 collective-permute-done.6.refs_7_
  38.3 0.7 copy-done.3
  39.0 8.2 %all-to-all-done.refs_1_ = bf16[16,144,256]{2,1,0:T(8,128)(2,1)S(1)} async-done(((bf16[16,144,256]{2,1,0:T(8,128)(2,1)}), bf16[16,144,256]{2,1,0:T(8,128)(2,1)S(1)}, u32[]{:S(2)}, u32[]{:S(2)}) %all-to-all-start) | async-done | bytes 1179680 | tf_op jit(solution)/shard_map/all_to_all | solution.py:296
  47.3 0.9 copy-done.4
  48.2 4.9 %shard_map.39 = (f32[2048,1024]{1,0:T(8,128)S(1)}, f32[2048,1024]{1,0:T(8,128)S(1)}, f32[8,16,128]{2,1,0:T(8,128)S(1)}, f32[8,128]{1,0:T(8,128)S(1)}, bf16[1024,...) custom-call(s32[2]{0:T(128)S(1)} %pad_add_fusion.place_ref.refs_0_, bf16[16,144,256]{2,1,0:T(8,128)(2,1)S(1)} %all-to-all-done.refs_1_, ...), custom_call_target="tpu_custom_call" | custom-call | flops 2147483648 | bytes 8388608 | tf_op jit(solution)/shard_map/pallas_call | solution.py:257
  53.1 9.6 %all_to_all.35.refs_0_ = f32[8,16,128]{2,1,0:T(8,128)S(1)} all-to-all(f32[8,16,128]{2,1,0:T(8,128)S(1)} %get-tuple-element.27), channel_id=1, replica_groups={{0,1,2,3,128,129,130,131},{4,5,6,7,132,133,134,135},{8,9,10,11,136,137,..., dimensions={0} | all-to-all | bytes 131072 | tf_op jit(solution)/shard_map/all_to_all | solution.py:49
  62.7 0.8 shard_map.40
  63.6 18.3 %all_to_all.36.refs_0_ = f32[32,16,128]{2,1,0:T(8,128)S(1)} all-to-all(f32[32,16,128]{2,1,0:T(8,128)S(1)} %get-tuple-element.30), channel_id=1, replica_groups={{0,4,8,12,16,20,24,28,32,36,40,44,48,52,56,60,64,68,72,76,80,84,88,92,9..., dimensions={0} | all-to-all | bytes 524288 | tf_op jit(solution)/shard_map/all_to_all | solution.py:49
  81.9 0.7 shard_map.41
  82.6 7.7 %all_to_all.37.refs_0_ = f32[8,16,128]{2,1,0:T(8,128)S(1)} all-to-all(f32[8,16,128]{2,1,0:T(8,128)S(1)} %get-tuple-element.31), channel_id=1, replica_groups={{0,1,2,3,128,129,130,131},{4,5,6,7,132,133,134,135},{8,9,10,11,136,137,..., dimensions={0} | all-to-all | bytes 131072 | tf_op jit(solution)/shard_map/all_to_all | solution.py:49
  90.3 0.8 shard_map.42
  91.1 14.7 %all_to_all.38.refs_0_ = f32[32,8,128]{2,1,0:T(8,128)S(1)} all-to-all(f32[32,8,128]{2,1,0:T(8,128)S(1)} %get-tuple-element.32), channel_id=1, replica_groups={{0,4,8,12,16,20,24,28,32,36,40,44,48,52,56,60,64,68,72,76,80,84,88,92,9..., dimensions={0} | all-to-all | bytes 262144 | tf_op jit(solution)/shard_map/all_to_all | solution.py:49
  105.8 0.7 shard_map.43
  106.5 7.7 %all_to_all.39.refs_0_ = f32[8,16,128]{2,1,0:T(8,128)S(1)} all-to-all(f32[8,16,128]{2,1,0:T(8,128)S(1)} %shard_map.43), channel_id=1, replica_groups={{0,1,2,3,128,129,130,131},{4,5,6,7,132,133,134,135},{8,9,10,11,136,137,..., dimensions={0} | all-to-all | bytes 131072 | tf_op jit(solution)/shard_map/all_to_all | solution.py:49
  114.2 0.7 shard_map.44
  114.9 14.6 %all_to_all.40.parts_ref = f32[32,8,128]{2,1,0:T(8,128)S(1)} all-to-all(f32[32,8,128]{2,1,0:T(8,128)S(1)} %get-tuple-element.33), channel_id=1, replica_groups={{0,4,8,12,16,20,24,28,32,36,40,44,48,52,56,60,64,68,72,76,80,84,88,92,9..., dimensions={0} | all-to-all | bytes 262144 | tf_op jit(solution)/shard_map/all_to_all | solution.py:49
  129.6 3.9 %shard_map.45 = (f32[2048,256]{1,0:T(8,128)S(1)}, bf16[2048,256]{1,0:T(8,128)(2,1)S(1)}) custom-call(f32[32,8,128]{2,1,0:T(8,128)S(1)} %all_to_all.40.parts_ref, f32[16,128]{1,0:T(8,128)S(1)} %get-tuple-element.34.scale_ref, f32[8,128]{1,0:T(8,128)S(1)} %get-tuple-element.35.student_ref, f32[8,128]{1,0:T(8,128)S(1)} %get-tuple-element.36.weight_ref, ...), custom_call_target="tpu_custom_call" | custom-call | flops 1073741824 | bytes 8388608 | tf_op jit(solution)/shard_map/pallas_call | solution.py:257
  133.4 1.3 collective-permute-start.9
  134.7 3.3 %collective-permute-done.9.received_ref = bf16[2048,256]{1,0:T(8,128)(2,1)S(1)} collective-permute-done((bf16[2048,256]{1,0:T(8,128)(2,1)S(1)}, bf16[2048,256]{1,0:T(8,128)(2,1)S(1)}, u32[]{:S(2)}, u32[]{:S(2)}) %collective-permute-start.9) | collective-permute-done | bytes 1048608 | tf_op jit(solution)/shard_map/ppermute | solution.py:370
  138.0 0.7 shard_map.46
  138.7 2.6 %collective-permute-start.10 = (bf16[512,256]{1,0:T(8,128)(2,1)S(1)}, bf16[512,256]{1,0:T(8,128)(2,1)S(1)}, u32[]{:S(2)}, u32[]{:S(2)}) collective-permute-start(bf16[512,256]{1,0:T(8,128)(2,1)S(1)} %get-tuple-element.42), channel_id=1, source_target_pairs={{3,0},{0,1},{1,2},{2,3},{7,4},{4,5},{5,6},{6,7},{11,8},{8,9},{9,10... | collective-permute-start | bytes 786440 | tf_op jit(solution)/shard_map/ppermute | solution.py:63
  141.4 3.7 %collective-permute-start.11 = (bf16[512,256]{1,0:T(8,128)(2,1)S(1)}, bf16[512,256]{1,0:T(8,128)(2,1)S(1)}, u32[]{:S(2)}, u32[]{:S(2)}) collective-permute-start(bf16[512,256]{1,0:T(8,128)(2,1)S(1)} %get-tuple-element.43), channel_id=1, source_target_pairs={{2,0},{3,1},{0,2},{1,3},{6,4},{7,5},{4,6},{5,7},{10,8},{11,9},{8,1... | collective-permute-start | bytes 786440 | tf_op jit(solution)/shard_map/ppermute | solution.py:63
  145.1 3.2 %collective-permute-start.12 = (bf16[512,256]{1,0:T(8,128)(2,1)S(1)}, bf16[512,256]{1,0:T(8,128)(2,1)S(1)}, u32[]{:S(2)}, u32[]{:S(2)}) collective-permute-start(bf16[512,256]{1,0:T(8,128)(2,1)S(1)} %get-tuple-element.44), channel_id=1, source_target_pairs={{1,0},{2,1},{3,2},{0,3},{5,4},{6,5},{7,6},{4,7},{9,8},{10,9},{11,1... | collective-permute-start | bytes 786440 | tf_op jit(solution)/shard_map/ppermute | solution.py:63
  148.3 2.9 %collective-permute-done.11 = bf16[512,256]{1,0:T(8,128)(2,1)S(1)} collective-permute-done((bf16[512,256]{1,0:T(8,128)(2,1)S(1)}, bf16[512,256]{1,0:T(8,128)(2,1)S(1)}, u32[]{:S(2)}, u32[]{:S(2)}) %collective-permute-start.11) | collective-permute-done | bytes 262176 | tf_op jit(solution)/shard_map/ppermute | solution.py:63
  151.2 2.6 %collective-permute-done.12 = bf16[512,256]{1,0:T(8,128)(2,1)S(1)} collective-permute-done((bf16[512,256]{1,0:T(8,128)(2,1)S(1)}, bf16[512,256]{1,0:T(8,128)(2,1)S(1)}, u32[]{:S(2)}, u32[]{:S(2)}) %collective-permute-start.12) | collective-permute-done | bytes 262176 | tf_op jit(solution)/shard_map/ppermute | solution.py:63
  153.8 0.9 select_bitcast_fusion
  (9 shorter events, 0.0 us)
Async XLA Ops:
  0.0 15.6 %copy-start = (f32[1,512,256]{2,1,0:T(8,128)S(1)}, f32[1,512,256]{2,1,0:T(8,128)}, u32[]{:S(2)}) copy-start(f32[1,512,256]{2,1,0:T(8,128)} %param.4) | copy-start | bytes 1572868
  0.8 1.2 collective-permute-start.1
  2.0 1.0 copy-start.1
  3.0 0.7 copy-start.2
  5.5 41.8 %all-to-all-start = ((bf16[16,144,256]{2,1,0:T(8,128)(2,1)}), bf16[16,144,256]{2,1,0:T(8,128)(2,1)S(1)}, u32[]{:S(2)}, u32[]{:S(2)}) async-start(bf16[16,144,256]{2,1,0:T(8,128)(2,1)} %shard_map.38), calls=%async_computation | async-start | bytes 2359296 | tf_op jit(solution)/shard_map/all_to_all | solution.py:296
  15.6 3.3 %collective-permute-start = (f32[512,256]{1,0:T(8,128)S(1)}, f32[512,256]{1,0:T(8,128)S(1)}, u32[]{:S(2)}, u32[]{:S(2)}) collective-permute-start(f32[512,256]{1,0:T(8,128)S(1)} %bitcast.9), channel_id=1, source_target_pairs={{0,128},{1,129},{2,130},{3,131},{4,132},{5,133},{6,134},{7,135},{8... | collective-permute-start | bytes 1572872 | tf_op jit(solution)/shard_map/ppermute | solution.py:282
  19.7 9.9 %collective-permute-start.4 = (bf16[512,256]{1,0:T(8,128)(2,1)S(1)}, bf16[512,256]{1,0:T(8,128)(2,1)S(1)}, u32[]{:S(2)}, u32[]{:S(2)}) collective-permute-start(bf16[512,256]{1,0:T(8,128)(2,1)S(1)} %get-tuple-element.26.refs_2_), channel_id=1, source_target_pairs={{3,0},{0,1},{1,2},{2,3},{7,4},{4,5},{5,6},{6,7},{11,8},{8,9},{9,10... | collective-permute-start | bytes 786440 | tf_op jit(solution)/shard_map/ppermute | solution.py:63
  21.4 15.1 %collective-permute-start.3 = (bf16[512,256]{1,0:T(8,128)(2,1)S(1)}, bf16[512,256]{1,0:T(8,128)(2,1)S(1)}, u32[]{:S(2)}, u32[]{:S(2)}) collective-permute-start(bf16[512,256]{1,0:T(8,128)(2,1)S(1)} %get-tuple-element.26.refs_2_), channel_id=1, source_target_pairs={{2,0},{3,1},{0,2},{1,3},{6,4},{7,5},{4,6},{5,7},{10,8},{11,9},{8,1... | collective-permute-start | bytes 786440 | tf_op jit(solution)/shard_map/ppermute | solution.py:63
  24.3 12.2 %collective-permute-start.2 = (bf16[512,256]{1,0:T(8,128)(2,1)S(1)}, bf16[512,256]{1,0:T(8,128)(2,1)S(1)}, u32[]{:S(2)}, u32[]{:S(2)}) collective-permute-start(bf16[512,256]{1,0:T(8,128)(2,1)S(1)} %get-tuple-element.26.refs_2_), channel_id=1, source_target_pairs={{1,0},{2,1},{3,2},{0,3},{5,4},{6,5},{7,6},{4,7},{9,8},{10,9},{11,1... | collective-permute-start | bytes 786440 | tf_op jit(solution)/shard_map/ppermute | solution.py:63
  25.6 11.3 %collective-permute-start.5 = (bf16[512,256]{1,0:T(8,128)(2,1)S(1)}, bf16[512,256]{1,0:T(8,128)(2,1)S(1)}, u32[]{:S(2)}, u32[]{:S(2)}) collective-permute-start(bf16[512,256]{1,0:T(8,128)(2,1)S(1)} %get-tuple-element.26.refs_2_), channel_id=1, source_target_pairs={{0,128},{128,0},{1,129},{129,1},{2,130},{130,2},{3,131},{131,3},{4... | collective-permute-start | bytes 786440 | tf_op jit(solution)/shard_map/ppermute | solution.py:53
  29.6 7.3 %collective-permute-start.8 = (bf16[512,256]{1,0:T(8,128)(2,1)S(1)}, bf16[512,256]{1,0:T(8,128)(2,1)S(1)}, u32[]{:S(2)}, u32[]{:S(2)}) collective-permute-start(bf16[512,256]{1,0:T(8,128)(2,1)S(1)} %collective-permute-done.4.refs_5_), channel_id=1, source_target_pairs={{0,128},{128,0},{1,129},{129,1},{2,130},{130,2},{3,131},{131,3},{4... | collective-permute-start | bytes 786440 | tf_op jit(solution)/shard_map/ppermute | solution.py:53
  36.4 1.5 collective-permute-start.7
  36.4 1.9 %collective-permute-start.6 = (bf16[512,256]{1,0:T(8,128)(2,1)S(1)}, bf16[512,256]{1,0:T(8,128)(2,1)S(1)}, u32[]{:S(2)}, u32[]{:S(2)}) collective-permute-start(bf16[512,256]{1,0:T(8,128)(2,1)S(1)} %collective-permute-done.2.refs_3_), channel_id=1, source_target_pairs={{0,128},{128,0},{1,129},{129,1},{2,130},{130,2},{3,131},{131,3},{4... | collective-permute-start | bytes 786440 | tf_op jit(solution)/shard_map/ppermute | solution.py:53
  38.3 0.7 copy-start.3
  47.3 1.0 copy-start.4
  133.4 4.6 %collective-permute-start.9 = (bf16[2048,256]{1,0:T(8,128)(2,1)S(1)}, bf16[2048,256]{1,0:T(8,128)(2,1)S(1)}, u32[]{:S(2)}, u32[]{:S(2)}) collective-permute-start(bf16[2048,256]{1,0:T(8,128)(2,1)S(1)} %get-tuple-element.40), channel_id=1, source_target_pairs={{128,0},{129,1},{130,2},{131,3},{132,4},{133,5},{134,6},{135,7},{1... | collective-permute-start | bytes 3145736 | tf_op jit(solution)/shard_map/ppermute | solution.py:370
  138.7 9.6 %collective-permute-start.10 = (bf16[512,256]{1,0:T(8,128)(2,1)S(1)}, bf16[512,256]{1,0:T(8,128)(2,1)S(1)}, u32[]{:S(2)}, u32[]{:S(2)}) collective-permute-start(bf16[512,256]{1,0:T(8,128)(2,1)S(1)} %get-tuple-element.42), channel_id=1, source_target_pairs={{3,0},{0,1},{1,2},{2,3},{7,4},{4,5},{5,6},{6,7},{11,8},{8,9},{9,10... | collective-permute-start | bytes 786440 | tf_op jit(solution)/shard_map/ppermute | solution.py:63
  141.4 9.8 %collective-permute-start.11 = (bf16[512,256]{1,0:T(8,128)(2,1)S(1)}, bf16[512,256]{1,0:T(8,128)(2,1)S(1)}, u32[]{:S(2)}, u32[]{:S(2)}) collective-permute-start(bf16[512,256]{1,0:T(8,128)(2,1)S(1)} %get-tuple-element.43), channel_id=1, source_target_pairs={{2,0},{3,1},{0,2},{1,3},{6,4},{7,5},{4,6},{5,7},{10,8},{11,9},{8,1... | collective-permute-start | bytes 786440 | tf_op jit(solution)/shard_map/ppermute | solution.py:63
  145.1 8.7 %collective-permute-start.12 = (bf16[512,256]{1,0:T(8,128)(2,1)S(1)}, bf16[512,256]{1,0:T(8,128)(2,1)S(1)}, u32[]{:S(2)}, u32[]{:S(2)}) collective-permute-start(bf16[512,256]{1,0:T(8,128)(2,1)S(1)} %get-tuple-element.44), channel_id=1, source_target_pairs={{1,0},{2,1},{3,2},{0,3},{5,4},{6,5},{7,6},{4,7},{9,8},{10,9},{11,1... | collective-permute-start | bytes 786440 | tf_op jit(solution)/shard_map/ppermute | solution.py:63

commit v3 on v2

v3 whole, which is shorter than its diff:
```python
import functools

import jax
import jax.numpy as jnp
from jax import lax
from jax.experimental import pallas as pl
from jax.experimental.pallas import tpu as pltpu
from jax.sharding import PartitionSpec as P

PROTOS = 65536
PATCHES = 256
MOMENTUM = 0.994
TEACHER_TEMP = 0.07
STUDENT_TEMP = 0.1
EPS = 1e-06
LOG2E = 1.4426950408889634

AXES = ("grp", "img", "tp")
N_GRP, N_IMG, N_TP = 2, 16, 8
N_X, N_Y, N_Z = 4, 4, 8
BLOCK = 512
HALF = 256
OWN_ROWS = 128
PACK = 2 * OWN_ROWS + 16
ROWS = N_Z * OWN_ROWS
COLS = N_X * BLOCK
N_ROWGRP = N_Y * N_Z
N_COLGRP = N_GRP * N_X
VMEM_LIMIT = 16 * 1024 * 1024


def coordinates(device):
    grp, rest = divmod(device, N_IMG * N_TP)
    img, tp = divmod(rest, N_TP)
    x_hi, z = divmod(img, N_Z)
    x_lo, y = divmod(tp, N_Y)
    return grp, x_hi * 2 + x_lo, y, z


def device_at(grp, x, y, z):
    return ((grp * 2 + x // 2) * N_Z + z) * N_TP + x % 2 * N_Y + y


def groups_of(key):
    found = {}
    for device in range(N_GRP * N_IMG * N_TP):
        found.setdefault(key(*coordinates(device)), []).append(device)
    return list(found.values())


X_GROUPS = groups_of(lambda grp, x, y, z: (grp, y, z))
COL_GROUPS = groups_of(lambda grp, x, y, z: (y, z))
ROW_GROUPS = groups_of(lambda grp, x, y, z: (grp, x))


def exchange(blocks, groups):
    return lax.all_to_all(blocks, AXES, 0, 0, axis_index_groups=groups, tiled=True)


def swapped(block):
    return lax.ppermute(block, "grp", [(0, 1), (1, 0)])


def from_x(block, distance):
    route = []
    for device in range(N_GRP * N_IMG * N_TP):
        grp, x, y, z = coordinates(device)
        route.append((device_at(grp, (x + distance) % N_X, y, z), device))
    return lax.ppermute(block, AXES, route)


def from_z(block, distance):
    route = []
    for device in range(N_GRP * N_IMG * N_TP):
        grp, x, y, z = coordinates(device)
        route.append((device_at(grp, x, y, (z + distance) % N_Z), device))
    return lax.ppermute(block, AXES, route)


def unit_rows(values):
    return (values / jnp.sqrt(jnp.sum(values * values, -1, keepdims=True) + EPS)).astype(
        jnp.bfloat16
    )


def diagonal():
    return lax.broadcasted_iota(jnp.int32, (128, 128), 0) == lax.broadcasted_iota(
        jnp.int32, (128, 128), 1
    )


def to_row(column):
    return jnp.sum(jnp.where(diagonal(), column, 0.0), axis=0, keepdims=True)


def to_column(row):
    return jnp.sum(jnp.where(diagonal(), row, 0.0), axis=1, keepdims=True)


def lanes(pieces):
    return jnp.concatenate([pieces[k : k + 1, :] for k in range(pieces.shape[0])], axis=1)


def pieces_of(row):
    return jnp.concatenate([row[:, k * 128 : (k + 1) * 128] for k in range(8)], axis=0)


def unit_kernel(
    place_ref,
    features_ref,
    other_features_ref,
    mask_ref,
    own_ref,
    other_ref,
    pack_ref,
    master_ref,
    unit_ref,
):
    grp, x = place_ref[0], place_ref[1]

    @pl.when(pl.program_id(0) == 0)
    def _():
        own = unit_rows(features_ref[...].astype(jnp.float32))
        other = unit_rows(other_features_ref[...].astype(jnp.float32))
        teacher = jnp.where(grp == 0, other, own)
        student = jnp.where(grp == 0, own, other)
        crop = mask_ref[pl.ds(x % 2 * 2, 2), :].astype(jnp.float32)
        count = jnp.maximum(jnp.sum(crop), 1.0)
        weight = mask_ref[pl.ds(x % 2 * 2 + grp, 1), :].astype(jnp.float32)
        weight = weight / (STUDENT_TEMP * count)
        weight = jnp.broadcast_to(jnp.concatenate([weight, weight], axis=1), (16, 256))
        weight = weight.astype(jnp.bfloat16)
        pack_ref[0:OWN_ROWS, :] = teacher
        pack_ref[OWN_ROWS : 2 * OWN_ROWS, :] = student
        pack_ref[2 * OWN_ROWS : PACK, :] = weight

    own_master = own_ref[...]
    blended = MOMENTUM * own_master + (1.0 - MOMENTUM) * other_ref[...]
    master = jnp.where(grp == 1, blended, own_master)
    master_ref[...] = master
    unit_ref[...] = unit_rows(master)


def in_hbm(array):
    return pltpu.with_memory_space_constraint(array, pltpu.HBM)


def unit_call(place, features, other_features, mask, own_master, other_master):
    rows = BLOCK // 4
    picked = pl.BlockSpec((OWN_ROWS, 256), lambda i, place: (place[1] % 2 * 2 + place[0], 0))
    part = pl.BlockSpec((rows, 256), lambda i, place: (i, 0))
    return pl.pallas_call(
        unit_kernel,
        out_shape=[
            shape((PACK, 256), jnp.bfloat16),
            shape((BLOCK, 256)),
            shape((BLOCK, 256), jnp.bfloat16),
        ],
        grid_spec=pltpu.PrefetchScalarGridSpec(
            num_scalar_prefetch=1,
            grid=(4,),
            in_specs=[
                picked,
                picked,
                pl.BlockSpec((4, 128), lambda i, place: (0, 0)),
                part,
                part,
            ],
            out_specs=[
                pl.BlockSpec((PACK, 256), lambda i, place: (0, 0)),
                part,
                part,
            ],
        ),
        compiler_params=pltpu.CompilerParams(vmem_limit_bytes=VMEM_LIMIT),
    )(place, in_hbm(features), other_features, mask, in_hbm(own_master), other_master)


def exp_of(protos, tokens, temperature):
    logits = lax.dot_general(
        protos, tokens, (((1,), (1,)), ((), ())), preferred_element_type=jnp.float32
    )
    return jnp.exp2(logits * (LOG2E / temperature))


def exp_kernel(*refs):
    place_ref, pack_refs = refs[0], refs[1:9]
    own_refs, other_refs = refs[9:13], refs[13:17]
    teacher_ref, student_ref, parts_ref, total_ref, token_ref, weight_ref = refs[17:23]
    scratch_ref, vector_ref = refs[23:]
    grp, x, z = place_ref[0], place_ref[1], place_ref[2]
    for k in range(N_Z):
        place = (z + k) % N_Z
        rows = pl.ds(pl.multiple_of(place * OWN_ROWS, OWN_ROWS), OWN_ROWS)
        scratch_ref[rows, :] = pack_refs[k][0:OWN_ROWS, :]
        token_ref[rows, :] = pack_refs[k][OWN_ROWS : 2 * OWN_ROWS, :]
        weight = pack_refs[k][2 * OWN_ROWS : PACK, 0:128].astype(jnp.float32)
        weight_ref[pl.ds(place, 1), :] = weight[0:1, :]
    teacher_tokens = scratch_ref[...]
    student_tokens = token_ref[...]
    total = jnp.zeros((8, ROWS), jnp.float32)
    for k in range(N_X):
        base = (x + k) % N_X * BLOCK
        for i in range(BLOCK // 256):
            block = slice(i * 256, (i + 1) * 256)
            rows = pl.ds(pl.multiple_of(base + i * 256, 256), 256)
            own, other = own_refs[k][block, :], other_refs[k][block, :]
            values = exp_of(jnp.where(grp == 0, other, own), teacher_tokens, TEACHER_TEMP)
            teacher_ref[rows, :] = values
            folded = sum(values[:, k * 128 : (k + 1) * 128] for k in range(8))
            column = jnp.sum(folded, axis=1, keepdims=True)
            for h in range(2):
                vector_ref[pl.ds(base // 128 + i * 2 + h, 1), :] = to_row(
                    column[h * 128 : (h + 1) * 128]
                )
            values = exp_of(jnp.where(grp == 0, own, other), student_tokens, STUDENT_TEMP)
            student_ref[rows, :] = values
            total += jnp.sum(values.reshape(32, 8, ROWS), axis=0)
    total_ref[...] = pieces_of(jnp.sum(total, axis=0, keepdims=True))
    for k in range(N_COLGRP):
        parts_ref[k] = vector_ref[...]


def row_kernel(with_student, *refs):
    if with_student:
        parts_ref, exp_ref, student_ref, out_ref, scale_ref = refs
    else:
        parts_ref, exp_ref, out_ref, scale_ref = refs
    scale = 1.0 / jnp.sum(parts_ref[...], axis=0)
    scale_ref[...] = scale
    total = jnp.zeros((8, ROWS), jnp.float32)
    for j in range(COLS // 128):
        weighted = exp_ref[j * 128 : (j + 1) * 128, :] * to_column(scale[j : j + 1, :])
        total += jnp.sum(weighted.reshape(16, 8, ROWS), axis=0)
    mine = pieces_of(jnp.sum(total, axis=0, keepdims=True))
    if with_student:
        mine = jnp.concatenate([mine, student_ref[...]], axis=0)
    mine = mine.astype(jnp.bfloat16)
    for k in range(N_ROWGRP):
        out_ref[k] = mine


def col_kernel(parts_ref, exp_ref, out_ref, vector_ref):
    row = lanes(1.0 / jnp.sum(parts_ref[...].astype(jnp.float32), axis=0))
    for j in range(COLS // 128):
        weighted = exp_ref[j * 128 : (j + 1) * 128, :] * row
        folded = sum(weighted[:, k * 128 : (k + 1) * 128] for k in range(8))
        vector_ref[j : j + 1, :] = to_row(jnp.sum(folded, axis=1, keepdims=True))
    for k in range(N_COLGRP):
        out_ref[k] = vector_ref[...]


def grad_kernel(
    other,
    place_ref,
    parts_ref,
    scale_ref,
    weight_ref,
    teacher_exp_ref,
    student_exp_ref,
    token_ref,
    out_ref,
):
    inverse = 1.0 / jnp.sum(parts_ref[...].astype(jnp.float32), axis=0)
    row_inverse, student_inverse = lanes(inverse[0:8, :]), lanes(inverse[8:16, :])
    weight = lanes(weight_ref[...])
    half = 1 - place_ref[0] if other else place_ref[0]
    for k in range(N_X):
        errors = []
        for h in range(2):
            start = k * BLOCK + half * HALF + h * 128
            column = to_column(scale_ref[pl.ds(start // 128, 1), :])
            rows = pl.ds(pl.multiple_of(start, 128), 128)
            targets = (teacher_exp_ref[rows, :] * column * row_inverse).astype(jnp.bfloat16)
            probs = student_exp_ref[rows, :] * student_inverse
            errors.append(
                (PROTOS * (probs - targets.astype(jnp.float32)) * weight).astype(jnp.bfloat16)
            )
        out_ref[k] = jnp.dot(
            jnp.concatenate(errors, axis=0), token_ref[...], preferred_element_type=jnp.float32
        ).astype(out_ref.dtype)


def call(kernel, outs, scratch, *args, flops=0, transcendentals=0):
    vmem = pl.BlockSpec(memory_space=pltpu.VMEM)
    smem = pl.BlockSpec(memory_space=pltpu.SMEM)
    return pl.pallas_call(
        kernel,
        out_shape=outs,
        in_specs=[smem if a.ndim == 1 else vmem for a in args],
        out_specs=[vmem] * len(outs),
        scratch_shapes=scratch,
        compiler_params=pltpu.CompilerParams(vmem_limit_bytes=VMEM_LIMIT),
        cost_estimate=pl.CostEstimate(
            flops=flops, transcendentals=transcendentals, bytes_accessed=COLS * ROWS * 4
        ),
    )(*args)


def shape(dims, dtype=jnp.float32):
    return jax.ShapeDtypeStruct(dims, dtype)


def per_device(features, masters, patch_mask):
    grp = lax.axis_index("grp")
    x = lax.axis_index("img") // N_Z * 2 + lax.axis_index("tp") // N_Y
    z = lax.axis_index("img") % N_Z
    place = jnp.stack([grp, x, z]).astype(jnp.int32)
    work = COLS * ROWS

    own_master = masters[0]
    other_master = lax.ppermute(own_master, "grp", [(0, 1)])
    other_features = swapped(features[0])
    pack, master, unit = unit_call(
        place,
        features[0],
        other_features,
        patch_mask.reshape(4, 128),
        own_master,
        other_master,
    )
    packs = {0: pack, 4: from_z(pack, 4), 1: from_z(pack, 1), 7: from_z(pack, -1)}
    packs[2], packs[5] = from_z(packs[1], 1), from_z(packs[4], 1)
    packs[6], packs[3] = from_z(packs[7], -1), from_z(packs[4], -1)
    own_units = [unit] + [from_x(unit, k) for k in range(1, N_X)]
    other_units = [swapped(block) for block in own_units]

    teacher_exp, student_exp, col_parts, student_part, student_tokens, weights = call(
        exp_kernel,
        [
            shape((COLS, ROWS)),
            shape((COLS, ROWS)),
            shape((N_COLGRP, 16, 128)),
            shape((8, 128)),
            shape((ROWS, 256), jnp.bfloat16),
            shape((8, 128)),
        ],
        [pltpu.VMEM((ROWS, 256), jnp.bfloat16), pltpu.VMEM((16, 128), jnp.float32)],
        place,
        *(packs[k] for k in range(N_Z)),
        *own_units,
        *other_units,
        flops=4 * work * 256,
        transcendentals=2 * work,
    )

    for sweep in range(3):
        last = sweep == 2
        col_parts = exchange(col_parts, COL_GROUPS)
        row_parts, col_scale = call(
            functools.partial(row_kernel, last),
            [shape((N_ROWGRP, 16 if last else 8, 128), jnp.bfloat16), shape((16, 128))],
            [],
            col_parts,
            teacher_exp,
            *((student_part,) if last else ()),
            flops=2 * work,
        )
        row_parts = exchange(row_parts, ROW_GROUPS)
        if not last:
            (col_parts,) = call(
                col_kernel,
                [shape((N_COLGRP, 16, 128))],
                [pltpu.VMEM((16, 128), jnp.float32)],
                row_parts,
                teacher_exp,
                flops=2 * work,
            )

    def partial_gradient(other, dtype):
        (out,) = call(
            functools.partial(grad_kernel, other),
            [shape((N_X, HALF, 256), dtype)],
            [],
            place,
            row_parts,
            col_scale,
            weights,
            teacher_exp,
            student_exp,
            student_tokens,
            flops=work * 256,
        )
        return out

    received = swapped(partial_gradient(True, jnp.bfloat16))
    chip = partial_gradient(False, jnp.float32) + received.astype(jnp.float32)
    pieces = exchange(chip.astype(jnp.bfloat16), X_GROUPS)
    half = jnp.sum(pieces.astype(jnp.float32), axis=0)
    second = lax.ppermute(half, "grp", [(1, 0)])
    return jnp.where(grp == 1, master, jnp.concatenate([half, second]))[None]


def solution(mesh):
    in_specs = (P("grp", "img", None), P("grp", ("img", "tp"), None), P("img"))
    out_specs = P("grp", ("img", "tp"), None)
    return jax.shard_map(
        per_device, mesh=mesh, in_specs=in_specs, out_specs=out_specs, check_vma=False
    )
```

time: 156 us -> 145 us (0.929); the launches traced: 155 us -> 142 us
  waiting for transfers between devices: 31.8 us -> 16 us
  blocking collectives: 72.7 us -> 84.4 us
  local copies, waits for them, and re-layouts: 4.11 us -> 0.68 us
  starting transfers between devices: 29.2 us -> 26 us
  Pallas kernels: 15.8 us -> 13.8 us
    all_to_all x6 -> x7, blocking collectives: 72.7 us -> 84.4 us  [exchange(): lax.all_to_all(blocks, AXES, 0, 0, axis_index_groups=groups, tiled=True)]
    all_to_all x1 -> x0, starting transfers between devices: 10.1 us -> none  [per_device(): packs = lax.all_to_all(pack, 'img', 0, 0, tiled=True)]
    all_to_all x1 -> x0, waiting for transfers between devices: 8.21 us -> none  [per_device(): packs = lax.all_to_all(pack, 'img', 0, 0, tiled=True)]
    ppermute x7 -> x11, starting transfers between devices: 16.7 us -> 23.4 us  [the longest x7 17.4 us: from_z(): return lax.ppermute(block, AXES, route)]
    ppermute x7 -> x11, waiting for transfers between devices: 19.6 us -> 14.1 us  [the longest x7 12 us: from_z(): return lax.ppermute(block, AXES, route)]
    pallas_call x10 -> x8, Pallas kernels: 15.8 us -> 10.8 us  [call(): pl.pallas_call(kernel, out_shape=outs, in_specs=[smem if a.ndim == 1 else...]
    pallas_call x0 -> x1, Pallas kernels: none -> 2.98 us  [unit_call(): pl.pallas_call(unit_kernel, out_shape=[shape((PACK, 256), jnp.bfloat16),...]
    unnamed x10 -> x2, local copies, waits for them, and re-layouts: 3.29 us -> 0.68 us
  transfers between devices with their start and end apart: 14 -> 18, of which waited for: 10 -> 6; matrix products, arithmetic and copies ran while one was open for 0% -> 0% of each run, Pallas kernels for 0% -> 1%
where the time goes in v3:
time: 145 us; the launch traced here: 142 us
  blocking collectives  84.4 us (58%)
  starting transfers between devices  26 us (18%)
  waiting for transfers between devices  16 us (11%)
  Pallas kernels  13.8 us (10%)
    all_to_all x7, blocking collectives, exchange(): lax.all_to_all(blocks, AXES, 0, 0, axis_index_groups=groups, tiled=True)  84.4 us
    ppermute x7, starting transfers between devices, from_z(): return lax.ppermute(block, AXES, route)  17.4 us
    ppermute x7, waiting for transfers between devices, from_z(): return lax.ppermute(block, AXES, route)  12 us
    pallas_call x8, Pallas kernels, call(): pl.pallas_call(kernel, out_shape=outs, in_specs=[smem if a.ndim == 1 else...  10.8 us
    ppermute x3, starting transfers between devices, from_x(): return lax.ppermute(block, AXES, route)  4.76 us
    pallas_call x1, Pallas kernels, unit_call(): pl.pallas_call(unit_kernel, out_shape=[shape((PACK, 256), jnp.bfloat16),...  2.98 us
  transfers between devices with their start and end apart: 18, of which 6 were waited for; matrix products, arithmetic and copies ran while one was open for 0% of the time, Pallas kernels for 1%

profile of v3, /device:TPU:2, one launch (start us, length us, event | category | flops | bytes accessed | tf_op | source)
XLA Modules:
  0.0 142.1 jit_solution(17406371707530823177)
XLA Ops:
  0.0 1.8 %collective-permute-start.1 = (f32[512,256]{1,0:T(8,128)}, f32[512,256]{1,0:T(8,128)S(1)}, u32[]{:S(2)}, u32[]{:S(2)}) collective-permute-start(f32[512,256]{1,0:T(8,128)} %bitcast.9), channel_id=1, source_target_pairs={{0,128},{1,129},{2,130},{3,131},{4,132},{5,133},{6,134},{7,135},{8... | collective-permute-start | bytes 1572872 | tf_op jit(solution)/shard_map/ppermute | solution.py:312
  1.8 0.1 collective-permute-start
  1.9 0.1 pad_add_fusion.place_ref.refs_0_
  2.0 1.9 %collective-permute-done.other_features_ref = bf16[512,256]{1,0:T(8,128)(2,1)S(1)} collective-permute-done((bf16[512,256]{1,0:T(8,128)(2,1)}, bf16[512,256]{1,0:T(8,128)(2,1)S(1)}, u32[]{:S(2)}, u32[]{:S(2)}) %collective-permute-start) | collective-permute-done | bytes 262176 | tf_op jit(solution)/shard_map/ppermute | solution.py:61
  3.8 0.0 collective-permute-done.1.other_ref
  3.8 0.7 copy-done
  4.5 3.0 %shard_map.37 = (bf16[272,256]{1,0:T(8,128)(2,1)S(1)}, f32[512,256]{1,0:T(8,128)S(1)}, bf16[512,256]{1,0:T(8,128)(2,1)S(1)}) custom-call(s32[3]{0:T(128)S(1)} %pad_add_fusion.place_ref.refs_0_, bf16[512,256]{1,0:T(8,128)(2,1)} %bitcast.12, bf16[512,256]{1,0:T(8,128)(2,1)S(1)} %collective-permute-done.other_features_ref, s32[4,128]{1,0:T(4,128)S(1)} %bitcast.8, ...), custom_call_target="tpu_custom_call" | custom-call | tf_op jit(solution)/shard_map/pallas_call | solution.py:152
  7.5 2.0 %collective-permute-start.7 = (bf16[272,256]{1,0:T(8,128)(2,1)S(1)}, bf16[272,256]{1,0:T(8,128)(2,1)S(1)}, u32[]{:S(2)}, u32[]{:S(2)}) collective-permute-start(bf16[272,256]{1,0:T(8,128)(2,1)S(1)} %get-tuple-element.19.refs_1_), channel_id=1, source_target_pairs={{56,0},{57,1},{58,2},{59,3},{60,4},{61,5},{62,6},{63,7},{0,8},{1,9... | collective-permute-start | bytes 417800 | tf_op jit(solution)/shard_map/ppermute | solution.py:77
  9.5 6.3 %collective-permute-start.4 = (bf16[272,256]{1,0:T(8,128)(2,1)S(1)}, bf16[272,256]{1,0:T(8,128)(2,1)S(1)}, u32[]{:S(2)}, u32[]{:S(2)}) collective-permute-start(bf16[272,256]{1,0:T(8,128)(2,1)S(1)} %get-tuple-element.19.refs_1_), channel_id=1, source_target_pairs={{32,0},{33,1},{34,2},{35,3},{36,4},{37,5},{38,6},{39,7},{40,8},{41... | collective-permute-start | bytes 417800 | tf_op jit(solution)/shard_map/ppermute | solution.py:77
  15.8 1.5 %collective-permute-start.11 = (bf16[512,256]{1,0:T(8,128)(2,1)S(1)}, bf16[512,256]{1,0:T(8,128)(2,1)S(1)}, u32[]{:S(2)}, u32[]{:S(2)}) collective-permute-start(bf16[512,256]{1,0:T(8,128)(2,1)S(1)} %get-tuple-element.20.refs_9_), channel_id=1, source_target_pairs={{68,0},{69,1},{70,2},{71,3},{0,4},{1,5},{2,6},{3,7},{76,8},{77,9},... | collective-permute-start | bytes 786440 | tf_op jit(solution)/shard_map/ppermute | solution.py:69
  17.3 1.1 collective-permute-start.10
  18.4 2.2 %collective-permute-start.9 = (bf16[512,256]{1,0:T(8,128)(2,1)S(1)}, bf16[512,256]{1,0:T(8,128)(2,1)S(1)}, u32[]{:S(2)}, u32[]{:S(2)}) collective-permute-start(bf16[512,256]{1,0:T(8,128)(2,1)S(1)} %get-tuple-element.20.refs_9_), channel_id=1, source_target_pairs={{4,0},{5,1},{6,2},{7,3},{64,4},{65,5},{66,6},{67,7},{12,8},{13,9},... | collective-permute-start | bytes 786440 | tf_op jit(solution)/shard_map/ppermute | solution.py:69
  20.6 3.4 %collective-permute-done.4.refs_5_ = bf16[272,256]{1,0:T(8,128)(2,1)S(1)} collective-permute-done((bf16[272,256]{1,0:T(8,128)(2,1)S(1)}, bf16[272,256]{1,0:T(8,128)(2,1)S(1)}, u32[]{:S(2)}, u32[]{:S(2)}) %collective-permute-start.4) | collective-permute-done | bytes 139296 | tf_op jit(solution)/shard_map/ppermute | solution.py:77
  24.0 2.1 %collective-permute-start.2 = (bf16[272,256]{1,0:T(8,128)(2,1)S(1)}, bf16[272,256]{1,0:T(8,128)(2,1)S(1)}, u32[]{:S(2)}, u32[]{:S(2)}) collective-permute-start(bf16[272,256]{1,0:T(8,128)(2,1)S(1)} %get-tuple-element.19.refs_1_), channel_id=1, source_target_pairs={{8,0},{9,1},{10,2},{11,3},{12,4},{13,5},{14,6},{15,7},{16,8},{17,9... | collective-permute-start | bytes 417800 | tf_op jit(solution)/shard_map/ppermute | solution.py:77
  26.1 3.1 %collective-permute-done.2.refs_2_ = bf16[272,256]{1,0:T(8,128)(2,1)S(1)} collective-permute-done((bf16[272,256]{1,0:T(8,128)(2,1)S(1)}, bf16[272,256]{1,0:T(8,128)(2,1)S(1)}, u32[]{:S(2)}, u32[]{:S(2)}) %collective-permute-start.2) | collective-permute-done | bytes 139296 | tf_op jit(solution)/shard_map/ppermute | solution.py:77
  29.3 1.9 %collective-permute-start.8 = (bf16[272,256]{1,0:T(8,128)(2,1)S(1)}, bf16[272,256]{1,0:T(8,128)(2,1)S(1)}, u32[]{:S(2)}, u32[]{:S(2)}) collective-permute-start(bf16[272,256]{1,0:T(8,128)(2,1)S(1)} %collective-permute-done.7.refs_8_), channel_id=1, source_target_pairs={{56,0},{57,1},{58,2},{59,3},{60,4},{61,5},{62,6},{63,7},{0,8},{1,9... | collective-permute-start | bytes 417800 | tf_op jit(solution)/shard_map/ppermute | solution.py:77
  31.1 0.0 collective-permute-done.12.refs_13_
  31.1 1.8 %collective-permute-start.6 = (bf16[272,256]{1,0:T(8,128)(2,1)S(1)}, bf16[272,256]{1,0:T(8,128)(2,1)S(1)}, u32[]{:S(2)}, u32[]{:S(2)}) collective-permute-start(bf16[272,256]{1,0:T(8,128)(2,1)S(1)} %collective-permute-done.4.refs_5_), channel_id=1, source_target_pairs={{8,0},{9,1},{10,2},{11,3},{12,4},{13,5},{14,6},{15,7},{16,8},{17,9... | collective-permute-start | bytes 417800 | tf_op jit(solution)/shard_map/ppermute | solution.py:77
  33.0 0.0 collective-permute-done.11.refs_12_
  33.0 0.0 collective-permute-start.15
  33.0 0.5 collective-permute-start.14
  33.5 0.1 collective-permute-start.13
  33.6 2.4 %collective-permute-done.8.refs_7_ = bf16[272,256]{1,0:T(8,128)(2,1)S(1)} collective-permute-done((bf16[272,256]{1,0:T(8,128)(2,1)S(1)}, bf16[272,256]{1,0:T(8,128)(2,1)S(1)}, u32[]{:S(2)}, u32[]{:S(2)}) %collective-permute-start.8) | collective-permute-done | bytes 139296 | tf_op jit(solution)/shard_map/ppermute | solution.py:77
  36.0 0.2 collective-permute-start.5
  36.2 0.0 collective-permute-done.6.refs_6_
  36.2 3.0 %collective-permute-start.3 = (bf16[272,256]{1,0:T(8,128)(2,1)S(1)}, bf16[272,256]{1,0:T(8,128)(2,1)S(1)}, u32[]{:S(2)}, u32[]{:S(2)}) collective-permute-start(bf16[272,256]{1,0:T(8,128)(2,1)S(1)} %collective-permute-done.2.refs_2_), channel_id=1, source_target_pairs={{8,0},{9,1},{10,2},{11,3},{12,4},{13,5},{14,6},{15,7},{16,8},{17,9... | collective-permute-start | bytes 417800 | tf_op jit(solution)/shard_map/ppermute | solution.py:77
  39.2 3.0 %collective-permute-done.5.refs_4_ = bf16[272,256]{1,0:T(8,128)(2,1)S(1)} collective-permute-done((bf16[272,256]{1,0:T(8,128)(2,1)S(1)}, bf16[272,256]{1,0:T(8,128)(2,1)S(1)}, u32[]{:S(2)}, u32[]{:S(2)}) %collective-permute-start.5) | collective-permute-done | bytes 139296 | tf_op jit(solution)/shard_map/ppermute | solution.py:77
  42.3 3.2 %shard_map.38 = (f32[2048,1024]{1,0:T(8,128)S(1)}, f32[2048,1024]{1,0:T(8,128)S(1)}, f32[8,16,128]{2,1,0:T(8,128)S(1)}, f32[8,128]{1,0:T(8,128)S(1)}, bf16[1024,...) custom-call(s32[3]{0:T(128)S(1)} %pad_add_fusion.place_ref.refs_0_, bf16[272,256]{1,0:T(8,128)(2,1)S(1)} %get-tuple-element.19.refs_1_, ...), custom_call_target="tpu_custom_call" | custom-call | flops 2147483648 | bytes 8388608 | tf_op jit(solution)/shard_map/pallas_call | solution.py:287
  45.4 8.7 %all_to_all.35.refs_0_ = f32[8,16,128]{2,1,0:T(8,128)S(1)} all-to-all(f32[8,16,128]{2,1,0:T(8,128)S(1)} %get-tuple-element.21), channel_id=1, replica_groups={{0,4,64,68,128,132,192,196},{1,5,65,69,129,133,193,197},{2,6,66,70,130,..., dimensions={0} | all-to-all | bytes 131072 | tf_op jit(solution)/shard_map/all_to_all | solution.py:57
  54.1 0.8 shard_map.39
  55.0 20.2 %all_to_all.36.parts_ref = bf16[32,8,128]{2,1,0:T(8,128)(2,1)S(1)} all-to-all(bf16[32,8,128]{2,1,0:T(8,128)(2,1)S(1)} %get-tuple-element.23), channel_id=1, replica_groups={{0,1,2,3,8,9,10,11,16,17,18,19,24,25,26,27,32,33,34,35,40,41,42,43,48,4..., dimensions={0} | all-to-all | bytes 131072 | tf_op jit(solution)/shard_map/all_to_all | solution.py:57
  75.2 0.7 shard_map.40
  75.9 7.9 %all_to_all.37.refs_0_ = f32[8,16,128]{2,1,0:T(8,128)S(1)} all-to-all(f32[8,16,128]{2,1,0:T(8,128)S(1)} %shard_map.40), channel_id=1, replica_groups={{0,4,64,68,128,132,192,196},{1,5,65,69,129,133,193,197},{2,6,66,70,130,..., dimensions={0} | all-to-all | bytes 131072 | tf_op jit(solution)/shard_map/all_to_all | solution.py:57
  83.7 0.8 shard_map.41
  84.5 13.1 %all_to_all.38.parts_ref = bf16[32,8,128]{2,1,0:T(8,128)(2,1)S(1)} all-to-all(bf16[32,8,128]{2,1,0:T(8,128)(2,1)S(1)} %get-tuple-element.24), channel_id=1, replica_groups={{0,1,2,3,8,9,10,11,16,17,18,19,24,25,26,27,32,33,34,35,40,41,42,43,48,4..., dimensions={0} | all-to-all | bytes 131072 | tf_op jit(solution)/shard_map/all_to_all | solution.py:57
  97.6 0.7 shard_map.42
  98.3 7.9 %all_to_all.39.refs_0_ = f32[8,16,128]{2,1,0:T(8,128)S(1)} all-to-all(f32[8,16,128]{2,1,0:T(8,128)S(1)} %shard_map.42), channel_id=1, replica_groups={{0,4,64,68,128,132,192,196},{1,5,65,69,129,133,193,197},{2,6,66,70,130,..., dimensions={0} | all-to-all | bytes 131072 | tf_op jit(solution)/shard_map/all_to_all | solution.py:57
  106.2 0.7 shard_map.43
  106.9 14.1 %all_to_all.40.parts_ref = bf16[32,16,128]{2,1,0:T(8,128)(2,1)S(1)} all-to-all(bf16[32,16,128]{2,1,0:T(8,128)(2,1)S(1)} %get-tuple-element.26), channel_id=1, replica_groups={{0,1,2,3,8,9,10,11,16,17,18,19,24,25,26,27,32,33,34,35,40,41,42,43,48,4..., dimensions={0} | all-to-all | bytes 262144 | tf_op jit(solution)/shard_map/all_to_all | solution.py:57
  121.0 1.9 %shard_map.45 = bf16[4,256,256]{2,1,0:T(8,128)(2,1)S(1)} custom-call(s32[3]{0:T(128)S(1)} %pad_add_fusion.place_ref.refs_0_, bf16[32,16,128]{2,1,0:T(8,128)(2,1)S(1)} %all_to_all.40.parts_ref, f32[16,128]{1,0:T(8,128)S(1)} %get-tuple-element.27.scale_ref, f32[8,128]{1,0:T(8,128)S(1)} %get-tuple-element.28.weight_ref, ...), custom_call_target="tpu_custom_call" | custom-call | flops 536870912 | bytes 8388608 | tf_op jit(solution)/shard_map/pallas_call | solution.py:287
  122.9 0.1 collective-permute-start.16
  123.0 1.9 %shard_map.44 = f32[4,256,256]{2,1,0:T(8,128)S(1)} custom-call(s32[3]{0:T(128)S(1)} %pad_add_fusion.place_ref.refs_0_, bf16[32,16,128]{2,1,0:T(8,128)(2,1)S(1)} %all_to_all.40.parts_ref, f32[16,128]{1,0:T(8,128)S(1)} %get-tuple-element.27.scale_ref, f32[8,128]{1,0:T(8,128)S(1)} %get-tuple-element.28.weight_ref, ...), custom_call_target="tpu_custom_call" | custom-call | flops 536870912 | bytes 8388608 | tf_op jit(solution)/shard_map/pallas_call | solution.py:287
  124.9 0.1 add_convert_fusion
  125.1 12.6 %all_to_all.41 = bf16[4,256,256]{2,1,0:T(8,128)(2,1)S(1)} all-to-all(bf16[4,256,256]{2,1,0:T(8,128)(2,1)S(1)} %add_convert_fusion), channel_id=1, replica_groups={{0,4,64,68},{1,5,65,69},{2,6,66,70},{3,7,67,71},{8,12,72,76},{9,13,73,7..., dimensions={0} | all-to-all | bytes 1048576 | tf_op jit(solution)/shard_map/all_to_all | solution.py:57
  137.7 0.1 convert_reduce_fusion
  137.8 1.3 collective-permute-start.17
  139.1 2.1 %collective-permute-done.17 = f32[256,256]{1,0:T(8,128)S(1)} collective-permute-done((f32[256,256]{1,0:T(8,128)S(1)}, f32[256,256]{1,0:T(8,128)S(1)}, u32[]{:S(2)}, u32[]{:S(2)}) %collective-permute-start.17) | collective-permute-done | bytes 262176 | tf_op jit(solution)/shard_map/ppermute | solution.py:390
  141.2 0.9 fusion
  (10 shorter events, 0.0 us)
Async XLA Ops:
  0.0 3.8 %collective-permute-start.1 = (f32[512,256]{1,0:T(8,128)}, f32[512,256]{1,0:T(8,128)S(1)}, u32[]{:S(2)}, u32[]{:S(2)}) collective-permute-start(f32[512,256]{1,0:T(8,128)} %bitcast.9), channel_id=1, source_target_pairs={{0,128},{1,129},{2,130},{3,131},{4,132},{5,133},{6,134},{7,135},{8... | collective-permute-start | bytes 1572872 | tf_op jit(solution)/shard_map/ppermute | solution.py:312
  1.8 2.1 %collective-permute-start = (bf16[512,256]{1,0:T(8,128)(2,1)}, bf16[512,256]{1,0:T(8,128)(2,1)S(1)}, u32[]{:S(2)}, u32[]{:S(2)}) collective-permute-start(bf16[512,256]{1,0:T(8,128)(2,1)} %bitcast.11), channel_id=1, source_target_pairs={{0,128},{128,0},{1,129},{129,1},{2,130},{130,2},{3,131},{131,3},{4... | collective-permute-start | bytes 786440 | tf_op jit(solution)/shard_map/ppermute | solution.py:61
  3.8 0.7 copy-start
  7.5 10.9 %collective-permute-start.7 = (bf16[272,256]{1,0:T(8,128)(2,1)S(1)}, bf16[272,256]{1,0:T(8,128)(2,1)S(1)}, u32[]{:S(2)}, u32[]{:S(2)}) collective-permute-start(bf16[272,256]{1,0:T(8,128)(2,1)S(1)} %get-tuple-element.19.refs_1_), channel_id=1, source_target_pairs={{56,0},{57,1},{58,2},{59,3},{60,4},{61,5},{62,6},{63,7},{0,8},{1,9... | collective-permute-start | bytes 417800 | tf_op jit(solution)/shard_map/ppermute | solution.py:77
  9.5 14.5 %collective-permute-start.4 = (bf16[272,256]{1,0:T(8,128)(2,1)S(1)}, bf16[272,256]{1,0:T(8,128)(2,1)S(1)}, u32[]{:S(2)}, u32[]{:S(2)}) collective-permute-start(bf16[272,256]{1,0:T(8,128)(2,1)S(1)} %get-tuple-element.19.refs_1_), channel_id=1, source_target_pairs={{32,0},{33,1},{34,2},{35,3},{36,4},{37,5},{38,6},{39,7},{40,8},{41... | collective-permute-start | bytes 417800 | tf_op jit(solution)/shard_map/ppermute | solution.py:77
  15.8 15.3 %collective-permute-start.12 = (bf16[512,256]{1,0:T(8,128)(2,1)S(1)}, bf16[512,256]{1,0:T(8,128)(2,1)S(1)}, u32[]{:S(2)}, u32[]{:S(2)}) collective-permute-start(bf16[512,256]{1,0:T(8,128)(2,1)S(1)} %get-tuple-element.20.refs_9_), channel_id=1, source_target_pairs={{0,128},{128,0},{1,129},{129,1},{2,130},{130,2},{3,131},{131,3},{4... | collective-permute-start | bytes 786440 | tf_op jit(solution)/shard_map/ppermute | solution.py:61
  15.8 17.1 %collective-permute-start.11 = (bf16[512,256]{1,0:T(8,128)(2,1)S(1)}, bf16[512,256]{1,0:T(8,128)(2,1)S(1)}, u32[]{:S(2)}, u32[]{:S(2)}) collective-permute-start(bf16[512,256]{1,0:T(8,128)(2,1)S(1)} %get-tuple-element.20.refs_9_), channel_id=1, source_target_pairs={{68,0},{69,1},{70,2},{71,3},{0,4},{1,5},{2,6},{3,7},{76,8},{77,9},... | collective-permute-start | bytes 786440 | tf_op jit(solution)/shard_map/ppermute | solution.py:69
  17.3 15.7 %collective-permute-start.10 = (bf16[512,256]{1,0:T(8,128)(2,1)S(1)}, bf16[512,256]{1,0:T(8,128)(2,1)S(1)}, u32[]{:S(2)}, u32[]{:S(2)}) collective-permute-start(bf16[512,256]{1,0:T(8,128)(2,1)S(1)} %get-tuple-element.20.refs_9_), channel_id=1, source_target_pairs={{64,0},{65,1},{66,2},{67,3},{68,4},{69,5},{70,6},{71,7},{72,8},{73... | collective-permute-start | bytes 786440 | tf_op jit(solution)/shard_map/ppermute | solution.py:69
  18.4 15.0 %collective-permute-start.9 = (bf16[512,256]{1,0:T(8,128)(2,1)S(1)}, bf16[512,256]{1,0:T(8,128)(2,1)S(1)}, u32[]{:S(2)}, u32[]{:S(2)}) collective-permute-start(bf16[512,256]{1,0:T(8,128)(2,1)S(1)} %get-tuple-element.20.refs_9_), channel_id=1, source_target_pairs={{4,0},{5,1},{6,2},{7,3},{64,4},{65,5},{66,6},{67,7},{12,8},{13,9},... | collective-permute-start | bytes 786440 | tf_op jit(solution)/shard_map/ppermute | solution.py:69
  24.0 5.3 %collective-permute-start.2 = (bf16[272,256]{1,0:T(8,128)(2,1)S(1)}, bf16[272,256]{1,0:T(8,128)(2,1)S(1)}, u32[]{:S(2)}, u32[]{:S(2)}) collective-permute-start(bf16[272,256]{1,0:T(8,128)(2,1)S(1)} %get-tuple-element.19.refs_1_), channel_id=1, source_target_pairs={{8,0},{9,1},{10,2},{11,3},{12,4},{13,5},{14,6},{15,7},{16,8},{17,9... | collective-permute-start | bytes 417800 | tf_op jit(solution)/shard_map/ppermute | solution.py:77
  29.3 6.7 %collective-permute-start.8 = (bf16[272,256]{1,0:T(8,128)(2,1)S(1)}, bf16[272,256]{1,0:T(8,128)(2,1)S(1)}, u32[]{:S(2)}, u32[]{:S(2)}) collective-permute-start(bf16[272,256]{1,0:T(8,128)(2,1)S(1)} %collective-permute-done.7.refs_8_), channel_id=1, source_target_pairs={{56,0},{57,1},{58,2},{59,3},{60,4},{61,5},{62,6},{63,7},{0,8},{1,9... | collective-permute-start | bytes 417800 | tf_op jit(solution)/shard_map/ppermute | solution.py:77
  31.1 5.1 %collective-permute-start.6 = (bf16[272,256]{1,0:T(8,128)(2,1)S(1)}, bf16[272,256]{1,0:T(8,128)(2,1)S(1)}, u32[]{:S(2)}, u32[]{:S(2)}) collective-permute-start(bf16[272,256]{1,0:T(8,128)(2,1)S(1)} %collective-permute-done.4.refs_5_), channel_id=1, source_target_pairs={{8,0},{9,1},{10,2},{11,3},{12,4},{13,5},{14,6},{15,7},{16,8},{17,9... | collective-permute-start | bytes 417800 | tf_op jit(solution)/shard_map/ppermute | solution.py:77
  33.0 9.3 %collective-permute-start.15 = (bf16[512,256]{1,0:T(8,128)(2,1)S(1)}, bf16[512,256]{1,0:T(8,128)(2,1)S(1)}, u32[]{:S(2)}, u32[]{:S(2)}) collective-permute-start(bf16[512,256]{1,0:T(8,128)(2,1)S(1)} %collective-permute-done.11.refs_12_), channel_id=1, source_target_pairs={{0,128},{128,0},{1,129},{129,1},{2,130},{130,2},{3,131},{131,3},{4... | collective-permute-start | bytes 786440 | tf_op jit(solution)/shard_map/ppermute | solution.py:61
  33.0 9.3 %collective-permute-start.14 = (bf16[512,256]{1,0:T(8,128)(2,1)S(1)}, bf16[512,256]{1,0:T(8,128)(2,1)S(1)}, u32[]{:S(2)}, u32[]{:S(2)}) collective-permute-start(bf16[512,256]{1,0:T(8,128)(2,1)S(1)} %collective-permute-done.10.refs_11_), channel_id=1, source_target_pairs={{0,128},{128,0},{1,129},{129,1},{2,130},{130,2},{3,131},{131,3},{4... | collective-permute-start | bytes 786440 | tf_op jit(solution)/shard_map/ppermute | solution.py:61
  33.5 8.8 %collective-permute-start.13 = (bf16[512,256]{1,0:T(8,128)(2,1)S(1)}, bf16[512,256]{1,0:T(8,128)(2,1)S(1)}, u32[]{:S(2)}, u32[]{:S(2)}) collective-permute-start(bf16[512,256]{1,0:T(8,128)(2,1)S(1)} %collective-permute-done.9.refs_10_), channel_id=1, source_target_pairs={{0,128},{128,0},{1,129},{129,1},{2,130},{130,2},{3,131},{131,3},{4... | collective-permute-start | bytes 786440 | tf_op jit(solution)/shard_map/ppermute | solution.py:61
  36.0 6.3 %collective-permute-start.5 = (bf16[272,256]{1,0:T(8,128)(2,1)S(1)}, bf16[272,256]{1,0:T(8,128)(2,1)S(1)}, u32[]{:S(2)}, u32[]{:S(2)}) collective-permute-start(bf16[272,256]{1,0:T(8,128)(2,1)S(1)} %collective-permute-done.4.refs_5_), channel_id=1, source_target_pairs={{56,0},{57,1},{58,2},{59,3},{60,4},{61,5},{62,6},{63,7},{0,8},{1,9... | collective-permute-start | bytes 417800 | tf_op jit(solution)/shard_map/ppermute | solution.py:77
  36.2 6.1 %collective-permute-start.3 = (bf16[272,256]{1,0:T(8,128)(2,1)S(1)}, bf16[272,256]{1,0:T(8,128)(2,1)S(1)}, u32[]{:S(2)}, u32[]{:S(2)}) collective-permute-start(bf16[272,256]{1,0:T(8,128)(2,1)S(1)} %collective-permute-done.2.refs_2_), channel_id=1, source_target_pairs={{8,0},{9,1},{10,2},{11,3},{12,4},{13,5},{14,6},{15,7},{16,8},{17,9... | collective-permute-start | bytes 417800 | tf_op jit(solution)/shard_map/ppermute | solution.py:77
  122.9 2.0 %collective-permute-start.16 = (bf16[4,256,256]{2,1,0:T(8,128)(2,1)S(1)}, bf16[4,256,256]{2,1,0:T(8,128)(2,1)S(1)}, u32[]{:S(2)}, u32[]{:S(2)}) collective-permute-start(bf16[4,256,256]{2,1,0:T(8,128)(2,1)S(1)} %shard_map.45), channel_id=1, source_target_pairs={{0,128},{128,0},{1,129},{129,1},{2,130},{130,2},{3,131},{131,3},{4... | collective-permute-start | bytes 1572872 | tf_op jit(solution)/shard_map/ppermute | solution.py:61
  137.8 3.4 %collective-permute-start.17 = (f32[256,256]{1,0:T(8,128)S(1)}, f32[256,256]{1,0:T(8,128)S(1)}, u32[]{:S(2)}, u32[]{:S(2)}) collective-permute-start(f32[256,256]{1,0:T(8,128)S(1)} %convert_reduce_fusion), channel_id=1, source_target_pairs={{128,0},{129,1},{130,2},{131,3},{132,4},{133,5},{134,6},{135,7},{1... | collective-permute-start | bytes 786440 | tf_op jit(solution)/shard_map/ppermute | solution.py:390

commit v4 on v3

--- a/solution.py
+++ b/solution.py
@@ -21,7 +21,7 @@
 BLOCK = 512
 HALF = 256
 OWN_ROWS = 128
-PACK = 2 * OWN_ROWS + 16
+PACK = 2 * OWN_ROWS
 ROWS = N_Z * OWN_ROWS
 COLS = N_X * BLOCK
 N_ROWGRP = N_Y * N_Z
@@ -48,7 +48,6 @@
     return list(found.values())
 
 
-X_GROUPS = groups_of(lambda grp, x, y, z: (grp, y, z))
 COL_GROUPS = groups_of(lambda grp, x, y, z: (y, z))
 ROW_GROUPS = groups_of(lambda grp, x, y, z: (grp, x))
 
@@ -61,20 +60,21 @@
     return lax.ppermute(block, "grp", [(0, 1), (1, 0)])
 
 
-def from_x(block, distance):
+def permuted(block, target_of):
     route = []
     for device in range(N_GRP * N_IMG * N_TP):
-        grp, x, y, z = coordinates(device)
-        route.append((device_at(grp, (x + distance) % N_X, y, z), device))
+        target = target_of(*coordinates(device))
+        if target is not None:
+            route.append((device, device_at(*target)))
     return lax.ppermute(block, AXES, route)
 
 
+def from_x(block, distance):
+    return permuted(block, lambda grp, x, y, z: (grp, (x - distance) % N_X, y, z))
+
+
 def from_z(block, distance):
-    route = []
-    for device in range(N_GRP * N_IMG * N_TP):
-        grp, x, y, z = coordinates(device)
-        route.append((device_at(grp, x, y, (z + distance) % N_Z), device))
-    return lax.ppermute(block, AXES, route)
+    return permuted(block, lambda grp, x, y, z: (grp, x, y, (z - distance) % N_Z))
 
 
 def unit_rows(values):
@@ -113,7 +113,7 @@
     own_ref,
     other_ref,
     pack_ref,
-    master_ref,
+    weight_ref,
     unit_ref,
 ):
     grp, x = place_ref[0], place_ref[1]
@@ -128,16 +128,13 @@
         count = jnp.maximum(jnp.sum(crop), 1.0)
         weight = mask_ref[pl.ds(x % 2 * 2 + grp, 1), :].astype(jnp.float32)
         weight = weight / (STUDENT_TEMP * count)
-        weight = jnp.broadcast_to(jnp.concatenate([weight, weight], axis=1), (16, 256))
-        weight = weight.astype(jnp.bfloat16)
+        weight_ref[...] = jnp.broadcast_to(weight, (8, 128)).astype(jnp.bfloat16)
         pack_ref[0:OWN_ROWS, :] = teacher
-        pack_ref[OWN_ROWS : 2 * OWN_ROWS, :] = student
-        pack_ref[2 * OWN_ROWS : PACK, :] = weight
+        pack_ref[OWN_ROWS:PACK, :] = student
 
     own_master = own_ref[...]
     blended = MOMENTUM * own_master + (1.0 - MOMENTUM) * other_ref[...]
     master = jnp.where(grp == 1, blended, own_master)
-    master_ref[...] = master
     unit_ref[...] = unit_rows(master)
 
 
@@ -146,19 +143,19 @@
 
 
 def unit_call(place, features, other_features, mask, own_master, other_master):
-    rows = BLOCK // 4
+    rows = BLOCK // 2
     picked = pl.BlockSpec((OWN_ROWS, 256), lambda i, place: (place[1] % 2 * 2 + place[0], 0))
     part = pl.BlockSpec((rows, 256), lambda i, place: (i, 0))
     return pl.pallas_call(
         unit_kernel,
         out_shape=[
             shape((PACK, 256), jnp.bfloat16),
-            shape((BLOCK, 256)),
+            shape((8, 128), jnp.bfloat16),
             shape((BLOCK, 256), jnp.bfloat16),
         ],
         grid_spec=pltpu.PrefetchScalarGridSpec(
             num_scalar_prefetch=1,
-            grid=(4,),
+            grid=(2,),
             in_specs=[
                 picked,
                 picked,
@@ -168,12 +165,12 @@
             ],
             out_specs=[
                 pl.BlockSpec((PACK, 256), lambda i, place: (0, 0)),
-                part,
+                pl.BlockSpec((8, 128), lambda i, place: (0, 0)),
                 part,
             ],
         ),
         compiler_params=pltpu.CompilerParams(vmem_limit_bytes=VMEM_LIMIT),
-    )(place, in_hbm(features), other_features, mask, in_hbm(own_master), other_master)
+    )(place, in_hbm(features), other_features, in_hbm(mask), in_hbm(own_master), other_master)
 
 
 def exp_of(protos, tokens, temperature):
@@ -186,16 +183,13 @@
 def exp_kernel(*refs):
     place_ref, pack_refs = refs[0], refs[1:9]
     own_refs, other_refs = refs[9:13], refs[13:17]
-    teacher_ref, student_ref, parts_ref, total_ref, token_ref, weight_ref = refs[17:23]
-    scratch_ref, vector_ref = refs[23:]
+    teacher_ref, student_ref, parts_ref, total_ref, token_ref = refs[17:22]
+    scratch_ref, vector_ref = refs[22:]
     grp, x, z = place_ref[0], place_ref[1], place_ref[2]
     for k in range(N_Z):
-        place = (z + k) % N_Z
-        rows = pl.ds(pl.multiple_of(place * OWN_ROWS, OWN_ROWS), OWN_ROWS)
+        rows = pl.ds(pl.multiple_of((z + k) % N_Z * OWN_ROWS, OWN_ROWS), OWN_ROWS)
         scratch_ref[rows, :] = pack_refs[k][0:OWN_ROWS, :]
-        token_ref[rows, :] = pack_refs[k][OWN_ROWS : 2 * OWN_ROWS, :]
-        weight = pack_refs[k][2 * OWN_ROWS : PACK, 0:128].astype(jnp.float32)
-        weight_ref[pl.ds(place, 1), :] = weight[0:1, :]
+        token_ref[rows, :] = pack_refs[k][OWN_ROWS:PACK, :]
     teacher_tokens = scratch_ref[...]
     student_tokens = token_ref[...]
     total = jnp.zeros((8, ROWS), jnp.float32)
@@ -221,9 +215,9 @@
         parts_ref[k] = vector_ref[...]
 
 
-def row_kernel(with_student, *refs):
-    if with_student:
-        parts_ref, exp_ref, student_ref, out_ref, scale_ref = refs
+def row_kernel(with_extra, *refs):
+    if with_extra:
+        parts_ref, exp_ref, extra_ref, out_ref, scale_ref = refs
     else:
         parts_ref, exp_ref, out_ref, scale_ref = refs
     scale = 1.0 / jnp.sum(parts_ref[...], axis=0)
@@ -233,15 +227,22 @@
         weighted = exp_ref[j * 128 : (j + 1) * 128, :] * to_column(scale[j : j + 1, :])
         total += jnp.sum(weighted.reshape(16, 8, ROWS), axis=0)
     mine = pieces_of(jnp.sum(total, axis=0, keepdims=True))
-    if with_student:
-        mine = jnp.concatenate([mine, student_ref[...]], axis=0)
+    if with_extra:
+        mine = jnp.concatenate([mine, extra_ref[...].astype(jnp.float32)], axis=0)
     mine = mine.astype(jnp.bfloat16)
     for k in range(N_ROWGRP):
         out_ref[k] = mine
 
 
-def col_kernel(parts_ref, exp_ref, out_ref, vector_ref):
-    row = lanes(1.0 / jnp.sum(parts_ref[...].astype(jnp.float32), axis=0))
+def col_kernel(with_weight, *refs):
+    if with_weight:
+        parts_ref, exp_ref, out_ref, weight_ref, vector_ref = refs
+        for z in range(N_Z):
+            extra = parts_ref[z * N_Y, 8:16, :].astype(jnp.float32)
+            weight_ref[z : z + 1, :] = extra[0:1, :]
+    else:
+        parts_ref, exp_ref, out_ref, vector_ref = refs
+    row = lanes(1.0 / jnp.sum(parts_ref[:, 0:8, :].astype(jnp.float32), axis=0))
     for j in range(COLS // 128):
         weighted = exp_ref[j * 128 : (j + 1) * 128, :] * row
         folded = sum(weighted[:, k * 128 : (k + 1) * 128] for k in range(8))
@@ -264,21 +265,25 @@
     inverse = 1.0 / jnp.sum(parts_ref[...].astype(jnp.float32), axis=0)
     row_inverse, student_inverse = lanes(inverse[0:8, :]), lanes(inverse[8:16, :])
     weight = lanes(weight_ref[...])
-    half = 1 - place_ref[0] if other else place_ref[0]
-    for k in range(N_X):
-        errors = []
-        for h in range(2):
-            start = k * BLOCK + half * HALF + h * 128
-            column = to_column(scale_ref[pl.ds(start // 128, 1), :])
-            rows = pl.ds(pl.multiple_of(start, 128), 128)
-            targets = (teacher_exp_ref[rows, :] * column * row_inverse).astype(jnp.bfloat16)
-            probs = student_exp_ref[rows, :] * student_inverse
-            errors.append(
-                (PROTOS * (probs - targets.astype(jnp.float32)) * weight).astype(jnp.bfloat16)
-            )
-        out_ref[k] = jnp.dot(
-            jnp.concatenate(errors, axis=0), token_ref[...], preferred_element_type=jnp.float32
-        ).astype(out_ref.dtype)
+    first = 1 - place_ref[0] if other else place_ref[0]
+    for k in range(2):
+        base = (place_ref[1] + 2 * k + first) % N_X * BLOCK
+        for i in range(BLOCK // 256):
+            errors = []
+            for h in range(2):
+                start = base + i * 256 + h * 128
+                column = to_column(scale_ref[pl.ds(start // 128, 1), :])
+                rows = pl.ds(pl.multiple_of(start, 128), 128)
+                targets = (teacher_exp_ref[rows, :] * column * row_inverse).astype(jnp.bfloat16)
+                probs = student_exp_ref[rows, :] * student_inverse
+                errors.append(
+                    (PROTOS * (probs - targets.astype(jnp.float32)) * weight).astype(jnp.bfloat16)
+                )
+            out_ref[k, i * 256 : (i + 1) * 256, :] = jnp.dot(
+                jnp.concatenate(errors, axis=0),
+                token_ref[...],
+                preferred_element_type=jnp.float32,
+            ).astype(out_ref.dtype)
 
 
 def call(kernel, outs, scratch, *args, flops=0, transcendentals=0):
@@ -311,7 +316,7 @@
     own_master = masters[0]
     other_master = lax.ppermute(own_master, "grp", [(0, 1)])
     other_features = swapped(features[0])
-    pack, master, unit = unit_call(
+    pack, weight, unit = unit_call(
         place,
         features[0],
         other_features,
@@ -323,9 +328,10 @@
     packs[2], packs[5] = from_z(packs[1], 1), from_z(packs[4], 1)
     packs[6], packs[3] = from_z(packs[7], -1), from_z(packs[4], -1)
     own_units = [unit] + [from_x(unit, k) for k in range(1, N_X)]
-    other_units = [swapped(block) for block in own_units]
-
-    teacher_exp, student_exp, col_parts, student_part, student_tokens, weights = call(
+    held, packs = lax.optimization_barrier((tuple(own_units), packs))
+    other_units = [swapped(block) for block in held]
+
+    teacher_exp, student_exp, col_parts, student_part, student_tokens = call(
         exp_kernel,
         [
             shape((COLS, ROWS)),
@@ -333,7 +339,6 @@
             shape((N_COLGRP, 16, 128)),
             shape((8, 128)),
             shape((ROWS, 256), jnp.bfloat16),
-            shape((8, 128)),
         ],
         [pltpu.VMEM((ROWS, 256), jnp.bfloat16), pltpu.VMEM((16, 128), jnp.float32)],
         place,
@@ -345,32 +350,35 @@
     )
 
     for sweep in range(3):
-        last = sweep == 2
+        first, last = sweep == 0, sweep == 2
+        extra = (weight,) if first else (student_part,) if last else ()
         col_parts = exchange(col_parts, COL_GROUPS)
         row_parts, col_scale = call(
-            functools.partial(row_kernel, last),
-            [shape((N_ROWGRP, 16 if last else 8, 128), jnp.bfloat16), shape((16, 128))],
+            functools.partial(row_kernel, first or last),
+            [shape((N_ROWGRP, 16 if extra else 8, 128), jnp.bfloat16), shape((16, 128))],
             [],
             col_parts,
             teacher_exp,
-            *((student_part,) if last else ()),
+            *extra,
             flops=2 * work,
         )
         row_parts = exchange(row_parts, ROW_GROUPS)
         if not last:
-            (col_parts,) = call(
-                col_kernel,
-                [shape((N_COLGRP, 16, 128))],
+            col_parts, *rest = call(
+                functools.partial(col_kernel, first),
+                [shape((N_COLGRP, 16, 128))] + [shape((8, 128))] * first,
                 [pltpu.VMEM((16, 128), jnp.float32)],
                 row_parts,
                 teacher_exp,
                 flops=2 * work,
             )
+            if first:
+                (weights,) = rest
 
     def partial_gradient(other, dtype):
         (out,) = call(
             functools.partial(grad_kernel, other),
-            [shape((N_X, HALF, 256), dtype)],
+            [shape((2, BLOCK, 256), dtype)],
             [],
             place,
             row_parts,
@@ -385,10 +393,17 @@
 
     received = swapped(partial_gradient(True, jnp.bfloat16))
     chip = partial_gradient(False, jnp.float32) + received.astype(jnp.float32)
-    pieces = exchange(chip.astype(jnp.bfloat16), X_GROUPS)
-    half = jnp.sum(pieces.astype(jnp.float32), axis=0)
-    second = lax.ppermute(half, "grp", [(1, 0)])
-    return jnp.where(grp == 1, master, jnp.concatenate([half, second]))[None]
+    near, far = chip[0].astype(jnp.bfloat16), chip[1].astype(jnp.bfloat16)
+
+    def sent(block, source, distance):
+        return permuted(
+            block,
+            lambda grp, x, y, z: (0, (x + distance) % N_X, y, z) if grp == source else None,
+        ).astype(jnp.float32)
+
+    gradient = chip[0] + sent(far, 0, 2) + sent(near, 1, 1) + sent(far, 1, 3)
+    blended = MOMENTUM * own_master + (1.0 - MOMENTUM) * other_master
+    return jnp.where(grp == 1, blended, gradient)[None]
 
 
 def solution(mesh):

time: 145 us -> 133 us (0.917); the launches traced: 142 us -> 133 us
  blocking collectives: 84.4 us -> 69.7 us
  starting transfers between devices: 26 us -> 32.9 us
    all_to_all x7 -> x6, blocking collectives: 84.4 us -> 69.7 us  [exchange(): lax.all_to_all(blocks, AXES, 0, 0, axis_index_groups=groups, tiled=True)]
    ppermute x11 -> x13, starting transfers between devices: 23.4 us -> 30 us  [permuted(): return lax.ppermute(block, AXES, route)]
    ppermute x11 -> x13, waiting for transfers between devices: 14.1 us -> 12.4 us  [permuted(): return lax.ppermute(block, AXES, route)]
    ppermute x6, waiting for transfers between devices: 1.87 us -> 3.5 us  [swapped(): return lax.ppermute(block, 'grp', [(0, 1), (1, 0)])]
  transfers between devices with their start and end apart: 18 -> 20, of which waited for: 6 -> 10; matrix products, arithmetic and copies ran while one was open for 0% -> 0% of each run, Pallas kernels for 1% -> 1%
where the time goes in v4:
time: 133 us
  blocking collectives  69.7 us (52%)
  starting transfers between devices  32.9 us (25%)
  waiting for transfers between devices  15.9 us (12%)
  Pallas kernels  12.7 us (10%)
    all_to_all x6, blocking collectives, exchange(): lax.all_to_all(blocks, AXES, 0, 0, axis_index_groups=groups, tiled=True)  69.7 us
    ppermute x13, starting transfers between devices, permuted(): return lax.ppermute(block, AXES, route)  30 us
    ppermute x13, waiting for transfers between devices, permuted(): return lax.ppermute(block, AXES, route)  12.4 us
    pallas_call x8, Pallas kernels, call(): pl.pallas_call(kernel, out_shape=outs, in_specs=[smem if a.ndim == 1 else...  10.7 us
    ppermute x6, waiting for transfers between devices, swapped(): return lax.ppermute(block, 'grp', [(0, 1), (1, 0)])  3.5 us
  transfers between devices with their start and end apart: 20, of which 10 were waited for; matrix products, arithmetic and copies ran while one was open for 0% of the time, Pallas kernels for 1%

profile of v4, /device:TPU:2, one launch (start us, length us, event | category | flops | bytes accessed | tf_op | source)
XLA Modules:
  0.0 132.7 jit_solution(4447862059650861303)
XLA Ops:
  0.0 1.8 %collective-permute-start = (f32[512,256]{1,0:T(8,128)}, f32[512,256]{1,0:T(8,128)S(1)}, u32[]{:S(2)}, u32[]{:S(2)}) collective-permute-start(f32[512,256]{1,0:T(8,128)} %bitcast.17), channel_id=1, source_target_pairs={{0,128},{1,129},{2,130},{3,131},{4,132},{5,133},{6,134},{7,135},{8... | collective-permute-start | bytes 1572872 | tf_op jit(solution)/shard_map/ppermute | solution.py:317
  1.8 0.1 collective-permute-start.1
  1.9 0.1 pad_add_fusion.place_ref.refs_0_
  2.0 1.9 %collective-permute-done.1.other_features_ref = bf16[512,256]{1,0:T(8,128)(2,1)S(1)} collective-permute-done((bf16[512,256]{1,0:T(8,128)(2,1)}, bf16[512,256]{1,0:T(8,128)(2,1)S(1)}, u32[]{:S(2)}, u32[]{:S(2)}) %collective-permute-start.1) | collective-permute-done | bytes 262176 | tf_op jit(solution)/shard_map/ppermute | solution.py:60
  3.8 2.0 %shard_map.37 = (bf16[256,256]{1,0:T(8,128)(2,1)S(1)}, bf16[8,128]{1,0:T(8,128)(2,1)S(1)}, bf16[512,256]{1,0:T(8,128)(2,1)S(1)}) custom-call(s32[3]{0:T(128)S(1)} %pad_add_fusion.place_ref.refs_0_, bf16[512,256]{1,0:T(8,128)(2,1)} %bitcast.20, bf16[512,256]{1,0:T(8,128)(2,1)S(1)} %collective-permute-done.1.other_features_ref, s32[4,128]{1,0:T(4,128)} %bitcast.21, ...), custom_call_target="tpu_custom_call" | custom-call | tf_op jit(solution)/shard_map/pallas_call | solution.py:149
  5.9 2.0 %collective-permute-start.10 = (bf16[256,256]{1,0:T(8,128)(2,1)S(1)}, bf16[256,256]{1,0:T(8,128)(2,1)S(1)}, u32[]{:S(2)}, u32[]{:S(2)}) collective-permute-start(bf16[256,256]{1,0:T(8,128)(2,1)S(1)} %get-tuple-element.33.refs_1_), channel_id=1, source_target_pairs={{0,8},{1,9},{2,10},{3,11},{4,12},{5,13},{6,14},{7,15},{8,16},{9,17... | collective-permute-start | bytes 393224 | tf_op jit(solution)/shard_map/ppermute | solution.py:69
  7.9 1.5 %collective-permute-start.4 = (bf16[512,256]{1,0:T(8,128)(2,1)S(1)}, bf16[512,256]{1,0:T(8,128)(2,1)S(1)}, u32[]{:S(2)}, u32[]{:S(2)}) collective-permute-start(bf16[512,256]{1,0:T(8,128)(2,1)S(1)} %get-tuple-element.41.refs_9_), channel_id=1, source_target_pairs={{0,4},{1,5},{2,6},{3,7},{4,64},{5,65},{6,66},{7,67},{8,12},{9,13},... | collective-permute-start | bytes 786440 | tf_op jit(solution)/shard_map/ppermute | solution.py:69
  9.4 1.1 collective-permute-start.3
  10.5 6.3 %collective-permute-start.7 = (bf16[256,256]{1,0:T(8,128)(2,1)S(1)}, bf16[256,256]{1,0:T(8,128)(2,1)S(1)}, u32[]{:S(2)}, u32[]{:S(2)}) collective-permute-start(bf16[256,256]{1,0:T(8,128)(2,1)S(1)} %get-tuple-element.33.refs_1_), channel_id=1, source_target_pairs={{0,32},{1,33},{2,34},{3,35},{4,36},{5,37},{6,38},{7,39},{8,40},{9,... | collective-permute-start | bytes 393224 | tf_op jit(solution)/shard_map/ppermute | solution.py:69
  16.8 2.2 %collective-permute-start.5 = (bf16[256,256]{1,0:T(8,128)(2,1)S(1)}, bf16[256,256]{1,0:T(8,128)(2,1)S(1)}, u32[]{:S(2)}, u32[]{:S(2)}) collective-permute-start(bf16[256,256]{1,0:T(8,128)(2,1)S(1)} %get-tuple-element.33.refs_1_), channel_id=1, source_target_pairs={{0,56},{1,57},{2,58},{3,59},{4,60},{5,61},{6,62},{7,63},{8,0},{9,1... | collective-permute-start | bytes 393224 | tf_op jit(solution)/shard_map/ppermute | solution.py:69
  19.0 2.2 %collective-permute-start.2 = (bf16[512,256]{1,0:T(8,128)(2,1)S(1)}, bf16[512,256]{1,0:T(8,128)(2,1)S(1)}, u32[]{:S(2)}, u32[]{:S(2)}) collective-permute-start(bf16[512,256]{1,0:T(8,128)(2,1)S(1)} %get-tuple-element.41.refs_9_), channel_id=1, source_target_pairs={{0,68},{1,69},{2,70},{3,71},{4,0},{5,1},{6,2},{7,3},{8,76},{9,77},... | collective-permute-start | bytes 786440 | tf_op jit(solution)/shard_map/ppermute | solution.py:69
  21.2 3.3 %collective-permute-start.11 = (bf16[256,256]{1,0:T(8,128)(2,1)S(1)}, bf16[256,256]{1,0:T(8,128)(2,1)S(1)}, u32[]{:S(2)}, u32[]{:S(2)}) collective-permute-start(bf16[256,256]{1,0:T(8,128)(2,1)S(1)} %collective-permute-done.10.refs_8_), channel_id=1, source_target_pairs={{0,8},{1,9},{2,10},{3,11},{4,12},{5,13},{6,14},{7,15},{8,16},{9,17... | collective-permute-start | bytes 393224 | tf_op jit(solution)/shard_map/ppermute | solution.py:69
  24.5 1.9 %collective-permute-done.5.refs_2_ = bf16[256,256]{1,0:T(8,128)(2,1)S(1)} collective-permute-done((bf16[256,256]{1,0:T(8,128)(2,1)S(1)}, bf16[256,256]{1,0:T(8,128)(2,1)S(1)}, u32[]{:S(2)}, u32[]{:S(2)}) %collective-permute-start.5) | collective-permute-done | bytes 131104 | tf_op jit(solution)/shard_map/ppermute | solution.py:69
  26.3 2.7 %collective-permute-start.9 = (bf16[256,256]{1,0:T(8,128)(2,1)S(1)}, bf16[256,256]{1,0:T(8,128)(2,1)S(1)}, u32[]{:S(2)}, u32[]{:S(2)}) collective-permute-start(bf16[256,256]{1,0:T(8,128)(2,1)S(1)} %collective-permute-done.7.refs_5_), channel_id=1, source_target_pairs={{0,56},{1,57},{2,58},{3,59},{4,60},{5,61},{6,62},{7,63},{8,0},{9,1... | collective-permute-start | bytes 393224 | tf_op jit(solution)/shard_map/ppermute | solution.py:69
  29.0 3.2 %collective-permute-start.6 = (bf16[256,256]{1,0:T(8,128)(2,1)S(1)}, bf16[256,256]{1,0:T(8,128)(2,1)S(1)}, u32[]{:S(2)}, u32[]{:S(2)}) collective-permute-start(bf16[256,256]{1,0:T(8,128)(2,1)S(1)} %collective-permute-done.5.refs_2_), channel_id=1, source_target_pairs={{0,56},{1,57},{2,58},{3,59},{4,60},{5,61},{6,62},{7,63},{8,0},{9,1... | collective-permute-start | bytes 393224 | tf_op jit(solution)/shard_map/ppermute | solution.py:69
  32.2 2.9 %collective-permute-done.8.refs_4_ = bf16[256,256]{1,0:T(8,128)(2,1)S(1)} collective-permute-done((bf16[256,256]{1,0:T(8,128)(2,1)S(1)}, bf16[256,256]{1,0:T(8,128)(2,1)S(1)}, u32[]{:S(2)}, u32[]{:S(2)}) %collective-permute-start.8) | collective-permute-done | bytes 131104 | tf_op jit(solution)/shard_map/ppermute | solution.py:69
  35.2 0.5 collective-permute-start.13
  35.7 0.0 collective-permute-start.14
  35.7 0.5 collective-permute-start.15
  36.2 0.5 collective-permute-done.12.refs_13_
  36.7 0.4 collective-permute-done.13.refs_14_
  37.1 0.4 collective-permute-done.14.refs_15_
  37.5 0.4 collective-permute-done.15.refs_16_
  37.8 3.1 %shard_map.38 = (f32[2048,1024]{1,0:T(8,128)S(1)}, f32[2048,1024]{1,0:T(8,128)S(1)}, f32[8,16,128]{2,1,0:T(8,128)S(1)}, f32[8,128]{1,0:T(8,128)S(1)}, bf16[1024,256]{1,0:T(8,128)(2,1)S(1)}) custom-call(s32[3]{0:T(128)S(1)} %pad_add_fusion.place_ref.refs_0_, bf16[256,256]{1,0:T(8,128)(2,1)S(1)} %get-tuple-element.33.refs_1_, ...), custom_call_target="tpu_custom_call" | custom-call | flops 2147483648 | bytes 8388608 | tf_op jit(solution)/shard_map/pallas_call | solution.py:292
  40.9 8.7 %all_to_all.30.refs_0_ = f32[8,16,128]{2,1,0:T(8,128)S(1)} all-to-all(f32[8,16,128]{2,1,0:T(8,128)S(1)} %get-tuple-element.45), channel_id=1, replica_groups={{0,4,64,68,128,132,192,196},{1,5,65,69,129,133,193,197},{2,6,66,70,130,..., dimensions={0} | all-to-all | bytes 131072 | tf_op jit(solution)/shard_map/all_to_all | solution.py:56
  49.7 0.8 shard_map.39
  50.5 18.1 %all_to_all.31.refs_0_ = bf16[32,16,128]{2,1,0:T(8,128)(2,1)S(1)} all-to-all(bf16[32,16,128]{2,1,0:T(8,128)(2,1)S(1)} %get-tuple-element.48), channel_id=1, replica_groups={{0,1,2,3,8,9,10,11,16,17,18,19,24,25,26,27,32,33,34,35,40,41,42,43,48,4..., dimensions={0} | all-to-all | bytes 262144 | tf_op jit(solution)/shard_map/all_to_all | solution.py:56
  68.6 0.7 shard_map.40
  69.3 7.7 %all_to_all.32.refs_0_ = f32[8,16,128]{2,1,0:T(8,128)S(1)} all-to-all(f32[8,16,128]{2,1,0:T(8,128)S(1)} %get-tuple-element.49), channel_id=1, replica_groups={{0,4,64,68,128,132,192,196},{1,5,65,69,129,133,193,197},{2,6,66,70,130,..., dimensions={0} | all-to-all | bytes 131072 | tf_op jit(solution)/shard_map/all_to_all | solution.py:56
  77.0 0.8 shard_map.41
  77.9 13.2 %all_to_all.33.refs_0_ = bf16[32,8,128]{2,1,0:T(8,128)(2,1)S(1)} all-to-all(bf16[32,8,128]{2,1,0:T(8,128)(2,1)S(1)} %get-tuple-element.50), channel_id=1, replica_groups={{0,1,2,3,8,9,10,11,16,17,18,19,24,25,26,27,32,33,34,35,40,41,42,43,48,4..., dimensions={0} | all-to-all | bytes 131072 | tf_op jit(solution)/shard_map/all_to_all | solution.py:56
  91.1 0.7 shard_map.42
  91.8 7.9 %all_to_all.34.refs_0_ = f32[8,16,128]{2,1,0:T(8,128)S(1)} all-to-all(f32[8,16,128]{2,1,0:T(8,128)S(1)} %shard_map.42), channel_id=1, replica_groups={{0,4,64,68,128,132,192,196},{1,5,65,69,129,133,193,197},{2,6,66,70,130,..., dimensions={0} | all-to-all | bytes 131072 | tf_op jit(solution)/shard_map/all_to_all | solution.py:56
  99.7 0.7 shard_map.43
  100.4 14.1 %all_to_all.35.parts_ref = bf16[32,16,128]{2,1,0:T(8,128)(2,1)S(1)} all-to-all(bf16[32,16,128]{2,1,0:T(8,128)(2,1)S(1)} %get-tuple-element.52), channel_id=1, replica_groups={{0,1,2,3,8,9,10,11,16,17,18,19,24,25,26,27,32,33,34,35,40,41,42,43,48,4..., dimensions={0} | all-to-all | bytes 262144 | tf_op jit(solution)/shard_map/all_to_all | solution.py:56
  114.4 1.9 %shard_map.45 = bf16[2,512,256]{2,1,0:T(8,128)(2,1)S(1)} custom-call(s32[3]{0:T(128)S(1)} %pad_add_fusion.place_ref.refs_0_, bf16[32,16,128]{2,1,0:T(8,128)(2,1)S(1)} %all_to_all.35.parts_ref, f32[16,128]{1,0:T(8,128)S(1)} %get-tuple-element.53.scale_ref, f32[8,128]{1,0:T(8,128)S(1)} %get-tuple-element.54.weight_ref, ...), custom_call_target="tpu_custom_call" | custom-call | flops 536870912 | bytes 8388608 | tf_op jit(solution)/shard_map/pallas_call | solution.py:292
  116.4 0.0 copy-start
  116.4 0.1 collective-permute-start.16
  116.5 1.9 %shard_map.44 = f32[2,512,256]{2,1,0:T(8,128)S(1)} custom-call(s32[3]{0:T(128)S(1)} %pad_add_fusion.place_ref.refs_0_, bf16[32,16,128]{2,1,0:T(8,128)(2,1)S(1)} %all_to_all.35.parts_ref, f32[16,128]{1,0:T(8,128)S(1)} %get-tuple-element.53.scale_ref, f32[8,128]{1,0:T(8,128)S(1)} %get-tuple-element.54.weight_ref, ...), custom_call_target="tpu_custom_call" | custom-call | flops 536870912 | bytes 8388608 | tf_op jit(solution)/shard_map/pallas_call | solution.py:292
  118.4 0.1 convert_add_fusion
  118.5 0.1 fusion
  118.6 1.3 collective-permute-start.18
  119.9 1.3 collective-permute-start.19
  121.2 2.9 %collective-permute-start.17 = (bf16[512,256]{1,0:T(8,128)(2,1)S(1)}, bf16[512,256]{1,0:T(8,128)(2,1)S(1)}, u32[]{:S(2)}, u32[]{:S(2)}) collective-permute-start(bf16[512,256]{1,0:T(8,128)(2,1)S(1)} %get-tuple-element.58), channel_id=1, source_target_pairs={{0,64},{1,65},{2,66},{3,67},{4,68},{5,69},{6,70},{7,71},{8,72},{9,... | collective-permute-start | bytes 786440 | tf_op jit(solution)/shard_map/ppermute | solution.py:69
  124.1 2.2 %collective-permute-done.18 = bf16[512,256]{1,0:T(8,128)(2,1)S(1)} collective-permute-done((bf16[512,256]{1,0:T(8,128)(2,1)S(1)}, bf16[512,256]{1,0:T(8,128)(2,1)S(1)}, u32[]{:S(2)}, u32[]{:S(2)}) %collective-permute-start.18) | collective-permute-done | bytes 262176 | tf_op jit(solution)/shard_map/ppermute | solution.py:69
  126.3 1.3 collective-permute-done.19
  127.6 4.1 %collective-permute-done.17 = bf16[512,256]{1,0:T(8,128)(2,1)S(1)} collective-permute-done((bf16[512,256]{1,0:T(8,128)(2,1)S(1)}, bf16[512,256]{1,0:T(8,128)(2,1)S(1)}, u32[]{:S(2)}, u32[]{:S(2)}) %collective-permute-start.17) | collective-permute-done | bytes 262176 | tf_op jit(solution)/shard_map/ppermute | solution.py:69
  131.7 1.0 select_bitcast_fusion
  (13 shorter events, 0.0 us)
Async XLA Ops:
  0.0 3.8 %collective-permute-start = (f32[512,256]{1,0:T(8,128)}, f32[512,256]{1,0:T(8,128)S(1)}, u32[]{:S(2)}, u32[]{:S(2)}) collective-permute-start(f32[512,256]{1,0:T(8,128)} %bitcast.17), channel_id=1, source_target_pairs={{0,128},{1,129},{2,130},{3,131},{4,132},{5,133},{6,134},{7,135},{8... | collective-permute-start | bytes 1572872 | tf_op jit(solution)/shard_map/ppermute | solution.py:317
  1.8 2.1 %collective-permute-start.1 = (bf16[512,256]{1,0:T(8,128)(2,1)}, bf16[512,256]{1,0:T(8,128)(2,1)S(1)}, u32[]{:S(2)}, u32[]{:S(2)}) collective-permute-start(bf16[512,256]{1,0:T(8,128)(2,1)} %bitcast.19), channel_id=1, source_target_pairs={{0,128},{128,0},{1,129},{129,1},{2,130},{130,2},{3,131},{131,3},{4... | collective-permute-start | bytes 786440 | tf_op jit(solution)/shard_map/ppermute | solution.py:60
  5.9 13.1 %collective-permute-start.10 = (bf16[256,256]{1,0:T(8,128)(2,1)S(1)}, bf16[256,256]{1,0:T(8,128)(2,1)S(1)}, u32[]{:S(2)}, u32[]{:S(2)}) collective-permute-start(bf16[256,256]{1,0:T(8,128)(2,1)S(1)} %get-tuple-element.33.refs_1_), channel_id=1, source_target_pairs={{0,8},{1,9},{2,10},{3,11},{4,12},{5,13},{6,14},{7,15},{8,16},{9,17... | collective-permute-start | bytes 393224 | tf_op jit(solution)/shard_map/ppermute | solution.py:69
  7.9 21.1 %collective-permute-start.4 = (bf16[512,256]{1,0:T(8,128)(2,1)S(1)}, bf16[512,256]{1,0:T(8,128)(2,1)S(1)}, u32[]{:S(2)}, u32[]{:S(2)}) collective-permute-start(bf16[512,256]{1,0:T(8,128)(2,1)S(1)} %get-tuple-element.41.refs_9_), channel_id=1, source_target_pairs={{0,4},{1,5},{2,6},{3,7},{4,64},{5,65},{6,66},{7,67},{8,12},{9,13},... | collective-permute-start | bytes 786440 | tf_op jit(solution)/shard_map/ppermute | solution.py:69
  9.4 19.6 %collective-permute-start.3 = (bf16[512,256]{1,0:T(8,128)(2,1)S(1)}, bf16[512,256]{1,0:T(8,128)(2,1)S(1)}, u32[]{:S(2)}, u32[]{:S(2)}) collective-permute-start(bf16[512,256]{1,0:T(8,128)(2,1)S(1)} %get-tuple-element.41.refs_9_), channel_id=1, source_target_pairs={{0,64},{1,65},{2,66},{3,67},{4,68},{5,69},{6,70},{7,71},{8,72},{9,... | collective-permute-start | bytes 786440 | tf_op jit(solution)/shard_map/ppermute | solution.py:69
  10.5 10.7 %collective-permute-start.7 = (bf16[256,256]{1,0:T(8,128)(2,1)S(1)}, bf16[256,256]{1,0:T(8,128)(2,1)S(1)}, u32[]{:S(2)}, u32[]{:S(2)}) collective-permute-start(bf16[256,256]{1,0:T(8,128)(2,1)S(1)} %get-tuple-element.33.refs_1_), channel_id=1, source_target_pairs={{0,32},{1,33},{2,34},{3,35},{4,36},{5,37},{6,38},{7,39},{8,40},{9,... | collective-permute-start | bytes 393224 | tf_op jit(solution)/shard_map/ppermute | solution.py:69
  16.8 9.5 %collective-permute-start.5 = (bf16[256,256]{1,0:T(8,128)(2,1)S(1)}, bf16[256,256]{1,0:T(8,128)(2,1)S(1)}, u32[]{:S(2)}, u32[]{:S(2)}) collective-permute-start(bf16[256,256]{1,0:T(8,128)(2,1)S(1)} %get-tuple-element.33.refs_1_), channel_id=1, source_target_pairs={{0,56},{1,57},{2,58},{3,59},{4,60},{5,61},{6,62},{7,63},{8,0},{9,1... | collective-permute-start | bytes 393224 | tf_op jit(solution)/shard_map/ppermute | solution.py:69
  19.0 13.2 %collective-permute-start.2 = (bf16[512,256]{1,0:T(8,128)(2,1)S(1)}, bf16[512,256]{1,0:T(8,128)(2,1)S(1)}, u32[]{:S(2)}, u32[]{:S(2)}) collective-permute-start(bf16[512,256]{1,0:T(8,128)(2,1)S(1)} %get-tuple-element.41.refs_9_), channel_id=1, source_target_pairs={{0,68},{1,69},{2,70},{3,71},{4,0},{5,1},{6,2},{7,3},{8,76},{9,77},... | collective-permute-start | bytes 786440 | tf_op jit(solution)/shard_map/ppermute | solution.py:69
  21.2 11.1 %collective-permute-start.11 = (bf16[256,256]{1,0:T(8,128)(2,1)S(1)}, bf16[256,256]{1,0:T(8,128)(2,1)S(1)}, u32[]{:S(2)}, u32[]{:S(2)}) collective-permute-start(bf16[256,256]{1,0:T(8,128)(2,1)S(1)} %collective-permute-done.10.refs_8_), channel_id=1, source_target_pairs={{0,8},{1,9},{2,10},{3,11},{4,12},{5,13},{6,14},{7,15},{8,16},{9,17... | collective-permute-start | bytes 393224 | tf_op jit(solution)/shard_map/ppermute | solution.py:69
  26.3 5.9 %collective-permute-start.9 = (bf16[256,256]{1,0:T(8,128)(2,1)S(1)}, bf16[256,256]{1,0:T(8,128)(2,1)S(1)}, u32[]{:S(2)}, u32[]{:S(2)}) collective-permute-start(bf16[256,256]{1,0:T(8,128)(2,1)S(1)} %collective-permute-done.7.refs_5_), channel_id=1, source_target_pairs={{0,56},{1,57},{2,58},{3,59},{4,60},{5,61},{6,62},{7,63},{8,0},{9,1... | collective-permute-start | bytes 393224 | tf_op jit(solution)/shard_map/ppermute | solution.py:69
  29.0 6.2 %collective-permute-start.8 = (bf16[256,256]{1,0:T(8,128)(2,1)S(1)}, bf16[256,256]{1,0:T(8,128)(2,1)S(1)}, u32[]{:S(2)}, u32[]{:S(2)}) collective-permute-start(bf16[256,256]{1,0:T(8,128)(2,1)S(1)} %collective-permute-done.7.refs_5_), channel_id=1, source_target_pairs={{0,8},{1,9},{2,10},{3,11},{4,12},{5,13},{6,14},{7,15},{8,16},{9,17... | collective-permute-start | bytes 393224 | tf_op jit(solution)/shard_map/ppermute | solution.py:69
  29.0 6.2 %collective-permute-start.6 = (bf16[256,256]{1,0:T(8,128)(2,1)S(1)}, bf16[256,256]{1,0:T(8,128)(2,1)S(1)}, u32[]{:S(2)}, u32[]{:S(2)}) collective-permute-start(bf16[256,256]{1,0:T(8,128)(2,1)S(1)} %collective-permute-done.5.refs_2_), channel_id=1, source_target_pairs={{0,56},{1,57},{2,58},{3,59},{4,60},{5,61},{6,62},{7,63},{8,0},{9,1... | collective-permute-start | bytes 393224 | tf_op jit(solution)/shard_map/ppermute | solution.py:69
  35.2 1.5 %collective-permute-start.12 = (bf16[512,256]{1,0:T(8,128)(2,1)S(1)}, bf16[512,256]{1,0:T(8,128)(2,1)S(1)}, u32[]{:S(2)}, u32[]{:S(2)}) collective-permute-start(bf16[512,256]{1,0:T(8,128)(2,1)S(1)} %get-tuple-element.41.refs_9_), channel_id=1, source_target_pairs={{0,128},{128,0},{1,129},{129,1},{2,130},{130,2},{3,131},{131,3},{4... | collective-permute-start | bytes 786440 | tf_op jit(solution)/shard_map/ppermute | solution.py:60
  35.2 1.9 %collective-permute-start.13 = (bf16[512,256]{1,0:T(8,128)(2,1)S(1)}, bf16[512,256]{1,0:T(8,128)(2,1)S(1)}, u32[]{:S(2)}, u32[]{:S(2)}) collective-permute-start(bf16[512,256]{1,0:T(8,128)(2,1)S(1)} %collective-permute-done.2.refs_10_), channel_id=1, source_target_pairs={{0,128},{128,0},{1,129},{129,1},{2,130},{130,2},{3,131},{131,3},{4... | collective-permute-start | bytes 786440 | tf_op jit(solution)/shard_map/ppermute | solution.py:60
  35.7 1.8 %collective-permute-start.14 = (bf16[512,256]{1,0:T(8,128)(2,1)S(1)}, bf16[512,256]{1,0:T(8,128)(2,1)S(1)}, u32[]{:S(2)}, u32[]{:S(2)}) collective-permute-start(bf16[512,256]{1,0:T(8,128)(2,1)S(1)} %collective-permute-done.3.refs_11_), channel_id=1, source_target_pairs={{0,128},{128,0},{1,129},{129,1},{2,130},{130,2},{3,131},{131,3},{4... | collective-permute-start | bytes 786440 | tf_op jit(solution)/shard_map/ppermute | solution.py:60
  35.7 2.1 %collective-permute-start.15 = (bf16[512,256]{1,0:T(8,128)(2,1)S(1)}, bf16[512,256]{1,0:T(8,128)(2,1)S(1)}, u32[]{:S(2)}, u32[]{:S(2)}) collective-permute-start(bf16[512,256]{1,0:T(8,128)(2,1)S(1)} %collective-permute-done.4.refs_12_), channel_id=1, source_target_pairs={{0,128},{128,0},{1,129},{129,1},{2,130},{130,2},{3,131},{131,3},{4... | collective-permute-start | bytes 786440 | tf_op jit(solution)/shard_map/ppermute | solution.py:60
  116.4 15.3 %copy-start = (f32[1,512,256]{2,1,0:T(8,128)S(1)}, f32[1,512,256]{2,1,0:T(8,128)}, u32[]{:S(2)}) copy-start(f32[1,512,256]{2,1,0:T(8,128)} %param.4) | copy-start | bytes 1572868
  116.4 2.0 %collective-permute-start.16 = (bf16[2,512,256]{2,1,0:T(8,128)(2,1)S(1)}, bf16[2,512,256]{2,1,0:T(8,128)(2,1)S(1)}, u32[]{:S(2)}, u32[]{:S(2)}) collective-permute-start(bf16[2,512,256]{2,1,0:T(8,128)(2,1)S(1)} %shard_map.45), channel_id=1, source_target_pairs={{0,128},{128,0},{1,129},{129,1},{2,130},{130,2},{3,131},{131,3},{4... | collective-permute-start | bytes 1572872 | tf_op jit(solution)/shard_map/ppermute | solution.py:60
  118.6 7.7 %collective-permute-start.18 = (bf16[512,256]{1,0:T(8,128)(2,1)S(1)}, bf16[512,256]{1,0:T(8,128)(2,1)S(1)}, u32[]{:S(2)}, u32[]{:S(2)}) collective-permute-start(bf16[512,256]{1,0:T(8,128)(2,1)S(1)} %get-tuple-element.57), channel_id=1, source_target_pairs={{128,4},{129,5},{130,6},{131,7},{132,64},{133,65},{134,66},{135,67... | collective-permute-start | bytes 786440 | tf_op jit(solution)/shard_map/ppermute | solution.py:69
  119.9 7.7 %collective-permute-start.19 = (bf16[512,256]{1,0:T(8,128)(2,1)S(1)}, bf16[512,256]{1,0:T(8,128)(2,1)S(1)}, u32[]{:S(2)}, u32[]{:S(2)}) collective-permute-start(bf16[512,256]{1,0:T(8,128)(2,1)S(1)} %get-tuple-element.58), channel_id=1, source_target_pairs={{128,68},{129,69},{130,70},{131,71},{132,0},{133,1},{134,2},{135,3... | collective-permute-start | bytes 786440 | tf_op jit(solution)/shard_map/ppermute | solution.py:69
  121.2 10.5 %collective-permute-start.17 = (bf16[512,256]{1,0:T(8,128)(2,1)S(1)}, bf16[512,256]{1,0:T(8,128)(2,1)S(1)}, u32[]{:S(2)}, u32[]{:S(2)}) collective-permute-start(bf16[512,256]{1,0:T(8,128)(2,1)S(1)} %get-tuple-element.58), channel_id=1, source_target_pairs={{0,64},{1,65},{2,66},{3,67},{4,68},{5,69},{6,70},{7,71},{8,72},{9,... | collective-permute-start | bytes 786440 | tf_op jit(solution)/shard_map/ppermute | solution.py:69

commit v5 on v4

--- a/solution.py
+++ b/solution.py
@@ -253,6 +253,7 @@
 
 def grad_kernel(
     other,
+    pieces,
     place_ref,
     parts_ref,
     scale_ref,
@@ -264,9 +265,10 @@
 ):
     inverse = 1.0 / jnp.sum(parts_ref[...].astype(jnp.float32), axis=0)
     row_inverse, student_inverse = lanes(inverse[0:8, :]), lanes(inverse[8:16, :])
-    weight = lanes(weight_ref[...])
+    weight = lanes(weight_ref[...] * PROTOS)
+    teacher_row, student_row = row_inverse * weight, student_inverse * weight
     first = 1 - place_ref[0] if other else place_ref[0]
-    for k in range(2):
+    for n, k in enumerate(pieces):
         base = (place_ref[1] + 2 * k + first) % N_X * BLOCK
         for i in range(BLOCK // 256):
             errors = []
@@ -274,12 +276,10 @@
                 start = base + i * 256 + h * 128
                 column = to_column(scale_ref[pl.ds(start // 128, 1), :])
                 rows = pl.ds(pl.multiple_of(start, 128), 128)
-                targets = (teacher_exp_ref[rows, :] * column * row_inverse).astype(jnp.bfloat16)
-                probs = student_exp_ref[rows, :] * student_inverse
-                errors.append(
-                    (PROTOS * (probs - targets.astype(jnp.float32)) * weight).astype(jnp.bfloat16)
-                )
-            out_ref[k, i * 256 : (i + 1) * 256, :] = jnp.dot(
+                targets = teacher_exp_ref[rows, :] * column * teacher_row
+                probs = student_exp_ref[rows, :] * student_row
+                errors.append((probs - targets).astype(jnp.bfloat16))
+            out_ref[n, i * 256 : (i + 1) * 256, :] = jnp.dot(
                 jnp.concatenate(errors, axis=0),
                 token_ref[...],
                 preferred_element_type=jnp.float32,
@@ -324,12 +324,15 @@
         own_master,
         other_master,
     )
-    packs = {0: pack, 4: from_z(pack, 4), 1: from_z(pack, 1), 7: from_z(pack, -1)}
-    packs[2], packs[5] = from_z(packs[1], 1), from_z(packs[4], 1)
-    packs[6], packs[3] = from_z(packs[7], -1), from_z(packs[4], -1)
-    own_units = [unit] + [from_x(unit, k) for k in range(1, N_X)]
-    held, packs = lax.optimization_barrier((tuple(own_units), packs))
-    other_units = [swapped(block) for block in held]
+    packs = {0: pack}
+    for k in range(1, 5):
+        packs[k] = from_z(packs[k - 1], 1)
+        if k < 4:
+            packs[N_Z - k] = from_z(packs[(N_Z - k + 1) % N_Z], -1)
+    own_units = [unit, from_x(unit, 1), None, from_x(unit, -1)]
+    own_units[2] = from_x(own_units[1], 1)
+    held, packs = lax.optimization_barrier((tuple(own_units[1:]), packs))
+    other_units = [swapped(unit)] + [swapped(block) for block in held]
 
     teacher_exp, student_exp, col_parts, student_part, student_tokens = call(
         exp_kernel,
@@ -375,10 +378,10 @@
             if first:
                 (weights,) = rest
 
-    def partial_gradient(other, dtype):
+    def partial_gradient(other, pieces, dtype):
         (out,) = call(
-            functools.partial(grad_kernel, other),
-            [shape((2, BLOCK, 256), dtype)],
+            functools.partial(grad_kernel, other, pieces),
+            [shape((len(pieces), BLOCK, 256), dtype)],
             [],
             place,
             row_parts,
@@ -391,8 +394,8 @@
         )
         return out
 
-    received = swapped(partial_gradient(True, jnp.bfloat16))
-    chip = partial_gradient(False, jnp.float32) + received.astype(jnp.float32)
+    received = swapped(partial_gradient(True, (0, 1), jnp.bfloat16))
+    chip = partial_gradient(False, (0, 1), jnp.float32) + received.astype(jnp.float32)
     near, far = chip[0].astype(jnp.bfloat16), chip[1].astype(jnp.bfloat16)
 
     def sent(block, source, distance):

time: 133 us -> 131 us (0.985)
  starting transfers between devices: 32.9 us -> 27.5 us
  waiting for transfers between devices: 15.9 us -> 19.9 us
    ppermute x13, starting transfers between devices: 30 us -> 25 us  [permuted(): return lax.ppermute(block, AXES, route)]
    ppermute x13, waiting for transfers between devices: 12.4 us -> 15.9 us  [permuted(): return lax.ppermute(block, AXES, route)]
  transfers between devices with their start and end apart: 20 -> 20, of which waited for: 10 -> 14; matrix products, arithmetic and copies ran while one was open for 0% -> 0% of each run, Pallas kernels for 1% -> 1%
where the time goes in v5:
time: 131 us
  blocking collectives  70.1 us (54%)
  starting transfers between devices  27.5 us (21%)
  waiting for transfers between devices  19.9 us (15%)
  Pallas kernels  11.9 us (9%)
    all_to_all x6, blocking collectives, exchange(): lax.all_to_all(blocks, AXES, 0, 0, axis_index_groups=groups, tiled=True)  70.1 us
    ppermute x13, starting transfers between devices, permuted(): return lax.ppermute(block, AXES, route)  25 us
    ppermute x13, waiting for transfers between devices, permuted(): return lax.ppermute(block, AXES, route)  15.9 us
    pallas_call x8, Pallas kernels, call(): pl.pallas_call(kernel, out_shape=outs, in_specs=[smem if a.ndim == 1 else...  9.86 us
    ppermute x6, waiting for transfers between devices, swapped(): return lax.ppermute(block, 'grp', [(0, 1), (1, 0)])  4.02 us
  transfers between devices with their start and end apart: 20, of which 14 were waited for; matrix products, arithmetic and copies ran while one was open for 0% of the time, Pallas kernels for 1%

profile of v5, /device:TPU:2, one launch (start us, length us, event | category | flops | bytes accessed | tf_op | source)
XLA Modules:
  0.0 130.8 jit_solution(18405104919311813620)
XLA Ops:
  0.0 1.8 %collective-permute-start = (f32[512,256]{1,0:T(8,128)}, f32[512,256]{1,0:T(8,128)S(1)}, u32[]{:S(2)}, u32[]{:S(2)}) collective-permute-start(f32[512,256]{1,0:T(8,128)} %bitcast.17), channel_id=1, source_target_pairs={{0,128},{1,129},{2,130},{3,131},{4,132},{5,133},{6,134},{7,135},{8... | collective-permute-start | bytes 1572872 | tf_op jit(solution)/shard_map/ppermute | solution.py:317
  1.8 0.1 collective-permute-start.1
  1.9 0.1 pad_add_fusion.place_ref.refs_0_
  2.0 1.9 %collective-permute-done.1.other_features_ref = bf16[512,256]{1,0:T(8,128)(2,1)S(1)} collective-permute-done((bf16[512,256]{1,0:T(8,128)(2,1)}, bf16[512,256]{1,0:T(8,128)(2,1)S(1)}, u32[]{:S(2)}, u32[]{:S(2)}) %collective-permute-start.1) | collective-permute-done | bytes 262176 | tf_op jit(solution)/shard_map/ppermute | solution.py:60
  3.8 2.0 %shard_map.37 = (bf16[256,256]{1,0:T(8,128)(2,1)S(1)}, bf16[8,128]{1,0:T(8,128)(2,1)S(1)}, bf16[512,256]{1,0:T(8,128)(2,1)S(1)}) custom-call(s32[3]{0:T(128)S(1)} %pad_add_fusion.place_ref.refs_0_, bf16[512,256]{1,0:T(8,128)(2,1)} %bitcast.20, bf16[512,256]{1,0:T(8,128)(2,1)S(1)} %collective-permute-done.1.other_features_ref, s32[4,128]{1,0:T(4,128)} %bitcast.21, ...), custom_call_target="tpu_custom_call" | custom-call | tf_op jit(solution)/shard_map/pallas_call | solution.py:149
  5.9 5.9 %collective-permute-start.5 = (bf16[256,256]{1,0:T(8,128)(2,1)S(1)}, bf16[256,256]{1,0:T(8,128)(2,1)S(1)}, u32[]{:S(2)}, u32[]{:S(2)}) collective-permute-start(bf16[256,256]{1,0:T(8,128)(2,1)S(1)} %get-tuple-element.32.refs_1_), channel_id=1, source_target_pairs={{0,56},{1,57},{2,58},{3,59},{4,60},{5,61},{6,62},{7,63},{8,0},{9,1... | collective-permute-start | bytes 393224 | tf_op jit(solution)/shard_map/ppermute | solution.py:69
  11.8 0.5 collective-permute-start.2
  12.4 2.7 %collective-permute-done.5.refs_2_ = bf16[256,256]{1,0:T(8,128)(2,1)S(1)} collective-permute-done((bf16[256,256]{1,0:T(8,128)(2,1)S(1)}, bf16[256,256]{1,0:T(8,128)(2,1)S(1)}, u32[]{:S(2)}, u32[]{:S(2)}) %collective-permute-start.5) | collective-permute-done | bytes 131104 | tf_op jit(solution)/shard_map/ppermute | solution.py:69
  15.1 3.7 %collective-permute-start.6 = (bf16[256,256]{1,0:T(8,128)(2,1)S(1)}, bf16[256,256]{1,0:T(8,128)(2,1)S(1)}, u32[]{:S(2)}, u32[]{:S(2)}) collective-permute-start(bf16[256,256]{1,0:T(8,128)(2,1)S(1)} %collective-permute-done.5.refs_2_), channel_id=1, source_target_pairs={{0,56},{1,57},{2,58},{3,59},{4,60},{5,61},{6,62},{7,63},{8,0},{9,1... | collective-permute-start | bytes 393224 | tf_op jit(solution)/shard_map/ppermute | solution.py:69
  18.8 1.5 %collective-permute-start.4 = (bf16[512,256]{1,0:T(8,128)(2,1)S(1)}, bf16[512,256]{1,0:T(8,128)(2,1)S(1)}, u32[]{:S(2)}, u32[]{:S(2)}) collective-permute-start(bf16[512,256]{1,0:T(8,128)(2,1)S(1)} %get-tuple-element.30.refs_9_), channel_id=1, source_target_pairs={{0,4},{1,5},{2,6},{3,7},{4,64},{5,65},{6,66},{7,67},{8,12},{9,13},... | collective-permute-start | bytes 786440 | tf_op jit(solution)/shard_map/ppermute | solution.py:69
  20.3 1.0 collective-permute-done.6.refs_3_
  21.3 3.7 %collective-permute-start.7 = (bf16[256,256]{1,0:T(8,128)(2,1)S(1)}, bf16[256,256]{1,0:T(8,128)(2,1)S(1)}, u32[]{:S(2)}, u32[]{:S(2)}) collective-permute-start(bf16[256,256]{1,0:T(8,128)(2,1)S(1)} %collective-permute-done.6.refs_3_), channel_id=1, source_target_pairs={{0,56},{1,57},{2,58},{3,59},{4,60},{5,61},{6,62},{7,63},{8,0},{9,1... | collective-permute-start | bytes 393224 | tf_op jit(solution)/shard_map/ppermute | solution.py:69
  25.0 0.5 collective-permute-start.3
  25.5 1.0 collective-permute-done.10.refs_7_
  26.5 1.0 collective-permute-done.7.refs_4_
  27.5 3.7 %collective-permute-start.8 = (bf16[256,256]{1,0:T(8,128)(2,1)S(1)}, bf16[256,256]{1,0:T(8,128)(2,1)S(1)}, u32[]{:S(2)}, u32[]{:S(2)}) collective-permute-start(bf16[256,256]{1,0:T(8,128)(2,1)S(1)} %collective-permute-done.7.refs_4_), channel_id=1, source_target_pairs={{0,56},{1,57},{2,58},{3,59},{4,60},{5,61},{6,62},{7,63},{8,0},{9,1... | collective-permute-start | bytes 393224 | tf_op jit(solution)/shard_map/ppermute | solution.py:69
  31.2 1.5 %collective-permute-done.11.refs_6_ = bf16[256,256]{1,0:T(8,128)(2,1)S(1)} collective-permute-done((bf16[256,256]{1,0:T(8,128)(2,1)S(1)}, bf16[256,256]{1,0:T(8,128)(2,1)S(1)}, u32[]{:S(2)}, u32[]{:S(2)}) %collective-permute-start.11) | collective-permute-done | bytes 131104 | tf_op jit(solution)/shard_map/ppermute | solution.py:69
  32.7 1.0 collective-permute-done.8.refs_5_
  33.7 0.5 collective-permute-start.14
  34.2 1.0 collective-permute-done.13.refs_14_
  35.2 0.4 collective-permute-done.14.refs_15_
  35.6 0.4 collective-permute-done.15.refs_16_
  36.0 3.1 %shard_map.38 = (f32[2048,1024]{1,0:T(8,128)S(1)}, f32[2048,1024]{1,0:T(8,128)S(1)}, f32[8,16,128]{2,1,0:T(8,128)S(1)}, f32[8,128]{1,0:T(8,128)S(1)}, bf16[1024,256]{1,0:T(8,128)(2,1)S(1)}) custom-call(s32[3]{0:T(128)S(1)} %pad_add_fusion.place_ref.refs_0_, bf16[256,256]{1,0:T(8,128)(2,1)S(1)} %get-tuple-element.32.refs_1_, ...), custom_call_target="tpu_custom_call" | custom-call | flops 2147483648 | bytes 8388608 | tf_op jit(solution)/shard_map/pallas_call | solution.py:292
  39.1 8.7 %all_to_all.30.refs_0_ = f32[8,16,128]{2,1,0:T(8,128)S(1)} all-to-all(f32[8,16,128]{2,1,0:T(8,128)S(1)} %get-tuple-element.43), channel_id=1, replica_groups={{0,4,64,68,128,132,192,196},{1,5,65,69,129,133,193,197},{2,6,66,70,130,..., dimensions={0} | all-to-all | bytes 131072 | tf_op jit(solution)/shard_map/all_to_all | solution.py:56
  47.8 0.8 shard_map.39
  48.6 18.5 %all_to_all.31.refs_0_ = bf16[32,16,128]{2,1,0:T(8,128)(2,1)S(1)} all-to-all(bf16[32,16,128]{2,1,0:T(8,128)(2,1)S(1)} %get-tuple-element.46), channel_id=1, replica_groups={{0,1,2,3,8,9,10,11,16,17,18,19,24,25,26,27,32,33,34,35,40,41,42,43,48,4..., dimensions={0} | all-to-all | bytes 262144 | tf_op jit(solution)/shard_map/all_to_all | solution.py:56
  67.1 0.7 shard_map.40
  67.8 7.7 %all_to_all.32.refs_0_ = f32[8,16,128]{2,1,0:T(8,128)S(1)} all-to-all(f32[8,16,128]{2,1,0:T(8,128)S(1)} %get-tuple-element.47), channel_id=1, replica_groups={{0,4,64,68,128,132,192,196},{1,5,65,69,129,133,193,197},{2,6,66,70,130,..., dimensions={0} | all-to-all | bytes 131072 | tf_op jit(solution)/shard_map/all_to_all | solution.py:56
  75.6 0.8 shard_map.41
  76.4 13.2 %all_to_all.33.refs_0_ = bf16[32,8,128]{2,1,0:T(8,128)(2,1)S(1)} all-to-all(bf16[32,8,128]{2,1,0:T(8,128)(2,1)S(1)} %get-tuple-element.48), channel_id=1, replica_groups={{0,1,2,3,8,9,10,11,16,17,18,19,24,25,26,27,32,33,34,35,40,41,42,43,48,4..., dimensions={0} | all-to-all | bytes 131072 | tf_op jit(solution)/shard_map/all_to_all | solution.py:56
  89.6 0.7 shard_map.42
  90.3 7.9 %all_to_all.34.refs_0_ = f32[8,16,128]{2,1,0:T(8,128)S(1)} all-to-all(f32[8,16,128]{2,1,0:T(8,128)S(1)} %shard_map.42), channel_id=1, replica_groups={{0,4,64,68,128,132,192,196},{1,5,65,69,129,133,193,197},{2,6,66,70,130,..., dimensions={0} | all-to-all | bytes 131072 | tf_op jit(solution)/shard_map/all_to_all | solution.py:56
  98.2 0.7 shard_map.43
  98.9 14.1 %all_to_all.35.parts_ref = bf16[32,16,128]{2,1,0:T(8,128)(2,1)S(1)} all-to-all(bf16[32,16,128]{2,1,0:T(8,128)(2,1)S(1)} %get-tuple-element.50), channel_id=1, replica_groups={{0,1,2,3,8,9,10,11,16,17,18,19,24,25,26,27,32,33,34,35,40,41,42,43,48,4..., dimensions={0} | all-to-all | bytes 262144 | tf_op jit(solution)/shard_map/all_to_all | solution.py:56
  113.0 1.5 %shard_map.45 = bf16[2,512,256]{2,1,0:T(8,128)(2,1)S(1)} custom-call(s32[3]{0:T(128)S(1)} %pad_add_fusion.place_ref.refs_0_, bf16[32,16,128]{2,1,0:T(8,128)(2,1)S(1)} %all_to_all.35.parts_ref, f32[16,128]{1,0:T(8,128)S(1)} %get-tuple-element.51.scale_ref, f32[8,128]{1,0:T(8,128)S(1)} %get-tuple-element.52.weight_ref, ...), custom_call_target="tpu_custom_call" | custom-call | flops 536870912 | bytes 8388608 | tf_op jit(solution)/shard_map/pallas_call | solution.py:292
  114.5 0.0 copy-start
  114.5 0.1 collective-permute-start.16
  114.6 1.5 %shard_map.44 = f32[2,512,256]{2,1,0:T(8,128)S(1)} custom-call(s32[3]{0:T(128)S(1)} %pad_add_fusion.place_ref.refs_0_, bf16[32,16,128]{2,1,0:T(8,128)(2,1)S(1)} %all_to_all.35.parts_ref, f32[16,128]{1,0:T(8,128)S(1)} %get-tuple-element.51.scale_ref, f32[8,128]{1,0:T(8,128)S(1)} %get-tuple-element.52.weight_ref, ...), custom_call_target="tpu_custom_call" | custom-call | flops 536870912 | bytes 8388608 | tf_op jit(solution)/shard_map/pallas_call | solution.py:292
  116.1 0.4 collective-permute-done.16
  116.5 0.1 convert_add_fusion
  116.6 0.1 fusion
  116.7 1.3 collective-permute-start.18
  118.0 1.3 collective-permute-start.19
  119.3 2.9 %collective-permute-start.17 = (bf16[512,256]{1,0:T(8,128)(2,1)S(1)}, bf16[512,256]{1,0:T(8,128)(2,1)S(1)}, u32[]{:S(2)}, u32[]{:S(2)}) collective-permute-start(bf16[512,256]{1,0:T(8,128)(2,1)S(1)} %get-tuple-element.56), channel_id=1, source_target_pairs={{0,64},{1,65},{2,66},{3,67},{4,68},{5,69},{6,70},{7,71},{8,72},{9,... | collective-permute-start | bytes 786440 | tf_op jit(solution)/shard_map/ppermute | solution.py:69
  122.2 2.2 %collective-permute-done.18 = bf16[512,256]{1,0:T(8,128)(2,1)S(1)} collective-permute-done((bf16[512,256]{1,0:T(8,128)(2,1)S(1)}, bf16[512,256]{1,0:T(8,128)(2,1)S(1)}, u32[]{:S(2)}, u32[]{:S(2)}) %collective-permute-start.18) | collective-permute-done | bytes 262176 | tf_op jit(solution)/shard_map/ppermute | solution.py:69
  124.4 1.3 collective-permute-done.19
  125.7 4.2 %collective-permute-done.17 = bf16[512,256]{1,0:T(8,128)(2,1)S(1)} collective-permute-done((bf16[512,256]{1,0:T(8,128)(2,1)S(1)}, bf16[512,256]{1,0:T(8,128)(2,1)S(1)}, u32[]{:S(2)}, u32[]{:S(2)}) %collective-permute-start.17) | collective-permute-done | bytes 262176 | tf_op jit(solution)/shard_map/ppermute | solution.py:69
  129.8 1.0 select_bitcast_fusion
  (13 shorter events, 0.0 us)
Async XLA Ops:
  0.0 3.8 %collective-permute-start = (f32[512,256]{1,0:T(8,128)}, f32[512,256]{1,0:T(8,128)S(1)}, u32[]{:S(2)}, u32[]{:S(2)}) collective-permute-start(f32[512,256]{1,0:T(8,128)} %bitcast.17), channel_id=1, source_target_pairs={{0,128},{1,129},{2,130},{3,131},{4,132},{5,133},{6,134},{7,135},{8... | collective-permute-start | bytes 1572872 | tf_op jit(solution)/shard_map/ppermute | solution.py:317
  1.8 2.1 %collective-permute-start.1 = (bf16[512,256]{1,0:T(8,128)(2,1)}, bf16[512,256]{1,0:T(8,128)(2,1)S(1)}, u32[]{:S(2)}, u32[]{:S(2)}) collective-permute-start(bf16[512,256]{1,0:T(8,128)(2,1)} %bitcast.19), channel_id=1, source_target_pairs={{0,128},{128,0},{1,129},{129,1},{2,130},{130,2},{3,131},{131,3},{4... | collective-permute-start | bytes 786440 | tf_op jit(solution)/shard_map/ppermute | solution.py:60
  5.9 9.2 %collective-permute-start.5 = (bf16[256,256]{1,0:T(8,128)(2,1)S(1)}, bf16[256,256]{1,0:T(8,128)(2,1)S(1)}, u32[]{:S(2)}, u32[]{:S(2)}) collective-permute-start(bf16[256,256]{1,0:T(8,128)(2,1)S(1)} %get-tuple-element.32.refs_1_), channel_id=1, source_target_pairs={{0,56},{1,57},{2,58},{3,59},{4,60},{5,61},{6,62},{7,63},{8,0},{9,1... | collective-permute-start | bytes 393224 | tf_op jit(solution)/shard_map/ppermute | solution.py:69
  11.8 13.2 %collective-permute-start.2 = (bf16[512,256]{1,0:T(8,128)(2,1)S(1)}, bf16[512,256]{1,0:T(8,128)(2,1)S(1)}, u32[]{:S(2)}, u32[]{:S(2)}) collective-permute-start(bf16[512,256]{1,0:T(8,128)(2,1)S(1)} %get-tuple-element.30.refs_9_), channel_id=1, source_target_pairs={{0,68},{1,69},{2,70},{3,71},{4,0},{5,1},{6,2},{7,3},{8,76},{9,77},... | collective-permute-start | bytes 786440 | tf_op jit(solution)/shard_map/ppermute | solution.py:69
  12.4 7.9 %collective-permute-start.9 = (bf16[256,256]{1,0:T(8,128)(2,1)S(1)}, bf16[256,256]{1,0:T(8,128)(2,1)S(1)}, u32[]{:S(2)}, u32[]{:S(2)}) collective-permute-start(bf16[256,256]{1,0:T(8,128)(2,1)S(1)} %get-tuple-element.32.refs_1_), channel_id=1, source_target_pairs={{0,8},{1,9},{2,10},{3,11},{4,12},{5,13},{6,14},{7,15},{8,16},{9,17... | collective-permute-start | bytes 393224 | tf_op jit(solution)/shard_map/ppermute | solution.py:69
  15.1 6.2 %collective-permute-start.6 = (bf16[256,256]{1,0:T(8,128)(2,1)S(1)}, bf16[256,256]{1,0:T(8,128)(2,1)S(1)}, u32[]{:S(2)}, u32[]{:S(2)}) collective-permute-start(bf16[256,256]{1,0:T(8,128)(2,1)S(1)} %collective-permute-done.5.refs_2_), channel_id=1, source_target_pairs={{0,56},{1,57},{2,58},{3,59},{4,60},{5,61},{6,62},{7,63},{8,0},{9,1... | collective-permute-start | bytes 393224 | tf_op jit(solution)/shard_map/ppermute | solution.py:69
  18.8 12.4 %collective-permute-start.4 = (bf16[512,256]{1,0:T(8,128)(2,1)S(1)}, bf16[512,256]{1,0:T(8,128)(2,1)S(1)}, u32[]{:S(2)}, u32[]{:S(2)}) collective-permute-start(bf16[512,256]{1,0:T(8,128)(2,1)S(1)} %get-tuple-element.30.refs_9_), channel_id=1, source_target_pairs={{0,4},{1,5},{2,6},{3,7},{4,64},{5,65},{6,66},{7,67},{8,12},{9,13},... | collective-permute-start | bytes 786440 | tf_op jit(solution)/shard_map/ppermute | solution.py:69
  20.3 6.2 %collective-permute-start.10 = (bf16[256,256]{1,0:T(8,128)(2,1)S(1)}, bf16[256,256]{1,0:T(8,128)(2,1)S(1)}, u32[]{:S(2)}, u32[]{:S(2)}) collective-permute-start(bf16[256,256]{1,0:T(8,128)(2,1)S(1)} %collective-permute-done.9.refs_8_), channel_id=1, source_target_pairs={{0,8},{1,9},{2,10},{3,11},{4,12},{5,13},{6,14},{7,15},{8,16},{9,17... | collective-permute-start | bytes 393224 | tf_op jit(solution)/shard_map/ppermute | solution.py:69
  21.3 6.2 %collective-permute-start.7 = (bf16[256,256]{1,0:T(8,128)(2,1)S(1)}, bf16[256,256]{1,0:T(8,128)(2,1)S(1)}, u32[]{:S(2)}, u32[]{:S(2)}) collective-permute-start(bf16[256,256]{1,0:T(8,128)(2,1)S(1)} %collective-permute-done.6.refs_3_), channel_id=1, source_target_pairs={{0,56},{1,57},{2,58},{3,59},{4,60},{5,61},{6,62},{7,63},{8,0},{9,1... | collective-permute-start | bytes 393224 | tf_op jit(solution)/shard_map/ppermute | solution.py:69
  25.0 8.7 %collective-permute-start.3 = (bf16[512,256]{1,0:T(8,128)(2,1)S(1)}, bf16[512,256]{1,0:T(8,128)(2,1)S(1)}, u32[]{:S(2)}, u32[]{:S(2)}) collective-permute-start(bf16[512,256]{1,0:T(8,128)(2,1)S(1)} %collective-permute-done.2.refs_10_), channel_id=1, source_target_pairs={{0,68},{1,69},{2,70},{3,71},{4,0},{5,1},{6,2},{7,3},{8,76},{9,77},... | collective-permute-start | bytes 786440 | tf_op jit(solution)/shard_map/ppermute | solution.py:69
  26.5 6.2 %collective-permute-start.11 = (bf16[256,256]{1,0:T(8,128)(2,1)S(1)}, bf16[256,256]{1,0:T(8,128)(2,1)S(1)}, u32[]{:S(2)}, u32[]{:S(2)}) collective-permute-start(bf16[256,256]{1,0:T(8,128)(2,1)S(1)} %collective-permute-done.10.refs_7_), channel_id=1, source_target_pairs={{0,8},{1,9},{2,10},{3,11},{4,12},{5,13},{6,14},{7,15},{8,16},{9,17... | collective-permute-start | bytes 393224 | tf_op jit(solution)/shard_map/ppermute | solution.py:69
  27.5 6.2 %collective-permute-start.8 = (bf16[256,256]{1,0:T(8,128)(2,1)S(1)}, bf16[256,256]{1,0:T(8,128)(2,1)S(1)}, u32[]{:S(2)}, u32[]{:S(2)}) collective-permute-start(bf16[256,256]{1,0:T(8,128)(2,1)S(1)} %collective-permute-done.7.refs_4_), channel_id=1, source_target_pairs={{0,56},{1,57},{2,58},{3,59},{4,60},{5,61},{6,62},{7,63},{8,0},{9,1... | collective-permute-start | bytes 393224 | tf_op jit(solution)/shard_map/ppermute | solution.py:69
  31.2 3.0 %collective-permute-start.12 = (bf16[512,256]{1,0:T(8,128)(2,1)S(1)}, bf16[512,256]{1,0:T(8,128)(2,1)S(1)}, u32[]{:S(2)}, u32[]{:S(2)}) collective-permute-start(bf16[512,256]{1,0:T(8,128)(2,1)S(1)} %get-tuple-element.30.refs_9_), channel_id=1, source_target_pairs={{0,128},{128,0},{1,129},{129,1},{2,130},{130,2},{3,131},{131,3},{4... | collective-permute-start | bytes 786440 | tf_op jit(solution)/shard_map/ppermute | solution.py:60
  33.7 1.5 %collective-permute-start.13 = (bf16[512,256]{1,0:T(8,128)(2,1)S(1)}, bf16[512,256]{1,0:T(8,128)(2,1)S(1)}, u32[]{:S(2)}, u32[]{:S(2)}) collective-permute-start(bf16[512,256]{1,0:T(8,128)(2,1)S(1)} %collective-permute-done.2.refs_10_), channel_id=1, source_target_pairs={{0,128},{128,0},{1,129},{129,1},{2,130},{130,2},{3,131},{131,3},{4... | collective-permute-start | bytes 786440 | tf_op jit(solution)/shard_map/ppermute | solution.py:60
  33.7 1.9 %collective-permute-start.14 = (bf16[512,256]{1,0:T(8,128)(2,1)S(1)}, bf16[512,256]{1,0:T(8,128)(2,1)S(1)}, u32[]{:S(2)}, u32[]{:S(2)}) collective-permute-start(bf16[512,256]{1,0:T(8,128)(2,1)S(1)} %collective-permute-done.3.refs_11_), channel_id=1, source_target_pairs={{0,128},{128,0},{1,129},{129,1},{2,130},{130,2},{3,131},{131,3},{4... | collective-permute-start | bytes 786440 | tf_op jit(solution)/shard_map/ppermute | solution.py:60
  34.2 1.8 %collective-permute-start.15 = (bf16[512,256]{1,0:T(8,128)(2,1)S(1)}, bf16[512,256]{1,0:T(8,128)(2,1)S(1)}, u32[]{:S(2)}, u32[]{:S(2)}) collective-permute-start(bf16[512,256]{1,0:T(8,128)(2,1)S(1)} %collective-permute-done.4.refs_12_), channel_id=1, source_target_pairs={{0,128},{128,0},{1,129},{129,1},{2,130},{130,2},{3,131},{131,3},{4... | collective-permute-start | bytes 786440 | tf_op jit(solution)/shard_map/ppermute | solution.py:60
  114.5 15.3 %copy-start = (f32[1,512,256]{2,1,0:T(8,128)S(1)}, f32[1,512,256]{2,1,0:T(8,128)}, u32[]{:S(2)}) copy-start(f32[1,512,256]{2,1,0:T(8,128)} %param.4) | copy-start | bytes 1572868
  114.5 2.0 %collective-permute-start.16 = (bf16[2,512,256]{2,1,0:T(8,128)(2,1)S(1)}, bf16[2,512,256]{2,1,0:T(8,128)(2,1)S(1)}, u32[]{:S(2)}, u32[]{:S(2)}) collective-permute-start(bf16[2,512,256]{2,1,0:T(8,128)(2,1)S(1)} %shard_map.45), channel_id=1, source_target_pairs={{0,128},{128,0},{1,129},{129,1},{2,130},{130,2},{3,131},{131,3},{4... | collective-permute-start | bytes 1572872 | tf_op jit(solution)/shard_map/ppermute | solution.py:60
  116.7 7.7 %collective-permute-start.18 = (bf16[512,256]{1,0:T(8,128)(2,1)S(1)}, bf16[512,256]{1,0:T(8,128)(2,1)S(1)}, u32[]{:S(2)}, u32[]{:S(2)}) collective-permute-start(bf16[512,256]{1,0:T(8,128)(2,1)S(1)} %get-tuple-element.55), channel_id=1, source_target_pairs={{128,4},{129,5},{130,6},{131,7},{132,64},{133,65},{134,66},{135,67... | collective-permute-start | bytes 786440 | tf_op jit(solution)/shard_map/ppermute | solution.py:69
  118.0 7.7 %collective-permute-start.19 = (bf16[512,256]{1,0:T(8,128)(2,1)S(1)}, bf16[512,256]{1,0:T(8,128)(2,1)S(1)}, u32[]{:S(2)}, u32[]{:S(2)}) collective-permute-start(bf16[512,256]{1,0:T(8,128)(2,1)S(1)} %get-tuple-element.56), channel_id=1, source_target_pairs={{128,68},{129,69},{130,70},{131,71},{132,0},{133,1},{134,2},{135,3... | collective-permute-start | bytes 786440 | tf_op jit(solution)/shard_map/ppermute | solution.py:69
  119.3 10.5 %collective-permute-start.17 = (bf16[512,256]{1,0:T(8,128)(2,1)S(1)}, bf16[512,256]{1,0:T(8,128)(2,1)S(1)}, u32[]{:S(2)}, u32[]{:S(2)}) collective-permute-start(bf16[512,256]{1,0:T(8,128)(2,1)S(1)} %get-tuple-element.56), channel_id=1, source_target_pairs={{0,64},{1,65},{2,66},{3,67},{4,68},{5,69},{6,70},{7,71},{8,72},{9,... | collective-permute-start | bytes 786440 | tf_op jit(solution)/shard_map/ppermute | solution.py:69

commit v6 on v5

--- a/solution.py
+++ b/solution.py
@@ -115,6 +115,7 @@
     pack_ref,
     weight_ref,
     unit_ref,
+    other_unit_ref,
 ):
     grp, x = place_ref[0], place_ref[1]
 
@@ -132,10 +133,12 @@
         pack_ref[0:OWN_ROWS, :] = teacher
         pack_ref[OWN_ROWS:PACK, :] = student
 
-    own_master = own_ref[...]
-    blended = MOMENTUM * own_master + (1.0 - MOMENTUM) * other_ref[...]
-    master = jnp.where(grp == 1, blended, own_master)
-    unit_ref[...] = unit_rows(master)
+    own, other = own_ref[...], other_ref[...]
+    student = jnp.where(grp == 0, own, other)
+    blended = MOMENTUM * jnp.where(grp == 0, other, own) + (1.0 - MOMENTUM) * student
+    student, blended = unit_rows(student), unit_rows(blended)
+    unit_ref[...] = jnp.where(grp == 0, student, blended)
+    other_unit_ref[...] = jnp.where(grp == 0, blended, student)
 
 
 def in_hbm(array):
@@ -151,6 +154,7 @@
         out_shape=[
             shape((PACK, 256), jnp.bfloat16),
             shape((8, 128), jnp.bfloat16),
+            shape((BLOCK, 256), jnp.bfloat16),
             shape((BLOCK, 256), jnp.bfloat16),
         ],
         grid_spec=pltpu.PrefetchScalarGridSpec(
@@ -166,6 +170,7 @@
             out_specs=[
                 pl.BlockSpec((PACK, 256), lambda i, place: (0, 0)),
                 pl.BlockSpec((8, 128), lambda i, place: (0, 0)),
+                part,
                 part,
             ],
         ),
@@ -314,9 +319,9 @@
     work = COLS * ROWS
 
     own_master = masters[0]
-    other_master = lax.ppermute(own_master, "grp", [(0, 1)])
+    other_master = swapped(own_master)
     other_features = swapped(features[0])
-    pack, weight, unit = unit_call(
+    pack, weight, unit, other_unit = unit_call(
         place,
         features[0],
         other_features,
@@ -331,8 +336,9 @@
             packs[N_Z - k] = from_z(packs[(N_Z - k + 1) % N_Z], -1)
     own_units = [unit, from_x(unit, 1), None, from_x(unit, -1)]
     own_units[2] = from_x(own_units[1], 1)
-    held, packs = lax.optimization_barrier((tuple(own_units[1:]), packs))
-    other_units = [swapped(unit)] + [swapped(block) for block in held]
+    near, _ = lax.optimization_barrier(((own_units[1], own_units[3]), (packs[3], packs[5])))
+    far, packs = lax.optimization_barrier((own_units[2], packs))
+    other_units = [other_unit, swapped(near[0]), swapped(far), swapped(near[1])]
 
     teacher_exp, student_exp, col_parts, student_part, student_tokens = call(
         exp_kernel,

time: 131 us -> 129 us (0.985)
  starting transfers between devices: 27.5 us -> 26.1 us
    ppermute x1 -> x0, starting transfers between devices: 1.76 us -> none  [per_device(): other_master = lax.ppermute(own_master, 'grp', [(0, 1)])]
  transfers between devices with their start and end apart: 20 -> 19, of which waited for: 14 -> 11; matrix products, arithmetic and copies ran while one was open for 0% -> 0% of each run, Pallas kernels for 1% -> 1%
where the time goes in v6:
time: 129 us
  blocking collectives  70.1 us (54%)
  starting transfers between devices  26.1 us (20%)
  waiting for transfers between devices  19 us (15%)
  Pallas kernels  12 us (9%)
    all_to_all x6, blocking collectives, exchange(): lax.all_to_all(blocks, AXES, 0, 0, axis_index_groups=groups, tiled=True)  70.1 us
    ppermute x13, starting transfers between devices, permuted(): return lax.ppermute(block, AXES, route)  25 us
    ppermute x13, waiting for transfers between devices, permuted(): return lax.ppermute(block, AXES, route)  15.2 us
    pallas_call x8, Pallas kernels, call(): pl.pallas_call(kernel, out_shape=outs, in_specs=[smem if a.ndim == 1 else...  9.86 us
    ppermute x6, waiting for transfers between devices, swapped(): return lax.ppermute(block, 'grp', [(0, 1), (1, 0)])  3.83 us
  transfers between devices with their start and end apart: 19, of which 11 were waited for; matrix products, arithmetic and copies ran while one was open for 0% of the time, Pallas kernels for 1%

profile of v6, /device:TPU:2, one launch (start us, length us, event | category | flops | bytes accessed | tf_op | source)
XLA Modules:
  0.0 128.6 jit_solution(8400400119198176727)
XLA Ops:
  0.0 0.0 collective-permute-start
  0.0 0.5 collective-permute-start.1
  0.5 0.1 pad_add_fusion.place_ref.refs_0_
  0.6 1.9 %collective-permute-done.1.other_features_ref = bf16[512,256]{1,0:T(8,128)(2,1)S(1)} collective-permute-done((bf16[512,256]{1,0:T(8,128)(2,1)}, bf16[512,256]{1,0:T(8,128)(2,1)S(1)}, u32[]{:S(2)}, u32[]{:S(2)}) %collective-permute-start.1) | collective-permute-done | bytes 262176 | tf_op jit(solution)/shard_map/ppermute | solution.py:60
  2.5 2.2 %shard_map.37 = (bf16[256,256]{1,0:T(8,128)(2,1)S(1)}, bf16[8,128]{1,0:T(8,128)(2,1)S(1)}, bf16[512,256]{1,0:T(8,128)(2,1)S(1)}, bf16[512,256]{1,0:T(8,128)(2,1)S(1)}) custom-call(s32[3]{0:T(128)S(1)} %pad_add_fusion.place_ref.refs_0_, bf16[512,256]{1,0:T(8,128)(2,1)} %bitcast.20, bf16[512,256]{1,0:T(8,128)(2,1)S(1)} %collective-permute-done.1.other_features_ref, ...), custom_call_target="tpu_custom_call" | custom-call | tf_op jit(solution)/shard_map/pallas_call | solution.py:152
  4.7 5.9 %collective-permute-start.4 = (bf16[256,256]{1,0:T(8,128)(2,1)S(1)}, bf16[256,256]{1,0:T(8,128)(2,1)S(1)}, u32[]{:S(2)}, u32[]{:S(2)}) collective-permute-start(bf16[256,256]{1,0:T(8,128)(2,1)S(1)} %get-tuple-element.33.refs_1_), channel_id=1, source_target_pairs={{0,56},{1,57},{2,58},{3,59},{4,60},{5,61},{6,62},{7,63},{8,0},{9,1... | collective-permute-start | bytes 393224 | tf_op jit(solution)/shard_map/ppermute | solution.py:69
  10.6 0.5 collective-permute-start.2
  11.2 0.0 collective-permute-start.8
  11.2 2.5 %collective-permute-done.4.refs_2_ = bf16[256,256]{1,0:T(8,128)(2,1)S(1)} collective-permute-done((bf16[256,256]{1,0:T(8,128)(2,1)S(1)}, bf16[256,256]{1,0:T(8,128)(2,1)S(1)}, u32[]{:S(2)}, u32[]{:S(2)}) %collective-permute-start.4) | collective-permute-done | bytes 131104 | tf_op jit(solution)/shard_map/ppermute | solution.py:69
  13.7 3.7 %collective-permute-start.5 = (bf16[256,256]{1,0:T(8,128)(2,1)S(1)}, bf16[256,256]{1,0:T(8,128)(2,1)S(1)}, u32[]{:S(2)}, u32[]{:S(2)}) collective-permute-start(bf16[256,256]{1,0:T(8,128)(2,1)S(1)} %collective-permute-done.4.refs_2_), channel_id=1, source_target_pairs={{0,56},{1,57},{2,58},{3,59},{4,60},{5,61},{6,62},{7,63},{8,0},{9,1... | collective-permute-start | bytes 393224 | tf_op jit(solution)/shard_map/ppermute | solution.py:69
  17.4 1.5 %collective-permute-start.11 = (bf16[512,256]{1,0:T(8,128)(2,1)S(1)}, bf16[512,256]{1,0:T(8,128)(2,1)S(1)}, u32[]{:S(2)}, u32[]{:S(2)}) collective-permute-start(bf16[512,256]{1,0:T(8,128)(2,1)S(1)} %get-tuple-element.31.refs_9_), channel_id=1, source_target_pairs={{0,4},{1,5},{2,6},{3,7},{4,64},{5,65},{6,66},{7,67},{8,12},{9,13},... | collective-permute-start | bytes 786440 | tf_op jit(solution)/shard_map/ppermute | solution.py:69
  18.9 1.0 collective-permute-done.5.refs_3_
  19.9 3.7 %collective-permute-start.6 = (bf16[256,256]{1,0:T(8,128)(2,1)S(1)}, bf16[256,256]{1,0:T(8,128)(2,1)S(1)}, u32[]{:S(2)}, u32[]{:S(2)}) collective-permute-start(bf16[256,256]{1,0:T(8,128)(2,1)S(1)} %collective-permute-done.5.refs_3_), channel_id=1, source_target_pairs={{0,56},{1,57},{2,58},{3,59},{4,60},{5,61},{6,62},{7,63},{8,0},{9,1... | collective-permute-start | bytes 393224 | tf_op jit(solution)/shard_map/ppermute | solution.py:69
  23.6 0.0 collective-permute-done.2.refs_10_
  23.6 0.5 collective-permute-start.3
  24.1 2.0 %collective-permute-done.6.refs_4_ = bf16[256,256]{1,0:T(8,128)(2,1)S(1)} collective-permute-done((bf16[256,256]{1,0:T(8,128)(2,1)S(1)}, bf16[256,256]{1,0:T(8,128)(2,1)S(1)}, u32[]{:S(2)}, u32[]{:S(2)}) %collective-permute-start.6) | collective-permute-done | bytes 131104 | tf_op jit(solution)/shard_map/ppermute | solution.py:69
  26.1 3.7 %collective-permute-start.7 = (bf16[256,256]{1,0:T(8,128)(2,1)S(1)}, bf16[256,256]{1,0:T(8,128)(2,1)S(1)}, u32[]{:S(2)}, u32[]{:S(2)}) collective-permute-start(bf16[256,256]{1,0:T(8,128)(2,1)S(1)} %collective-permute-done.6.refs_4_), channel_id=1, source_target_pairs={{0,56},{1,57},{2,58},{3,59},{4,60},{5,61},{6,62},{7,63},{8,0},{9,1... | collective-permute-start | bytes 393224 | tf_op jit(solution)/shard_map/ppermute | solution.py:69
  29.7 0.5 collective-permute-done.10.refs_6_
  30.3 0.5 collective-permute-start.14
  30.8 1.5 %collective-permute-done.7.refs_5_ = bf16[256,256]{1,0:T(8,128)(2,1)S(1)} collective-permute-done((bf16[256,256]{1,0:T(8,128)(2,1)S(1)}, bf16[256,256]{1,0:T(8,128)(2,1)S(1)}, u32[]{:S(2)}, u32[]{:S(2)}) %collective-permute-start.7) | collective-permute-done | bytes 131104 | tf_op jit(solution)/shard_map/ppermute | solution.py:69
  32.3 0.0 collective-permute-start.13
  32.3 1.5 %collective-permute-done.13.refs_15_ = bf16[512,256]{1,0:T(8,128)(2,1)S(1)} collective-permute-done((bf16[512,256]{1,0:T(8,128)(2,1)S(1)}, bf16[512,256]{1,0:T(8,128)(2,1)S(1)}, u32[]{:S(2)}, u32[]{:S(2)}) %collective-permute-start.13) | collective-permute-done | bytes 262176 | tf_op jit(solution)/shard_map/ppermute | solution.py:60
  33.8 3.1 %shard_map.38 = (f32[2048,1024]{1,0:T(8,128)S(1)}, f32[2048,1024]{1,0:T(8,128)S(1)}, f32[8,16,128]{2,1,0:T(8,128)S(1)}, f32[8,128]{1,0:T(8,128)S(1)}, bf16[1024,256]{1,0:T(8,128)(2,1)S(1)}) custom-call(s32[3]{0:T(128)S(1)} %pad_add_fusion.place_ref.refs_0_, bf16[256,256]{1,0:T(8,128)(2,1)S(1)} %get-tuple-element.33.refs_1_, ...), custom_call_target="tpu_custom_call" | custom-call | flops 2147483648 | bytes 8388608 | tf_op jit(solution)/shard_map/pallas_call | solution.py:297
  36.9 8.7 %all_to_all.30.refs_0_ = f32[8,16,128]{2,1,0:T(8,128)S(1)} all-to-all(f32[8,16,128]{2,1,0:T(8,128)S(1)} %get-tuple-element.45), channel_id=1, replica_groups={{0,4,64,68,128,132,192,196},{1,5,65,69,129,133,193,197},{2,6,66,70,130,..., dimensions={0} | all-to-all | bytes 131072 | tf_op jit(solution)/shard_map/all_to_all | solution.py:56
  45.6 0.8 shard_map.39
  46.4 18.5 %all_to_all.31.refs_0_ = bf16[32,16,128]{2,1,0:T(8,128)(2,1)S(1)} all-to-all(bf16[32,16,128]{2,1,0:T(8,128)(2,1)S(1)} %get-tuple-element.48), channel_id=1, replica_groups={{0,1,2,3,8,9,10,11,16,17,18,19,24,25,26,27,32,33,34,35,40,41,42,43,48,4..., dimensions={0} | all-to-all | bytes 262144 | tf_op jit(solution)/shard_map/all_to_all | solution.py:56
  65.0 0.7 shard_map.40
  65.7 7.7 %all_to_all.32.refs_0_ = f32[8,16,128]{2,1,0:T(8,128)S(1)} all-to-all(f32[8,16,128]{2,1,0:T(8,128)S(1)} %get-tuple-element.49), channel_id=1, replica_groups={{0,4,64,68,128,132,192,196},{1,5,65,69,129,133,193,197},{2,6,66,70,130,..., dimensions={0} | all-to-all | bytes 131072 | tf_op jit(solution)/shard_map/all_to_all | solution.py:56
  73.4 0.8 shard_map.41
  74.2 13.2 %all_to_all.33.refs_0_ = bf16[32,8,128]{2,1,0:T(8,128)(2,1)S(1)} all-to-all(bf16[32,8,128]{2,1,0:T(8,128)(2,1)S(1)} %get-tuple-element.50), channel_id=1, replica_groups={{0,1,2,3,8,9,10,11,16,17,18,19,24,25,26,27,32,33,34,35,40,41,42,43,48,4..., dimensions={0} | all-to-all | bytes 131072 | tf_op jit(solution)/shard_map/all_to_all | solution.py:56
  87.5 0.7 shard_map.42
  88.2 7.9 %all_to_all.34.refs_0_ = f32[8,16,128]{2,1,0:T(8,128)S(1)} all-to-all(f32[8,16,128]{2,1,0:T(8,128)S(1)} %shard_map.42), channel_id=1, replica_groups={{0,4,64,68,128,132,192,196},{1,5,65,69,129,133,193,197},{2,6,66,70,130,..., dimensions={0} | all-to-all | bytes 131072 | tf_op jit(solution)/shard_map/all_to_all | solution.py:56
  96.0 0.7 shard_map.43
  96.7 14.1 %all_to_all.35.parts_ref = bf16[32,16,128]{2,1,0:T(8,128)(2,1)S(1)} all-to-all(bf16[32,16,128]{2,1,0:T(8,128)(2,1)S(1)} %get-tuple-element.52), channel_id=1, replica_groups={{0,1,2,3,8,9,10,11,16,17,18,19,24,25,26,27,32,33,34,35,40,41,42,43,48,4..., dimensions={0} | all-to-all | bytes 262144 | tf_op jit(solution)/shard_map/all_to_all | solution.py:56
  110.8 1.5 %shard_map.45 = bf16[2,512,256]{2,1,0:T(8,128)(2,1)S(1)} custom-call(s32[3]{0:T(128)S(1)} %pad_add_fusion.place_ref.refs_0_, bf16[32,16,128]{2,1,0:T(8,128)(2,1)S(1)} %all_to_all.35.parts_ref, f32[16,128]{1,0:T(8,128)S(1)} %get-tuple-element.53.scale_ref, f32[8,128]{1,0:T(8,128)S(1)} %get-tuple-element.54.weight_ref, ...), custom_call_target="tpu_custom_call" | custom-call | flops 536870912 | bytes 8388608 | tf_op jit(solution)/shard_map/pallas_call | solution.py:297
  112.3 0.0 copy-start
  112.3 0.1 collective-permute-start.15
  112.4 1.5 %shard_map.44 = f32[2,512,256]{2,1,0:T(8,128)S(1)} custom-call(s32[3]{0:T(128)S(1)} %pad_add_fusion.place_ref.refs_0_, bf16[32,16,128]{2,1,0:T(8,128)(2,1)S(1)} %all_to_all.35.parts_ref, f32[16,128]{1,0:T(8,128)S(1)} %get-tuple-element.53.scale_ref, f32[8,128]{1,0:T(8,128)S(1)} %get-tuple-element.54.weight_ref, ...), custom_call_target="tpu_custom_call" | custom-call | flops 536870912 | bytes 8388608 | tf_op jit(solution)/shard_map/pallas_call | solution.py:297
  113.9 0.4 collective-permute-done.15
  114.3 0.1 convert_add_fusion
  114.4 0.1 fusion
  114.5 1.3 %collective-permute-start.17 = (bf16[512,256]{1,0:T(8,128)(2,1)S(1)}, bf16[512,256]{1,0:T(8,128)(2,1)S(1)}, u32[]{:S(2)}, u32[]{:S(2)}) collective-permute-start(bf16[512,256]{1,0:T(8,128)(2,1)S(1)} %get-tuple-element.57), channel_id=1, source_target_pairs={{128,4},{129,5},{130,6},{131,7},{132,64},{133,65},{134,66},{135,67... | collective-permute-start | bytes 786440 | tf_op jit(solution)/shard_map/ppermute | solution.py:69
  115.8 1.3 %collective-permute-start.18 = (bf16[512,256]{1,0:T(8,128)(2,1)S(1)}, bf16[512,256]{1,0:T(8,128)(2,1)S(1)}, u32[]{:S(2)}, u32[]{:S(2)}) collective-permute-start(bf16[512,256]{1,0:T(8,128)(2,1)S(1)} %get-tuple-element.58), channel_id=1, source_target_pairs={{128,68},{129,69},{130,70},{131,71},{132,0},{133,1},{134,2},{135,3... | collective-permute-start | bytes 786440 | tf_op jit(solution)/shard_map/ppermute | solution.py:69
  117.1 2.9 %collective-permute-start.16 = (bf16[512,256]{1,0:T(8,128)(2,1)S(1)}, bf16[512,256]{1,0:T(8,128)(2,1)S(1)}, u32[]{:S(2)}, u32[]{:S(2)}) collective-permute-start(bf16[512,256]{1,0:T(8,128)(2,1)S(1)} %get-tuple-element.58), channel_id=1, source_target_pairs={{0,64},{1,65},{2,66},{3,67},{4,68},{5,69},{6,70},{7,71},{8,72},{9,... | collective-permute-start | bytes 786440 | tf_op jit(solution)/shard_map/ppermute | solution.py:69
  120.0 2.2 %collective-permute-done.17 = bf16[512,256]{1,0:T(8,128)(2,1)S(1)} collective-permute-done((bf16[512,256]{1,0:T(8,128)(2,1)S(1)}, bf16[512,256]{1,0:T(8,128)(2,1)S(1)}, u32[]{:S(2)}, u32[]{:S(2)}) %collective-permute-start.17) | collective-permute-done | bytes 262176 | tf_op jit(solution)/shard_map/ppermute | solution.py:69
  122.2 1.3 %collective-permute-done.18 = bf16[512,256]{1,0:T(8,128)(2,1)S(1)} collective-permute-done((bf16[512,256]{1,0:T(8,128)(2,1)S(1)}, bf16[512,256]{1,0:T(8,128)(2,1)S(1)}, u32[]{:S(2)}, u32[]{:S(2)}) %collective-permute-start.18) | collective-permute-done | bytes 262176 | tf_op jit(solution)/shard_map/ppermute | solution.py:69
  123.5 4.2 %collective-permute-done.16 = bf16[512,256]{1,0:T(8,128)(2,1)S(1)} collective-permute-done((bf16[512,256]{1,0:T(8,128)(2,1)S(1)}, bf16[512,256]{1,0:T(8,128)(2,1)S(1)}, u32[]{:S(2)}, u32[]{:S(2)}) %collective-permute-start.16) | collective-permute-done | bytes 262176 | tf_op jit(solution)/shard_map/ppermute | solution.py:69
  127.6 1.0 select_bitcast_fusion
  (11 shorter events, 0.0 us)
Async XLA Ops:
  0.0 2.5 %collective-permute-start = (f32[512,256]{1,0:T(8,128)}, f32[512,256]{1,0:T(8,128)S(1)}, u32[]{:S(2)}, u32[]{:S(2)}) collective-permute-start(f32[512,256]{1,0:T(8,128)} %bitcast.17), channel_id=1, source_target_pairs={{0,128},{128,0},{1,129},{129,1},{2,130},{130,2},{3,131},{131,3},{4... | collective-permute-start | bytes 1572872 | tf_op jit(solution)/shard_map/ppermute | solution.py:60
  0.0 2.5 %collective-permute-start.1 = (bf16[512,256]{1,0:T(8,128)(2,1)}, bf16[512,256]{1,0:T(8,128)(2,1)S(1)}, u32[]{:S(2)}, u32[]{:S(2)}) collective-permute-start(bf16[512,256]{1,0:T(8,128)(2,1)} %bitcast.19), channel_id=1, source_target_pairs={{0,128},{128,0},{1,129},{129,1},{2,130},{130,2},{3,131},{131,3},{4... | collective-permute-start | bytes 786440 | tf_op jit(solution)/shard_map/ppermute | solution.py:60
  4.7 9.0 %collective-permute-start.4 = (bf16[256,256]{1,0:T(8,128)(2,1)S(1)}, bf16[256,256]{1,0:T(8,128)(2,1)S(1)}, u32[]{:S(2)}, u32[]{:S(2)}) collective-permute-start(bf16[256,256]{1,0:T(8,128)(2,1)S(1)} %get-tuple-element.33.refs_1_), channel_id=1, source_target_pairs={{0,56},{1,57},{2,58},{3,59},{4,60},{5,61},{6,62},{7,63},{8,0},{9,1... | collective-permute-start | bytes 393224 | tf_op jit(solution)/shard_map/ppermute | solution.py:69
  10.6 12.9 %collective-permute-start.2 = (bf16[512,256]{1,0:T(8,128)(2,1)S(1)}, bf16[512,256]{1,0:T(8,128)(2,1)S(1)}, u32[]{:S(2)}, u32[]{:S(2)}) collective-permute-start(bf16[512,256]{1,0:T(8,128)(2,1)S(1)} %get-tuple-element.31.refs_9_), channel_id=1, source_target_pairs={{0,68},{1,69},{2,70},{3,71},{4,0},{5,1},{6,2},{7,3},{8,76},{9,77},... | collective-permute-start | bytes 786440 | tf_op jit(solution)/shard_map/ppermute | solution.py:69
  11.2 6.2 %collective-permute-start.8 = (bf16[256,256]{1,0:T(8,128)(2,1)S(1)}, bf16[256,256]{1,0:T(8,128)(2,1)S(1)}, u32[]{:S(2)}, u32[]{:S(2)}) collective-permute-start(bf16[256,256]{1,0:T(8,128)(2,1)S(1)} %get-tuple-element.33.refs_1_), channel_id=1, source_target_pairs={{0,8},{1,9},{2,10},{3,11},{4,12},{5,13},{6,14},{7,15},{8,16},{9,17... | collective-permute-start | bytes 393224 | tf_op jit(solution)/shard_map/ppermute | solution.py:69
  13.7 6.2 %collective-permute-start.5 = (bf16[256,256]{1,0:T(8,128)(2,1)S(1)}, bf16[256,256]{1,0:T(8,128)(2,1)S(1)}, u32[]{:S(2)}, u32[]{:S(2)}) collective-permute-start(bf16[256,256]{1,0:T(8,128)(2,1)S(1)} %collective-permute-done.4.refs_2_), channel_id=1, source_target_pairs={{0,56},{1,57},{2,58},{3,59},{4,60},{5,61},{6,62},{7,63},{8,0},{9,1... | collective-permute-start | bytes 393224 | tf_op jit(solution)/shard_map/ppermute | solution.py:69
  17.4 6.7 %collective-permute-start.9 = (bf16[256,256]{1,0:T(8,128)(2,1)S(1)}, bf16[256,256]{1,0:T(8,128)(2,1)S(1)}, u32[]{:S(2)}, u32[]{:S(2)}) collective-permute-start(bf16[256,256]{1,0:T(8,128)(2,1)S(1)} %collective-permute-done.8.refs_8_), channel_id=1, source_target_pairs={{0,8},{1,9},{2,10},{3,11},{4,12},{5,13},{6,14},{7,15},{8,16},{9,17... | collective-permute-start | bytes 393224 | tf_op jit(solution)/shard_map/ppermute | solution.py:69
  17.4 12.4 %collective-permute-start.11 = (bf16[512,256]{1,0:T(8,128)(2,1)S(1)}, bf16[512,256]{1,0:T(8,128)(2,1)S(1)}, u32[]{:S(2)}, u32[]{:S(2)}) collective-permute-start(bf16[512,256]{1,0:T(8,128)(2,1)S(1)} %get-tuple-element.31.refs_9_), channel_id=1, source_target_pairs={{0,4},{1,5},{2,6},{3,7},{4,64},{5,65},{6,66},{7,67},{8,12},{9,13},... | collective-permute-start | bytes 786440 | tf_op jit(solution)/shard_map/ppermute | solution.py:69
  19.9 6.2 %collective-permute-start.6 = (bf16[256,256]{1,0:T(8,128)(2,1)S(1)}, bf16[256,256]{1,0:T(8,128)(2,1)S(1)}, u32[]{:S(2)}, u32[]{:S(2)}) collective-permute-start(bf16[256,256]{1,0:T(8,128)(2,1)S(1)} %collective-permute-done.5.refs_3_), channel_id=1, source_target_pairs={{0,56},{1,57},{2,58},{3,59},{4,60},{5,61},{6,62},{7,63},{8,0},{9,1... | collective-permute-start | bytes 393224 | tf_op jit(solution)/shard_map/ppermute | solution.py:69
  23.6 8.7 %collective-permute-start.3 = (bf16[512,256]{1,0:T(8,128)(2,1)S(1)}, bf16[512,256]{1,0:T(8,128)(2,1)S(1)}, u32[]{:S(2)}, u32[]{:S(2)}) collective-permute-start(bf16[512,256]{1,0:T(8,128)(2,1)S(1)} %collective-permute-done.2.refs_10_), channel_id=1, source_target_pairs={{0,68},{1,69},{2,70},{3,71},{4,0},{5,1},{6,2},{7,3},{8,76},{9,77},... | collective-permute-start | bytes 786440 | tf_op jit(solution)/shard_map/ppermute | solution.py:69
  24.1 6.2 %collective-permute-start.10 = (bf16[256,256]{1,0:T(8,128)(2,1)S(1)}, bf16[256,256]{1,0:T(8,128)(2,1)S(1)}, u32[]{:S(2)}, u32[]{:S(2)}) collective-permute-start(bf16[256,256]{1,0:T(8,128)(2,1)S(1)} %collective-permute-done.9.refs_7_), channel_id=1, source_target_pairs={{0,8},{1,9},{2,10},{3,11},{4,12},{5,13},{6,14},{7,15},{8,16},{9,17... | collective-permute-start | bytes 393224 | tf_op jit(solution)/shard_map/ppermute | solution.py:69
  26.1 6.2 %collective-permute-start.7 = (bf16[256,256]{1,0:T(8,128)(2,1)S(1)}, bf16[256,256]{1,0:T(8,128)(2,1)S(1)}, u32[]{:S(2)}, u32[]{:S(2)}) collective-permute-start(bf16[256,256]{1,0:T(8,128)(2,1)S(1)} %collective-permute-done.6.refs_4_), channel_id=1, source_target_pairs={{0,56},{1,57},{2,58},{3,59},{4,60},{5,61},{6,62},{7,63},{8,0},{9,1... | collective-permute-start | bytes 393224 | tf_op jit(solution)/shard_map/ppermute | solution.py:69
  30.3 2.0 %collective-permute-start.12 = (bf16[512,256]{1,0:T(8,128)(2,1)S(1)}, bf16[512,256]{1,0:T(8,128)(2,1)S(1)}, u32[]{:S(2)}, u32[]{:S(2)}) collective-permute-start(bf16[512,256]{1,0:T(8,128)(2,1)S(1)} %collective-permute-done.2.refs_10_), channel_id=1, source_target_pairs={{0,128},{128,0},{1,129},{129,1},{2,130},{130,2},{3,131},{131,3},{4... | collective-permute-start | bytes 786440 | tf_op jit(solution)/shard_map/ppermute | solution.py:60
  30.3 2.0 %collective-permute-start.14 = (bf16[512,256]{1,0:T(8,128)(2,1)S(1)}, bf16[512,256]{1,0:T(8,128)(2,1)S(1)}, u32[]{:S(2)}, u32[]{:S(2)}) collective-permute-start(bf16[512,256]{1,0:T(8,128)(2,1)S(1)} %collective-permute-done.11.refs_12_), channel_id=1, source_target_pairs={{0,128},{128,0},{1,129},{129,1},{2,130},{130,2},{3,131},{131,3},{4... | collective-permute-start | bytes 786440 | tf_op jit(solution)/shard_map/ppermute | solution.py:60
  32.3 1.5 %collective-permute-start.13 = (bf16[512,256]{1,0:T(8,128)(2,1)S(1)}, bf16[512,256]{1,0:T(8,128)(2,1)S(1)}, u32[]{:S(2)}, u32[]{:S(2)}) collective-permute-start(bf16[512,256]{1,0:T(8,128)(2,1)S(1)} %collective-permute-done.3.refs_11_), channel_id=1, source_target_pairs={{0,128},{128,0},{1,129},{129,1},{2,130},{130,2},{3,131},{131,3},{4... | collective-permute-start | bytes 786440 | tf_op jit(solution)/shard_map/ppermute | solution.py:60
  112.3 15.3 %copy-start = (f32[1,512,256]{2,1,0:T(8,128)S(1)}, f32[1,512,256]{2,1,0:T(8,128)}, u32[]{:S(2)}) copy-start(f32[1,512,256]{2,1,0:T(8,128)} %param.4) | copy-start | bytes 1572868
  112.3 2.0 %collective-permute-start.15 = (bf16[2,512,256]{2,1,0:T(8,128)(2,1)S(1)}, bf16[2,512,256]{2,1,0:T(8,128)(2,1)S(1)}, u32[]{:S(2)}, u32[]{:S(2)}) collective-permute-start(bf16[2,512,256]{2,1,0:T(8,128)(2,1)S(1)} %shard_map.45), channel_id=1, source_target_pairs={{0,128},{128,0},{1,129},{129,1},{2,130},{130,2},{3,131},{131,3},{4... | collective-permute-start | bytes 1572872 | tf_op jit(solution)/shard_map/ppermute | solution.py:60
  114.5 7.7 %collective-permute-start.17 = (bf16[512,256]{1,0:T(8,128)(2,1)S(1)}, bf16[512,256]{1,0:T(8,128)(2,1)S(1)}, u32[]{:S(2)}, u32[]{:S(2)}) collective-permute-start(bf16[512,256]{1,0:T(8,128)(2,1)S(1)} %get-tuple-element.57), channel_id=1, source_target_pairs={{128,4},{129,5},{130,6},{131,7},{132,64},{133,65},{134,66},{135,67... | collective-permute-start | bytes 786440 | tf_op jit(solution)/shard_map/ppermute | solution.py:69
  115.8 7.7 %collective-permute-start.18 = (bf16[512,256]{1,0:T(8,128)(2,1)S(1)}, bf16[512,256]{1,0:T(8,128)(2,1)S(1)}, u32[]{:S(2)}, u32[]{:S(2)}) collective-permute-start(bf16[512,256]{1,0:T(8,128)(2,1)S(1)} %get-tuple-element.58), channel_id=1, source_target_pairs={{128,68},{129,69},{130,70},{131,71},{132,0},{133,1},{134,2},{135,3... | collective-permute-start | bytes 786440 | tf_op jit(solution)/shard_map/ppermute | solution.py:69
  117.1 10.5 %collective-permute-start.16 = (bf16[512,256]{1,0:T(8,128)(2,1)S(1)}, bf16[512,256]{1,0:T(8,128)(2,1)S(1)}, u32[]{:S(2)}, u32[]{:S(2)}) collective-permute-start(bf16[512,256]{1,0:T(8,128)(2,1)S(1)} %get-tuple-element.58), channel_id=1, source_target_pairs={{0,64},{1,65},{2,66},{3,67},{4,68},{5,69},{6,70},{7,71},{8,72},{9,... | collective-permute-start | bytes 786440 | tf_op jit(solution)/shard_map/ppermute | solution.py:69

commit v7 on v6

--- a/solution.py
+++ b/solution.py
@@ -20,6 +20,7 @@
 N_X, N_Y, N_Z = 4, 4, 8
 BLOCK = 512
 HALF = 256
+STEP = 512
 OWN_ROWS = 128
 PACK = 2 * OWN_ROWS
 ROWS = N_Z * OWN_ROWS
@@ -185,39 +186,56 @@
     return jnp.exp2(logits * (LOG2E / temperature))
 
 
-def exp_kernel(*refs):
-    place_ref, pack_refs = refs[0], refs[1:9]
-    own_refs, other_refs = refs[9:13], refs[13:17]
-    teacher_ref, student_ref, parts_ref, total_ref, token_ref = refs[17:22]
-    scratch_ref, vector_ref = refs[22:]
+def exp_kernel(chunks, resumed, *refs):
+    place_ref, pack_refs = refs[0], refs[1 : 1 + len(chunks)]
+    refs = refs[1 + len(chunks) :]
+    own_refs, other_refs, refs = refs[0:4], refs[4:8], refs[8:]
+    if resumed:
+        sums_ref, refs = refs[0], refs[5:]
+    parts_ref, teacher_ref, student_ref, total_ref, token_ref, scratch_ref = refs
     grp, x, z = place_ref[0], place_ref[1], place_ref[2]
-    for k in range(N_Z):
-        rows = pl.ds(pl.multiple_of((z + k) % N_Z * OWN_ROWS, OWN_ROWS), OWN_ROWS)
-        scratch_ref[rows, :] = pack_refs[k][0:OWN_ROWS, :]
-        token_ref[rows, :] = pack_refs[k][OWN_ROWS:PACK, :]
-    teacher_tokens = scratch_ref[...]
-    student_tokens = token_ref[...]
-    total = jnp.zeros((8, ROWS), jnp.float32)
+    places = [(z + k) % N_Z for k in chunks]
+    pairs = range(len(chunks) // 2)
+    for n, place in enumerate(places):
+        scratch_ref[n * OWN_ROWS : (n + 1) * OWN_ROWS, :] = pack_refs[n][0:OWN_ROWS, :]
+        rows = pl.ds(pl.multiple_of(place * OWN_ROWS, OWN_ROWS), OWN_ROWS)
+        token_ref[rows, :] = pack_refs[n][OWN_ROWS:PACK, :]
+    totals = [jnp.zeros((8, 128), jnp.float32) for _ in chunks]
     for k in range(N_X):
         base = (x + k) % N_X * BLOCK
-        for i in range(BLOCK // 256):
-            block = slice(i * 256, (i + 1) * 256)
-            rows = pl.ds(pl.multiple_of(base + i * 256, 256), 256)
+        for i in range(BLOCK // STEP):
+            block = slice(i * STEP, (i + 1) * STEP)
+            rows = pl.ds(pl.multiple_of(base + i * STEP, STEP), STEP)
             own, other = own_refs[k][block, :], other_refs[k][block, :]
-            values = exp_of(jnp.where(grp == 0, other, own), teacher_tokens, TEACHER_TEMP)
-            teacher_ref[rows, :] = values
-            folded = sum(values[:, k * 128 : (k + 1) * 128] for k in range(8))
+            teacher, student = jnp.where(grp == 0, other, own), jnp.where(grp == 0, own, other)
+            folded = jnp.zeros((STEP, 128), jnp.float32)
+            for p in pairs:
+                tokens = scratch_ref[p * 256 : (p + 1) * 256, :]
+                values = exp_of(teacher, tokens, TEACHER_TEMP)
+                tokens = jnp.concatenate(
+                    [pack_refs[2 * p + h][OWN_ROWS:PACK, :] for h in range(2)], axis=0
+                )
+                others = exp_of(student, tokens, STUDENT_TEMP)
+                for h in range(2):
+                    n = 2 * p + h
+                    half = values[:, h * 128 : (h + 1) * 128]
+                    teacher_ref[places[n], rows, :] = half
+                    folded += half
+                    half = others[:, h * 128 : (h + 1) * 128]
+                    student_ref[places[n], rows, :] = half
+                    totals[n] += jnp.sum(half.reshape(STEP // 8, 8, 128), axis=0)
             column = jnp.sum(folded, axis=1, keepdims=True)
-            for h in range(2):
-                vector_ref[pl.ds(base // 128 + i * 2 + h, 1), :] = to_row(
-                    column[h * 128 : (h + 1) * 128]
-                )
-            values = exp_of(jnp.where(grp == 0, own, other), student_tokens, STUDENT_TEMP)
-            student_ref[rows, :] = values
-            total += jnp.sum(values.reshape(32, 8, ROWS), axis=0)
-    total_ref[...] = pieces_of(jnp.sum(total, axis=0, keepdims=True))
-    for k in range(N_COLGRP):
-        parts_ref[k] = vector_ref[...]
+            for h in range(STEP // 128):
+                line = pl.ds(base // 128 + i * (STEP // 128) + h, 1)
+                sums = to_row(column[h * 128 : (h + 1) * 128])
+                if resumed:
+                    sums += sums_ref[line, :]
+                    for target in range(N_COLGRP):
+                        parts_ref[target, line, :] = sums
+                else:
+                    parts_ref[line, :] = sums
+    for n, place in enumerate(places):
+        total_ref[pl.ds(place, 1), :] = jnp.sum(totals[n], axis=0, keepdims=True)
 
 
 def row_kernel(with_extra, *refs):
@@ -227,11 +245,13 @@
         parts_ref, exp_ref, out_ref, scale_ref = refs
     scale = 1.0 / jnp.sum(parts_ref[...], axis=0)
     scale_ref[...] = scale
-    total = jnp.zeros((8, ROWS), jnp.float32)
+    totals = [jnp.zeros((8, 128), jnp.float32) for _ in range(N_Z)]
     for j in range(COLS // 128):
-        weighted = exp_ref[j * 128 : (j + 1) * 128, :] * to_column(scale[j : j + 1, :])
-        total += jnp.sum(weighted.reshape(16, 8, ROWS), axis=0)
-    mine = pieces_of(jnp.sum(total, axis=0, keepdims=True))
+        column = to_column(scale[j : j + 1, :])
+        for k in range(N_Z):
+            weighted = exp_ref[k, j * 128 : (j + 1) * 128, :] * column
+            totals[k] += jnp.sum(weighted.reshape(16, 8, 128), axis=0)
+    mine = jnp.concatenate([jnp.sum(t, axis=0, keepdims=True) for t in totals], axis=0)
     if with_extra:
         mine = jnp.concatenate([mine, extra_ref[...].astype(jnp.float32)], axis=0)
     mine = mine.astype(jnp.bfloat16)
@@ -247,10 +267,10 @@
             weight_ref[z : z + 1, :] = extra[0:1, :]
     else:
         parts_ref, exp_ref, out_ref, vector_ref = refs
-    row = lanes(1.0 / jnp.sum(parts_ref[:, 0:8, :].astype(jnp.float32), axis=0))
+    scale = 1.0 / jnp.sum(parts_ref[:, 0:8, :].astype(jnp.float32), axis=0)
     for j in range(COLS // 128):
-        weighted = exp_ref[j * 128 : (j + 1) * 128, :] * row
-        folded = sum(weighted[:, k * 128 : (k + 1) * 128] for k in range(8))
+        rows = slice(j * 128, (j + 1) * 128)
+        folded = sum(exp_ref[k, rows, :] * scale[k : k + 1, :] for k in range(N_Z))
         vector_ref[j : j + 1, :] = to_row(jnp.sum(folded, axis=1, keepdims=True))
     for k in range(N_COLGRP):
         out_ref[k] = vector_ref[...]
@@ -269,9 +289,8 @@
     out_ref,
 ):
     inverse = 1.0 / jnp.sum(parts_ref[...].astype(jnp.float32), axis=0)
-    row_inverse, student_inverse = lanes(inverse[0:8, :]), lanes(inverse[8:16, :])
-    weight = lanes(weight_ref[...] * PROTOS)
-    teacher_row, student_row = row_inverse * weight, student_inverse * weight
+    weight = weight_ref[...] * PROTOS
+    teacher_row, student_row = inverse[0:8, :] * weight, inverse[8:16, :] * weight
     first = 1 - place_ref[0] if other else place_ref[0]
     for n, k in enumerate(pieces):
         base = (place_ref[1] + 2 * k + first) % N_X * BLOCK
@@ -281,9 +300,12 @@
                 start = base + i * 256 + h * 128
                 column = to_column(scale_ref[pl.ds(start // 128, 1), :])
                 rows = pl.ds(pl.multiple_of(start, 128), 128)
-                targets = teacher_exp_ref[rows, :] * column * teacher_row
-                probs = student_exp_ref[rows, :] * student_row
-                errors.append((probs - targets).astype(jnp.bfloat16))
+                line = []
+                for z in range(N_Z):
+                    targets = teacher_exp_ref[z, rows, :] * column * teacher_row[z : z + 1, :]
+                    probs = student_exp_ref[z, rows, :] * student_row[z : z + 1, :]
+                    line.append((probs - targets).astype(jnp.bfloat16))
+                errors.append(jnp.concatenate(line, axis=1))
             out_ref[n, i * 256 : (i + 1) * 256, :] = jnp.dot(
                 jnp.concatenate(errors, axis=0),
                 token_ref[...],
@@ -291,7 +313,7 @@
             ).astype(out_ref.dtype)
 
 
-def call(kernel, outs, scratch, *args, flops=0, transcendentals=0):
+def call(kernel, outs, scratch, *args, flops=0, transcendentals=0, aliases=None):
     vmem = pl.BlockSpec(memory_space=pltpu.VMEM)
     smem = pl.BlockSpec(memory_space=pltpu.SMEM)
     return pl.pallas_call(
@@ -300,6 +322,7 @@
         in_specs=[smem if a.ndim == 1 else vmem for a in args],
         out_specs=[vmem] * len(outs),
         scratch_shapes=scratch,
+        input_output_aliases=aliases or {},
         compiler_params=pltpu.CompilerParams(vmem_limit_bytes=VMEM_LIMIT),
         cost_estimate=pl.CostEstimate(
             flops=flops, transcendentals=transcendentals, bytes_accessed=COLS * ROWS * 4
@@ -336,26 +359,39 @@
             packs[N_Z - k] = from_z(packs[(N_Z - k + 1) % N_Z], -1)
     own_units = [unit, from_x(unit, 1), None, from_x(unit, -1)]
     own_units[2] = from_x(own_units[1], 1)
-    near, _ = lax.optimization_barrier(((own_units[1], own_units[3]), (packs[3], packs[5])))
-    far, packs = lax.optimization_barrier((own_units[2], packs))
-    other_units = [other_unit, swapped(near[0]), swapped(far), swapped(near[1])]
-
-    teacher_exp, student_exp, col_parts, student_part, student_tokens = call(
-        exp_kernel,
-        [
-            shape((COLS, ROWS)),
-            shape((COLS, ROWS)),
-            shape((N_COLGRP, 16, 128)),
-            shape((8, 128)),
-            shape((ROWS, 256), jnp.bfloat16),
-        ],
-        [pltpu.VMEM((ROWS, 256), jnp.bfloat16), pltpu.VMEM((16, 128), jnp.float32)],
-        place,
-        *(packs[k] for k in range(N_Z)),
-        *own_units,
-        *other_units,
-        flops=4 * work * 256,
-        transcendentals=2 * work,
+    near, _ = lax.optimization_barrier((tuple(own_units[1:]), (packs[3], packs[5])))
+    other_units = [other_unit] + [swapped(block) for block in near]
+
+    held = [
+        shape((N_Z, COLS, 128)),
+        shape((N_Z, COLS, 128)),
+        shape((8, 128)),
+        shape((ROWS, 256), jnp.bfloat16),
+    ]
+
+    def exponents(chunks, first_out, aliases, *carried):
+        return call(
+            functools.partial(exp_kernel, chunks, bool(carried)),
+            [first_out] + held,
+            [pltpu.VMEM((len(chunks) * OWN_ROWS, 256), jnp.bfloat16)],
+            place,
+            *(packs[k] for k in chunks),
+            *own_units,
+            *other_units,
+            *carried,
+            flops=len(chunks) * work * 256 // 2,
+            transcendentals=len(chunks) * work // 4,
+            aliases=aliases,
+        )
+
+    early, late = (0, 1, 7, 2, 6, 3), (5, 4)
+    carried = exponents(early, shape((16, 128)), None)
+    start = 1 + len(late) + 2 * N_X + 1
+    col_parts, teacher_exp, student_exp, student_part, student_tokens = exponents(
+        late,
+        shape((N_COLGRP, 16, 128)),
+        {start + n: 1 + n for n in range(4)},
+        *carried,
     )
 
     for sweep in range(3):

time: 129 us -> 129 us (level)
  Pallas kernels: 12 us -> 13.7 us
  starting transfers between devices: 26.1 us -> 24.5 us
  blocking collectives: 70.1 us -> 68.6 us
    pallas_call x8 -> x9, Pallas kernels: 9.86 us -> 11.5 us  [call(): pl.pallas_call(kernel, out_shape=outs, in_specs=[smem if a.ndim == 1 else...]
    ppermute x13, starting transfers between devices: 25 us -> 23.4 us  [permuted(): return lax.ppermute(block, AXES, route)]
    all_to_all x6, blocking collectives: 70.1 us -> 68.6 us  [exchange(): lax.all_to_all(blocks, AXES, 0, 0, axis_index_groups=groups, tiled=True)]
  transfers between devices with their start and end apart: 19 -> 19, of which waited for: 11 -> 12; matrix products, arithmetic and copies ran while one was open for 0% -> 0% of each run, Pallas kernels for 1% -> 4%
where the time goes in v7:
time: 129 us; the launch traced here: 128 us
  blocking collectives  68.6 us (53%)
  starting transfers between devices  24.5 us (19%)
  waiting for transfers between devices  20.1 us (16%)
  Pallas kernels  13.7 us (11%)
    all_to_all x6, blocking collectives, exchange(): lax.all_to_all(blocks, AXES, 0, 0, axis_index_groups=groups, tiled=True)  68.6 us
    ppermute x13, starting transfers between devices, permuted(): return lax.ppermute(block, AXES, route)  23.4 us
    ppermute x13, waiting for transfers between devices, permuted(): return lax.ppermute(block, AXES, route)  16 us
    pallas_call x9, Pallas kernels, call(): pl.pallas_call(kernel, out_shape=outs, in_specs=[smem if a.ndim == 1 else...  11.5 us
    ppermute x6, waiting for transfers between devices, swapped(): return lax.ppermute(block, 'grp', [(0, 1), (1, 0)])  4.08 us
  transfers between devices with their start and end apart: 19, of which 12 were waited for; matrix products, arithmetic and copies ran while one was open for 0% of the time, Pallas kernels for 4%

profile of v7, /device:TPU:2, one launch (start us, length us, event | category | flops | bytes accessed | tf_op | source)
XLA Modules:
  0.0 128.1 jit_solution(11921441491799743478)
XLA Ops:
  0.0 0.5 collective-permute-start.1
  0.5 0.1 pad_add_fusion.place_ref.refs_0_
  0.6 1.9 %collective-permute-done.1.other_features_ref = bf16[512,256]{1,0:T(8,128)(2,1)S(1)} collective-permute-done((bf16[512,256]{1,0:T(8,128)(2,1)}, bf16[512,256]{1,0:T(8,128)(2,1)S(1)}, u32[]{:S(2)}, u32[]{:S(2)}) %collective-permute-start.1) | collective-permute-done | bytes 262176 | tf_op jit(solution)/shard_map/ppermute | solution.py:61
  2.5 2.2 %shard_map.37 = (bf16[256,256]{1,0:T(8,128)(2,1)S(1)}, bf16[8,128]{1,0:T(8,128)(2,1)S(1)}, bf16[512,256]{1,0:T(8,128)(2,1)S(1)}, bf16[512,256]{1,0:T(8,128)(2,1)S(1)}) custom-call(s32[3]{0:T(128)S(1)} %pad_add_fusion.place_ref.refs_0_, bf16[512,256]{1,0:T(8,128)(2,1)} %bitcast.20, bf16[512,256]{1,0:T(8,128)(2,1)S(1)} %collective-permute-done.1.other_features_ref, ...), custom_call_target="tpu_custom_call" | custom-call | tf_op jit(solution)/shard_map/pallas_call | solution.py:153
  4.7 2.3 %collective-permute-start.9 = (bf16[512,256]{1,0:T(8,128)(2,1)S(1)}, bf16[512,256]{1,0:T(8,128)(2,1)S(1)}, u32[]{:S(2)}, u32[]{:S(2)}) collective-permute-start(bf16[512,256]{1,0:T(8,128)(2,1)S(1)} %get-tuple-element.29.refs_7_.refs_3_), channel_id=1, source_target_pairs={{0,68},{1,69},{2,70},{3,71},{4,0},{5,1},{6,2},{7,3},{8,76},{9,77},... | collective-permute-start | bytes 786440 | tf_op jit(solution)/shard_map/ppermute | solution.py:70
  7.0 4.1 %collective-permute-start.5 = (bf16[256,256]{1,0:T(8,128)(2,1)S(1)}, bf16[256,256]{1,0:T(8,128)(2,1)S(1)}, u32[]{:S(2)}, u32[]{:S(2)}) collective-permute-start(bf16[256,256]{1,0:T(8,128)(2,1)S(1)} %get-tuple-element.28.refs_1_), channel_id=1, source_target_pairs={{0,56},{1,57},{2,58},{3,59},{4,60},{5,61},{6,62},{7,63},{8,0},{9,1... | collective-permute-start | bytes 393224 | tf_op jit(solution)/shard_map/ppermute | solution.py:70
  11.2 1.5 %collective-permute-start.11 = (bf16[512,256]{1,0:T(8,128)(2,1)S(1)}, bf16[512,256]{1,0:T(8,128)(2,1)S(1)}, u32[]{:S(2)}, u32[]{:S(2)}) collective-permute-start(bf16[512,256]{1,0:T(8,128)(2,1)S(1)} %get-tuple-element.29.refs_7_.refs_3_), channel_id=1, source_target_pairs={{0,4},{1,5},{2,6},{3,7},{4,64},{5,65},{6,66},{7,67},{8,12},{9,13},... | collective-permute-start | bytes 786440 | tf_op jit(solution)/shard_map/ppermute | solution.py:70
  12.7 1.3 %collective-permute-done.5.refs_2_ = bf16[256,256]{1,0:T(8,128)(2,1)S(1)} collective-permute-done((bf16[256,256]{1,0:T(8,128)(2,1)S(1)}, bf16[256,256]{1,0:T(8,128)(2,1)S(1)}, u32[]{:S(2)}, u32[]{:S(2)}) %collective-permute-start.5) | collective-permute-done | bytes 131104 | tf_op jit(solution)/shard_map/ppermute | solution.py:70
  13.9 3.7 %collective-permute-start.6 = (bf16[256,256]{1,0:T(8,128)(2,1)S(1)}, bf16[256,256]{1,0:T(8,128)(2,1)S(1)}, u32[]{:S(2)}, u32[]{:S(2)}) collective-permute-start(bf16[256,256]{1,0:T(8,128)(2,1)S(1)} %collective-permute-done.5.refs_2_), channel_id=1, source_target_pairs={{0,56},{1,57},{2,58},{3,59},{4,60},{5,61},{6,62},{7,63},{8,0},{9,1... | collective-permute-start | bytes 393224 | tf_op jit(solution)/shard_map/ppermute | solution.py:70
  17.6 2.8 %collective-permute-start.10 = (bf16[512,256]{1,0:T(8,128)(2,1)S(1)}, bf16[512,256]{1,0:T(8,128)(2,1)S(1)}, u32[]{:S(2)}, u32[]{:S(2)}) collective-permute-start(bf16[512,256]{1,0:T(8,128)(2,1)S(1)} %collective-permute-done.9.refs_8_.refs_4_), channel_id=1, source_target_pairs={{0,68},{1,69},{2,70},{3,71},{4,0},{5,1},{6,2},{7,3},{8,76},{9,77},... | collective-permute-start | bytes 786440 | tf_op jit(solution)/shard_map/ppermute | solution.py:70
  20.5 3.3 %collective-permute-start.7 = (bf16[256,256]{1,0:T(8,128)(2,1)S(1)}, bf16[256,256]{1,0:T(8,128)(2,1)S(1)}, u32[]{:S(2)}, u32[]{:S(2)}) collective-permute-start(bf16[256,256]{1,0:T(8,128)(2,1)S(1)} %collective-permute-done.6.refs_4_), channel_id=1, source_target_pairs={{0,56},{1,57},{2,58},{3,59},{4,60},{5,61},{6,62},{7,63},{8,0},{9,1... | collective-permute-start | bytes 393224 | tf_op jit(solution)/shard_map/ppermute | solution.py:70
  23.8 0.0 collective-permute-done.3.refs_5_
  23.8 2.5 %collective-permute-done.7.refs_6_ = bf16[256,256]{1,0:T(8,128)(2,1)S(1)} collective-permute-done((bf16[256,256]{1,0:T(8,128)(2,1)S(1)}, bf16[256,256]{1,0:T(8,128)(2,1)S(1)}, u32[]{:S(2)}, u32[]{:S(2)}) %collective-permute-start.7) | collective-permute-done | bytes 131104 | tf_op jit(solution)/shard_map/ppermute | solution.py:70
  26.3 3.7 %collective-permute-done.4.refs_1_ = bf16[256,256]{1,0:T(8,128)(2,1)S(1)} collective-permute-done((bf16[256,256]{1,0:T(8,128)(2,1)S(1)}, bf16[256,256]{1,0:T(8,128)(2,1)S(1)}, u32[]{:S(2)}, u32[]{:S(2)}) %collective-permute-start.4) | collective-permute-done | bytes 131104 | tf_op jit(solution)/shard_map/ppermute | solution.py:70
  30.0 0.5 collective-permute-start.13
  30.5 0.0 collective-permute-start.14
  30.5 0.1 collective-permute-start.8
  30.6 0.9 collective-permute-done.12.refs_12_.refs_8_
  31.5 0.4 collective-permute-done.13.refs_13_.refs_9_
  31.9 0.4 collective-permute-done.14.refs_14_.refs_10_
  32.3 3.2 %shard_map.38 = (f32[16,128]{1,0:T(8,128)S(1)}, f32[8,2048,128]{2,1,0:T(8,128)S(1)}, f32[8,2048,128]{2,1,0:T(8,128)S(1)}, f32[8,128]{1,0:T(8,128)S(1)}, bf16[1024,256]{1,0:T(8,128)(2,1)S(1)}) custom-call(s32[3]{0:T(128)S(1)} %pad_add_fusion.place_ref.refs_0_, bf16[256,256]{1,0:T(8,128)(2,1)S(1)} %get-tuple-element.28.refs_1_, ...), custom_call_target="tpu_custom_call" | custom-call | flops 1610612736 | bytes 8388608 | tf_op jit(solution)/shard_map/pallas_call | solution.py:319
  35.5 0.9 collective-permute-done.8.refs_2_
  36.4 1.6 %shard_map.39 = (f32[8,16,128]{2,1,0:T(8,128)S(1)}, f32[8,2048,128]{2,1,0:T(8,128)S(1)}, f32[8,2048,128]{2,1,0:T(8,128)S(1)}, f32[8,128]{1,0:T(8,128)S(1)}, bf16[1024,256]{1,0:T(8,128)(2,1)S(1)}) custom-call(s32[3]{0:T(128)S(1)} %pad_add_fusion.place_ref.refs_0_, ...), custom_call_target="tpu_custom_call", output_to_operand_aliasing={{1}: (12, {}), {2}: (13, {}), {3}: (14, {}), {4}: (15, {})} | custom-call | flops 536870912 | bytes 8388608 | tf_op jit(solution)/shard_map/pallas_call | solution.py:319
  38.1 9.2 %all_to_all.30.refs_0_ = f32[8,16,128]{2,1,0:T(8,128)S(1)} all-to-all(f32[8,16,128]{2,1,0:T(8,128)S(1)} %get-tuple-element.39), channel_id=1, replica_groups={{0,4,64,68,128,132,192,196},{1,5,65,69,129,133,193,197},{2,6,66,70,130,..., dimensions={0} | all-to-all | bytes 131072 | tf_op jit(solution)/shard_map/all_to_all | solution.py:57
  47.3 0.8 shard_map.40
  48.1 16.5 %all_to_all.31.refs_0_ = bf16[32,16,128]{2,1,0:T(8,128)(2,1)S(1)} all-to-all(bf16[32,16,128]{2,1,0:T(8,128)(2,1)S(1)} %get-tuple-element.42), channel_id=1, replica_groups={{0,1,2,3,8,9,10,11,16,17,18,19,24,25,26,27,32,33,34,35,40,41,42,43,48,4..., dimensions={0} | all-to-all | bytes 262144 | tf_op jit(solution)/shard_map/all_to_all | solution.py:57
  64.6 0.7 shard_map.41
  65.3 7.7 %all_to_all.32.refs_0_ = f32[8,16,128]{2,1,0:T(8,128)S(1)} all-to-all(f32[8,16,128]{2,1,0:T(8,128)S(1)} %get-tuple-element.43), channel_id=1, replica_groups={{0,4,64,68,128,132,192,196},{1,5,65,69,129,133,193,197},{2,6,66,70,130,..., dimensions={0} | all-to-all | bytes 131072 | tf_op jit(solution)/shard_map/all_to_all | solution.py:57
  73.0 0.8 shard_map.42
  73.8 13.2 %all_to_all.33.refs_0_ = bf16[32,8,128]{2,1,0:T(8,128)(2,1)S(1)} all-to-all(bf16[32,8,128]{2,1,0:T(8,128)(2,1)S(1)} %get-tuple-element.44), channel_id=1, replica_groups={{0,1,2,3,8,9,10,11,16,17,18,19,24,25,26,27,32,33,34,35,40,41,42,43,48,4..., dimensions={0} | all-to-all | bytes 131072 | tf_op jit(solution)/shard_map/all_to_all | solution.py:57
  87.1 0.7 shard_map.43
  87.8 7.9 %all_to_all.34.refs_0_ = f32[8,16,128]{2,1,0:T(8,128)S(1)} all-to-all(f32[8,16,128]{2,1,0:T(8,128)S(1)} %shard_map.43), channel_id=1, replica_groups={{0,4,64,68,128,132,192,196},{1,5,65,69,129,133,193,197},{2,6,66,70,130,..., dimensions={0} | all-to-all | bytes 131072 | tf_op jit(solution)/shard_map/all_to_all | solution.py:57
  95.7 0.7 shard_map.44
  96.4 14.1 %all_to_all.35.parts_ref = bf16[32,16,128]{2,1,0:T(8,128)(2,1)S(1)} all-to-all(bf16[32,16,128]{2,1,0:T(8,128)(2,1)S(1)} %get-tuple-element.46), channel_id=1, replica_groups={{0,1,2,3,8,9,10,11,16,17,18,19,24,25,26,27,32,33,34,35,40,41,42,43,48,4..., dimensions={0} | all-to-all | bytes 262144 | tf_op jit(solution)/shard_map/all_to_all | solution.py:57
  110.4 1.4 %shard_map.46 = bf16[2,512,256]{2,1,0:T(8,128)(2,1)S(1)} custom-call(s32[3]{0:T(128)S(1)} %pad_add_fusion.place_ref.refs_0_, bf16[32,16,128]{2,1,0:T(8,128)(2,1)S(1)} %all_to_all.35.parts_ref, f32[16,128]{1,0:T(8,128)S(1)} %get-tuple-element.47.scale_ref, f32[8,128]{1,0:T(8,128)S(1)} %get-tuple-element.48.weight_ref, ...), custom_call_target="tpu_custom_call" | custom-call | flops 536870912 | bytes 8388608 | tf_op jit(solution)/shard_map/pallas_call | solution.py:319
  111.9 0.0 copy-start
  111.9 0.1 collective-permute-start.15
  112.0 1.4 %shard_map.45 = f32[2,512,256]{2,1,0:T(8,128)S(1)} custom-call(s32[3]{0:T(128)S(1)} %pad_add_fusion.place_ref.refs_0_, bf16[32,16,128]{2,1,0:T(8,128)(2,1)S(1)} %all_to_all.35.parts_ref, f32[16,128]{1,0:T(8,128)S(1)} %get-tuple-element.47.scale_ref, f32[8,128]{1,0:T(8,128)S(1)} %get-tuple-element.48.weight_ref, ...), custom_call_target="tpu_custom_call" | custom-call | flops 536870912 | bytes 8388608 | tf_op jit(solution)/shard_map/pallas_call | solution.py:319
  113.4 0.5 collective-permute-done.15
  113.9 0.1 convert_add_fusion
  114.0 0.1 fusion
  114.0 1.3 %collective-permute-start.17 = (bf16[512,256]{1,0:T(8,128)(2,1)S(1)}, bf16[512,256]{1,0:T(8,128)(2,1)S(1)}, u32[]{:S(2)}, u32[]{:S(2)}) collective-permute-start(bf16[512,256]{1,0:T(8,128)(2,1)S(1)} %get-tuple-element.51), channel_id=1, source_target_pairs={{128,4},{129,5},{130,6},{131,7},{132,64},{133,65},{134,66},{135,67... | collective-permute-start | bytes 786440 | tf_op jit(solution)/shard_map/ppermute | solution.py:70
  115.3 1.3 %collective-permute-start.18 = (bf16[512,256]{1,0:T(8,128)(2,1)S(1)}, bf16[512,256]{1,0:T(8,128)(2,1)S(1)}, u32[]{:S(2)}, u32[]{:S(2)}) collective-permute-start(bf16[512,256]{1,0:T(8,128)(2,1)S(1)} %get-tuple-element.52), channel_id=1, source_target_pairs={{128,68},{129,69},{130,70},{131,71},{132,0},{133,1},{134,2},{135,3... | collective-permute-start | bytes 786440 | tf_op jit(solution)/shard_map/ppermute | solution.py:70
  116.6 2.9 %collective-permute-start.16 = (bf16[512,256]{1,0:T(8,128)(2,1)S(1)}, bf16[512,256]{1,0:T(8,128)(2,1)S(1)}, u32[]{:S(2)}, u32[]{:S(2)}) collective-permute-start(bf16[512,256]{1,0:T(8,128)(2,1)S(1)} %get-tuple-element.52), channel_id=1, source_target_pairs={{0,64},{1,65},{2,66},{3,67},{4,68},{5,69},{6,70},{7,71},{8,72},{9,... | collective-permute-start | bytes 786440 | tf_op jit(solution)/shard_map/ppermute | solution.py:70
  119.5 2.2 %collective-permute-done.17 = bf16[512,256]{1,0:T(8,128)(2,1)S(1)} collective-permute-done((bf16[512,256]{1,0:T(8,128)(2,1)S(1)}, bf16[512,256]{1,0:T(8,128)(2,1)S(1)}, u32[]{:S(2)}, u32[]{:S(2)}) %collective-permute-start.17) | collective-permute-done | bytes 262176 | tf_op jit(solution)/shard_map/ppermute | solution.py:70
  121.7 1.3 %collective-permute-done.18 = bf16[512,256]{1,0:T(8,128)(2,1)S(1)} collective-permute-done((bf16[512,256]{1,0:T(8,128)(2,1)S(1)}, bf16[512,256]{1,0:T(8,128)(2,1)S(1)}, u32[]{:S(2)}, u32[]{:S(2)}) %collective-permute-start.18) | collective-permute-done | bytes 262176 | tf_op jit(solution)/shard_map/ppermute | solution.py:70
  123.0 4.2 %collective-permute-done.16 = bf16[512,256]{1,0:T(8,128)(2,1)S(1)} collective-permute-done((bf16[512,256]{1,0:T(8,128)(2,1)S(1)}, bf16[512,256]{1,0:T(8,128)(2,1)S(1)}, u32[]{:S(2)}, u32[]{:S(2)}) %collective-permute-start.16) | collective-permute-done | bytes 262176 | tf_op jit(solution)/shard_map/ppermute | solution.py:70
  127.2 1.0 select_bitcast_fusion
  (12 shorter events, 0.0 us)
Async XLA Ops:
  0.0 2.5 %collective-permute-start = (f32[512,256]{1,0:T(8,128)}, f32[512,256]{1,0:T(8,128)S(1)}, u32[]{:S(2)}, u32[]{:S(2)}) collective-permute-start(f32[512,256]{1,0:T(8,128)} %bitcast.17), channel_id=1, source_target_pairs={{0,128},{128,0},{1,129},{129,1},{2,130},{130,2},{3,131},{131,3},{4... | collective-permute-start | bytes 1572872 | tf_op jit(solution)/shard_map/ppermute | solution.py:61
  0.0 2.5 %collective-permute-start.1 = (bf16[512,256]{1,0:T(8,128)(2,1)}, bf16[512,256]{1,0:T(8,128)(2,1)S(1)}, u32[]{:S(2)}, u32[]{:S(2)}) collective-permute-start(bf16[512,256]{1,0:T(8,128)(2,1)} %bitcast.19), channel_id=1, source_target_pairs={{0,128},{128,0},{1,129},{129,1},{2,130},{130,2},{3,131},{131,3},{4... | collective-permute-start | bytes 786440 | tf_op jit(solution)/shard_map/ppermute | solution.py:61
  4.7 12.9 %collective-permute-start.9 = (bf16[512,256]{1,0:T(8,128)(2,1)S(1)}, bf16[512,256]{1,0:T(8,128)(2,1)S(1)}, u32[]{:S(2)}, u32[]{:S(2)}) collective-permute-start(bf16[512,256]{1,0:T(8,128)(2,1)S(1)} %get-tuple-element.29.refs_7_.refs_3_), channel_id=1, source_target_pairs={{0,68},{1,69},{2,70},{3,71},{4,0},{5,1},{6,2},{7,3},{8,76},{9,77},... | collective-permute-start | bytes 786440 | tf_op jit(solution)/shard_map/ppermute | solution.py:70
  7.0 6.9 %collective-permute-start.5 = (bf16[256,256]{1,0:T(8,128)(2,1)S(1)}, bf16[256,256]{1,0:T(8,128)(2,1)S(1)}, u32[]{:S(2)}, u32[]{:S(2)}) collective-permute-start(bf16[256,256]{1,0:T(8,128)(2,1)S(1)} %get-tuple-element.28.refs_1_), channel_id=1, source_target_pairs={{0,56},{1,57},{2,58},{3,59},{4,60},{5,61},{6,62},{7,63},{8,0},{9,1... | collective-permute-start | bytes 393224 | tf_op jit(solution)/shard_map/ppermute | solution.py:70
  11.2 6.5 %collective-permute-start.2 = (bf16[256,256]{1,0:T(8,128)(2,1)S(1)}, bf16[256,256]{1,0:T(8,128)(2,1)S(1)}, u32[]{:S(2)}, u32[]{:S(2)}) collective-permute-start(bf16[256,256]{1,0:T(8,128)(2,1)S(1)} %get-tuple-element.28.refs_1_), channel_id=1, source_target_pairs={{0,8},{1,9},{2,10},{3,11},{4,12},{5,13},{6,14},{7,15},{8,16},{9,17... | collective-permute-start | bytes 393224 | tf_op jit(solution)/shard_map/ppermute | solution.py:70
  11.2 12.7 %collective-permute-start.11 = (bf16[512,256]{1,0:T(8,128)(2,1)S(1)}, bf16[512,256]{1,0:T(8,128)(2,1)S(1)}, u32[]{:S(2)}, u32[]{:S(2)}) collective-permute-start(bf16[512,256]{1,0:T(8,128)(2,1)S(1)} %get-tuple-element.29.refs_7_.refs_3_), channel_id=1, source_target_pairs={{0,4},{1,5},{2,6},{3,7},{4,64},{5,65},{6,66},{7,67},{8,12},{9,13},... | collective-permute-start | bytes 786440 | tf_op jit(solution)/shard_map/ppermute | solution.py:70
  13.9 6.5 %collective-permute-start.6 = (bf16[256,256]{1,0:T(8,128)(2,1)S(1)}, bf16[256,256]{1,0:T(8,128)(2,1)S(1)}, u32[]{:S(2)}, u32[]{:S(2)}) collective-permute-start(bf16[256,256]{1,0:T(8,128)(2,1)S(1)} %collective-permute-done.5.refs_2_), channel_id=1, source_target_pairs={{0,56},{1,57},{2,58},{3,59},{4,60},{5,61},{6,62},{7,63},{8,0},{9,1... | collective-permute-start | bytes 393224 | tf_op jit(solution)/shard_map/ppermute | solution.py:70
  17.6 6.2 %collective-permute-start.3 = (bf16[256,256]{1,0:T(8,128)(2,1)S(1)}, bf16[256,256]{1,0:T(8,128)(2,1)S(1)}, u32[]{:S(2)}, u32[]{:S(2)}) collective-permute-start(bf16[256,256]{1,0:T(8,128)(2,1)S(1)} %collective-permute-done.2.refs_3_), channel_id=1, source_target_pairs={{0,8},{1,9},{2,10},{3,11},{4,12},{5,13},{6,14},{7,15},{8,16},{9,17... | collective-permute-start | bytes 393224 | tf_op jit(solution)/shard_map/ppermute | solution.py:70
  17.6 12.4 %collective-permute-start.10 = (bf16[512,256]{1,0:T(8,128)(2,1)S(1)}, bf16[512,256]{1,0:T(8,128)(2,1)S(1)}, u32[]{:S(2)}, u32[]{:S(2)}) collective-permute-start(bf16[512,256]{1,0:T(8,128)(2,1)S(1)} %collective-permute-done.9.refs_8_.refs_4_), channel_id=1, source_target_pairs={{0,68},{1,69},{2,70},{3,71},{4,0},{5,1},{6,2},{7,3},{8,76},{9,77},... | collective-permute-start | bytes 786440 | tf_op jit(solution)/shard_map/ppermute | solution.py:70
  20.5 5.8 %collective-permute-start.7 = (bf16[256,256]{1,0:T(8,128)(2,1)S(1)}, bf16[256,256]{1,0:T(8,128)(2,1)S(1)}, u32[]{:S(2)}, u32[]{:S(2)}) collective-permute-start(bf16[256,256]{1,0:T(8,128)(2,1)S(1)} %collective-permute-done.6.refs_4_), channel_id=1, source_target_pairs={{0,56},{1,57},{2,58},{3,59},{4,60},{5,61},{6,62},{7,63},{8,0},{9,1... | collective-permute-start | bytes 393224 | tf_op jit(solution)/shard_map/ppermute | solution.py:70
  23.8 6.2 %collective-permute-start.4 = (bf16[256,256]{1,0:T(8,128)(2,1)S(1)}, bf16[256,256]{1,0:T(8,128)(2,1)S(1)}, u32[]{:S(2)}, u32[]{:S(2)}) collective-permute-start(bf16[256,256]{1,0:T(8,128)(2,1)S(1)} %collective-permute-done.3.refs_5_), channel_id=1, source_target_pairs={{0,8},{1,9},{2,10},{3,11},{4,12},{5,13},{6,14},{7,15},{8,16},{9,17... | collective-permute-start | bytes 393224 | tf_op jit(solution)/shard_map/ppermute | solution.py:70
  30.0 1.5 %collective-permute-start.12 = (bf16[512,256]{1,0:T(8,128)(2,1)S(1)}, bf16[512,256]{1,0:T(8,128)(2,1)S(1)}, u32[]{:S(2)}, u32[]{:S(2)}) collective-permute-start(bf16[512,256]{1,0:T(8,128)(2,1)S(1)} %collective-permute-done.9.refs_8_.refs_4_), channel_id=1, source_target_pairs={{0,128},{128,0},{1,129},{129,1},{2,130},{130,2},{3,131},{131,3},{4... | collective-permute-start | bytes 786440 | tf_op jit(solution)/shard_map/ppermute | solution.py:61
  30.0 1.9 %collective-permute-start.13 = (bf16[512,256]{1,0:T(8,128)(2,1)S(1)}, bf16[512,256]{1,0:T(8,128)(2,1)S(1)}, u32[]{:S(2)}, u32[]{:S(2)}) collective-permute-start(bf16[512,256]{1,0:T(8,128)(2,1)S(1)} %collective-permute-done.10.refs_9_.refs_5_), channel_id=1, source_target_pairs={{0,128},{128,0},{1,129},{129,1},{2,130},{130,2},{3,131},{131,3},{4... | collective-permute-start | bytes 786440 | tf_op jit(solution)/shard_map/ppermute | solution.py:61
  30.5 1.8 %collective-permute-start.14 = (bf16[512,256]{1,0:T(8,128)(2,1)S(1)}, bf16[512,256]{1,0:T(8,128)(2,1)S(1)}, u32[]{:S(2)}, u32[]{:S(2)}) collective-permute-start(bf16[512,256]{1,0:T(8,128)(2,1)S(1)} %collective-permute-done.11.refs_10_.refs_6_), channel_id=1, source_target_pairs={{0,128},{128,0},{1,129},{129,1},{2,130},{130,2},{3,131},{131,3},{4... | collective-permute-start | bytes 786440 | tf_op jit(solution)/shard_map/ppermute | solution.py:61
  30.5 5.9 %collective-permute-start.8 = (bf16[256,256]{1,0:T(8,128)(2,1)S(1)}, bf16[256,256]{1,0:T(8,128)(2,1)S(1)}, u32[]{:S(2)}, u32[]{:S(2)}) collective-permute-start(bf16[256,256]{1,0:T(8,128)(2,1)S(1)} %collective-permute-done.7.refs_6_), channel_id=1, source_target_pairs={{0,56},{1,57},{2,58},{3,59},{4,60},{5,61},{6,62},{7,63},{8,0},{9,1... | collective-permute-start | bytes 393224 | tf_op jit(solution)/shard_map/ppermute | solution.py:70
  111.9 15.3 %copy-start = (f32[1,512,256]{2,1,0:T(8,128)S(1)}, f32[1,512,256]{2,1,0:T(8,128)}, u32[]{:S(2)}) copy-start(f32[1,512,256]{2,1,0:T(8,128)} %param.4) | copy-start | bytes 1572868
  111.9 2.0 %collective-permute-start.15 = (bf16[2,512,256]{2,1,0:T(8,128)(2,1)S(1)}, bf16[2,512,256]{2,1,0:T(8,128)(2,1)S(1)}, u32[]{:S(2)}, u32[]{:S(2)}) collective-permute-start(bf16[2,512,256]{2,1,0:T(8,128)(2,1)S(1)} %shard_map.46), channel_id=1, source_target_pairs={{0,128},{128,0},{1,129},{129,1},{2,130},{130,2},{3,131},{131,3},{4... | collective-permute-start | bytes 1572872 | tf_op jit(solution)/shard_map/ppermute | solution.py:61
  114.0 7.7 %collective-permute-start.17 = (bf16[512,256]{1,0:T(8,128)(2,1)S(1)}, bf16[512,256]{1,0:T(8,128)(2,1)S(1)}, u32[]{:S(2)}, u32[]{:S(2)}) collective-permute-start(bf16[512,256]{1,0:T(8,128)(2,1)S(1)} %get-tuple-element.51), channel_id=1, source_target_pairs={{128,4},{129,5},{130,6},{131,7},{132,64},{133,65},{134,66},{135,67... | collective-permute-start | bytes 786440 | tf_op jit(solution)/shard_map/ppermute | solution.py:70
  115.3 7.7 %collective-permute-start.18 = (bf16[512,256]{1,0:T(8,128)(2,1)S(1)}, bf16[512,256]{1,0:T(8,128)(2,1)S(1)}, u32[]{:S(2)}, u32[]{:S(2)}) collective-permute-start(bf16[512,256]{1,0:T(8,128)(2,1)S(1)} %get-tuple-element.52), channel_id=1, source_target_pairs={{128,68},{129,69},{130,70},{131,71},{132,0},{133,1},{134,2},{135,3... | collective-permute-start | bytes 786440 | tf_op jit(solution)/shard_map/ppermute | solution.py:70
  116.6 10.5 %collective-permute-start.16 = (bf16[512,256]{1,0:T(8,128)(2,1)S(1)}, bf16[512,256]{1,0:T(8,128)(2,1)S(1)}, u32[]{:S(2)}, u32[]{:S(2)}) collective-permute-start(bf16[512,256]{1,0:T(8,128)(2,1)S(1)} %get-tuple-element.52), channel_id=1, source_target_pairs={{0,64},{1,65},{2,66},{3,67},{4,68},{5,69},{6,70},{7,71},{8,72},{9,... | collective-permute-start | bytes 786440 | tf_op jit(solution)/shard_map/ppermute | solution.py:70

commit v8 on v7

--- a/solution.py
+++ b/solution.py
@@ -263,11 +263,10 @@
     if with_weight:
         parts_ref, exp_ref, out_ref, weight_ref, vector_ref = refs
         for z in range(N_Z):
-            extra = parts_ref[z * N_Y, 8:16, :].astype(jnp.float32)
-            weight_ref[z : z + 1, :] = extra[0:1, :]
+            weight_ref[z : z + 1, :] = parts_ref[z * N_Y].astype(jnp.float32)[8:9, :]
     else:
         parts_ref, exp_ref, out_ref, vector_ref = refs
-    scale = 1.0 / jnp.sum(parts_ref[:, 0:8, :].astype(jnp.float32), axis=0)
+    scale = 1.0 / jnp.sum(parts_ref[...].astype(jnp.float32), axis=0)[0:8, :]
     for j in range(COLS // 128):
         rows = slice(j * 128, (j + 1) * 128)
         folded = sum(exp_ref[k, rows, :] * scale[k : k + 1, :] for k in range(N_Z))

time: 129 us -> 129 us (level)
  no operation moved by 1% of the time
where the time goes in v8:
time: 129 us; the launch traced here: 128 us
  blocking collectives  68.6 us (53%)
  starting transfers between devices  24.5 us (19%)
  waiting for transfers between devices  20.1 us (16%)
  Pallas kernels  13.7 us (11%)
    all_to_all x6, blocking collectives, exchange(): lax.all_to_all(blocks, AXES, 0, 0, axis_index_groups=groups, tiled=True)  68.6 us
    ppermute x13, starting transfers between devices, permuted(): return lax.ppermute(block, AXES, route)  23.4 us
    ppermute x13, waiting for transfers between devices, permuted(): return lax.ppermute(block, AXES, route)  16 us
    pallas_call x9, Pallas kernels, call(): pl.pallas_call(kernel, out_shape=outs, in_specs=[smem if a.ndim == 1 else...  11.5 us
    ppermute x6, waiting for transfers between devices, swapped(): return lax.ppermute(block, 'grp', [(0, 1), (1, 0)])  4.08 us
  transfers between devices with their start and end apart: 19, of which 12 were waited for; matrix products, arithmetic and copies ran while one was open for 0% of the time, Pallas kernels for 4%

profile of v8, /device:TPU:2, one launch (start us, length us, event | category | flops | bytes accessed | tf_op | source)
XLA Modules:
  0.0 128.1 jit_solution(11921441491799743478)
XLA Ops:
  0.0 0.5 collective-permute-start.1
  0.5 0.1 pad_add_fusion.place_ref.refs_0_
  0.6 1.9 %collective-permute-done.1.other_features_ref = bf16[512,256]{1,0:T(8,128)(2,1)S(1)} collective-permute-done((bf16[512,256]{1,0:T(8,128)(2,1)}, bf16[512,256]{1,0:T(8,128)(2,1)S(1)}, u32[]{:S(2)}, u32[]{:S(2)}) %collective-permute-start.1) | collective-permute-done | bytes 262176 | tf_op jit(solution)/shard_map/ppermute | solution.py:61
  2.5 2.2 %shard_map.37 = (bf16[256,256]{1,0:T(8,128)(2,1)S(1)}, bf16[8,128]{1,0:T(8,128)(2,1)S(1)}, bf16[512,256]{1,0:T(8,128)(2,1)S(1)}, bf16[512,256]{1,0:T(8,128)(2,1)S(1)}) custom-call(s32[3]{0:T(128)S(1)} %pad_add_fusion.place_ref.refs_0_, bf16[512,256]{1,0:T(8,128)(2,1)} %bitcast.20, bf16[512,256]{1,0:T(8,128)(2,1)S(1)} %collective-permute-done.1.other_features_ref, ...), custom_call_target="tpu_custom_call" | custom-call | tf_op jit(solution)/shard_map/pallas_call | solution.py:153
  4.7 2.3 %collective-permute-start.9 = (bf16[512,256]{1,0:T(8,128)(2,1)S(1)}, bf16[512,256]{1,0:T(8,128)(2,1)S(1)}, u32[]{:S(2)}, u32[]{:S(2)}) collective-permute-start(bf16[512,256]{1,0:T(8,128)(2,1)S(1)} %get-tuple-element.29.refs_7_.refs_3_), channel_id=1, source_target_pairs={{0,68},{1,69},{2,70},{3,71},{4,0},{5,1},{6,2},{7,3},{8,76},{9,77},... | collective-permute-start | bytes 786440 | tf_op jit(solution)/shard_map/ppermute | solution.py:70
  7.0 4.1 %collective-permute-start.5 = (bf16[256,256]{1,0:T(8,128)(2,1)S(1)}, bf16[256,256]{1,0:T(8,128)(2,1)S(1)}, u32[]{:S(2)}, u32[]{:S(2)}) collective-permute-start(bf16[256,256]{1,0:T(8,128)(2,1)S(1)} %get-tuple-element.28.refs_1_), channel_id=1, source_target_pairs={{0,56},{1,57},{2,58},{3,59},{4,60},{5,61},{6,62},{7,63},{8,0},{9,1... | collective-permute-start | bytes 393224 | tf_op jit(solution)/shard_map/ppermute | solution.py:70
  11.2 1.5 %collective-permute-start.11 = (bf16[512,256]{1,0:T(8,128)(2,1)S(1)}, bf16[512,256]{1,0:T(8,128)(2,1)S(1)}, u32[]{:S(2)}, u32[]{:S(2)}) collective-permute-start(bf16[512,256]{1,0:T(8,128)(2,1)S(1)} %get-tuple-element.29.refs_7_.refs_3_), channel_id=1, source_target_pairs={{0,4},{1,5},{2,6},{3,7},{4,64},{5,65},{6,66},{7,67},{8,12},{9,13},... | collective-permute-start | bytes 786440 | tf_op jit(solution)/shard_map/ppermute | solution.py:70
  12.7 1.3 %collective-permute-done.5.refs_2_ = bf16[256,256]{1,0:T(8,128)(2,1)S(1)} collective-permute-done((bf16[256,256]{1,0:T(8,128)(2,1)S(1)}, bf16[256,256]{1,0:T(8,128)(2,1)S(1)}, u32[]{:S(2)}, u32[]{:S(2)}) %collective-permute-start.5) | collective-permute-done | bytes 131104 | tf_op jit(solution)/shard_map/ppermute | solution.py:70
  13.9 3.7 %collective-permute-start.6 = (bf16[256,256]{1,0:T(8,128)(2,1)S(1)}, bf16[256,256]{1,0:T(8,128)(2,1)S(1)}, u32[]{:S(2)}, u32[]{:S(2)}) collective-permute-start(bf16[256,256]{1,0:T(8,128)(2,1)S(1)} %collective-permute-done.5.refs_2_), channel_id=1, source_target_pairs={{0,56},{1,57},{2,58},{3,59},{4,60},{5,61},{6,62},{7,63},{8,0},{9,1... | collective-permute-start | bytes 393224 | tf_op jit(solution)/shard_map/ppermute | solution.py:70
  17.6 2.8 %collective-permute-start.10 = (bf16[512,256]{1,0:T(8,128)(2,1)S(1)}, bf16[512,256]{1,0:T(8,128)(2,1)S(1)}, u32[]{:S(2)}, u32[]{:S(2)}) collective-permute-start(bf16[512,256]{1,0:T(8,128)(2,1)S(1)} %collective-permute-done.9.refs_8_.refs_4_), channel_id=1, source_target_pairs={{0,68},{1,69},{2,70},{3,71},{4,0},{5,1},{6,2},{7,3},{8,76},{9,77},... | collective-permute-start | bytes 786440 | tf_op jit(solution)/shard_map/ppermute | solution.py:70
  20.5 3.3 %collective-permute-start.7 = (bf16[256,256]{1,0:T(8,128)(2,1)S(1)}, bf16[256,256]{1,0:T(8,128)(2,1)S(1)}, u32[]{:S(2)}, u32[]{:S(2)}) collective-permute-start(bf16[256,256]{1,0:T(8,128)(2,1)S(1)} %collective-permute-done.6.refs_4_), channel_id=1, source_target_pairs={{0,56},{1,57},{2,58},{3,59},{4,60},{5,61},{6,62},{7,63},{8,0},{9,1... | collective-permute-start | bytes 393224 | tf_op jit(solution)/shard_map/ppermute | solution.py:70
  23.8 0.0 collective-permute-done.3.refs_5_
  23.8 2.5 %collective-permute-done.7.refs_6_ = bf16[256,256]{1,0:T(8,128)(2,1)S(1)} collective-permute-done((bf16[256,256]{1,0:T(8,128)(2,1)S(1)}, bf16[256,256]{1,0:T(8,128)(2,1)S(1)}, u32[]{:S(2)}, u32[]{:S(2)}) %collective-permute-start.7) | collective-permute-done | bytes 131104 | tf_op jit(solution)/shard_map/ppermute | solution.py:70
  26.3 3.7 %collective-permute-done.4.refs_1_ = bf16[256,256]{1,0:T(8,128)(2,1)S(1)} collective-permute-done((bf16[256,256]{1,0:T(8,128)(2,1)S(1)}, bf16[256,256]{1,0:T(8,128)(2,1)S(1)}, u32[]{:S(2)}, u32[]{:S(2)}) %collective-permute-start.4) | collective-permute-done | bytes 131104 | tf_op jit(solution)/shard_map/ppermute | solution.py:70
  30.0 0.5 collective-permute-start.13
  30.5 0.0 collective-permute-start.14
  30.5 0.1 collective-permute-start.8
  30.6 0.9 collective-permute-done.12.refs_12_.refs_8_
  31.5 0.4 collective-permute-done.13.refs_13_.refs_9_
  31.9 0.4 collective-permute-done.14.refs_14_.refs_10_
  32.3 3.2 %shard_map.38 = (f32[16,128]{1,0:T(8,128)S(1)}, f32[8,2048,128]{2,1,0:T(8,128)S(1)}, f32[8,2048,128]{2,1,0:T(8,128)S(1)}, f32[8,128]{1,0:T(8,128)S(1)}, bf16[1024,256]{1,0:T(8,128)(2,1)S(1)}) custom-call(s32[3]{0:T(128)S(1)} %pad_add_fusion.place_ref.refs_0_, bf16[256,256]{1,0:T(8,128)(2,1)S(1)} %get-tuple-element.28.refs_1_, ...), custom_call_target="tpu_custom_call" | custom-call | flops 1610612736 | bytes 8388608 | tf_op jit(solution)/shard_map/pallas_call | solution.py:318
  35.5 0.9 collective-permute-done.8.refs_2_
  36.4 1.6 %shard_map.39 = (f32[8,16,128]{2,1,0:T(8,128)S(1)}, f32[8,2048,128]{2,1,0:T(8,128)S(1)}, f32[8,2048,128]{2,1,0:T(8,128)S(1)}, f32[8,128]{1,0:T(8,128)S(1)}, bf16[1024,256]{1,0:T(8,128)(2,1)S(1)}) custom-call(s32[3]{0:T(128)S(1)} %pad_add_fusion.place_ref.refs_0_, ...), custom_call_target="tpu_custom_call", output_to_operand_aliasing={{1}: (12, {}), {2}: (13, {}), {3}: (14, {}), {4}: (15, {})} | custom-call | flops 536870912 | bytes 8388608 | tf_op jit(solution)/shard_map/pallas_call | solution.py:318
  38.1 9.2 %all_to_all.30.refs_0_ = f32[8,16,128]{2,1,0:T(8,128)S(1)} all-to-all(f32[8,16,128]{2,1,0:T(8,128)S(1)} %get-tuple-element.39), channel_id=1, replica_groups={{0,4,64,68,128,132,192,196},{1,5,65,69,129,133,193,197},{2,6,66,70,130,..., dimensions={0} | all-to-all | bytes 131072 | tf_op jit(solution)/shard_map/all_to_all | solution.py:57
  47.3 0.8 shard_map.40
  48.1 16.5 %all_to_all.31.refs_0_ = bf16[32,16,128]{2,1,0:T(8,128)(2,1)S(1)} all-to-all(bf16[32,16,128]{2,1,0:T(8,128)(2,1)S(1)} %get-tuple-element.42), channel_id=1, replica_groups={{0,1,2,3,8,9,10,11,16,17,18,19,24,25,26,27,32,33,34,35,40,41,42,43,48,4..., dimensions={0} | all-to-all | bytes 262144 | tf_op jit(solution)/shard_map/all_to_all | solution.py:57
  64.6 0.7 shard_map.41
  65.3 7.7 %all_to_all.32.refs_0_ = f32[8,16,128]{2,1,0:T(8,128)S(1)} all-to-all(f32[8,16,128]{2,1,0:T(8,128)S(1)} %get-tuple-element.43), channel_id=1, replica_groups={{0,4,64,68,128,132,192,196},{1,5,65,69,129,133,193,197},{2,6,66,70,130,..., dimensions={0} | all-to-all | bytes 131072 | tf_op jit(solution)/shard_map/all_to_all | solution.py:57
  73.0 0.8 shard_map.42
  73.8 13.2 %all_to_all.33.refs_0_ = bf16[32,8,128]{2,1,0:T(8,128)(2,1)S(1)} all-to-all(bf16[32,8,128]{2,1,0:T(8,128)(2,1)S(1)} %get-tuple-element.44), channel_id=1, replica_groups={{0,1,2,3,8,9,10,11,16,17,18,19,24,25,26,27,32,33,34,35,40,41,42,43,48,4..., dimensions={0} | all-to-all | bytes 131072 | tf_op jit(solution)/shard_map/all_to_all | solution.py:57
  87.1 0.7 shard_map.43
  87.8 7.9 %all_to_all.34.refs_0_ = f32[8,16,128]{2,1,0:T(8,128)S(1)} all-to-all(f32[8,16,128]{2,1,0:T(8,128)S(1)} %shard_map.43), channel_id=1, replica_groups={{0,4,64,68,128,132,192,196},{1,5,65,69,129,133,193,197},{2,6,66,70,130,..., dimensions={0} | all-to-all | bytes 131072 | tf_op jit(solution)/shard_map/all_to_all | solution.py:57
  95.7 0.7 shard_map.44
  96.4 14.1 %all_to_all.35.parts_ref = bf16[32,16,128]{2,1,0:T(8,128)(2,1)S(1)} all-to-all(bf16[32,16,128]{2,1,0:T(8,128)(2,1)S(1)} %get-tuple-element.46), channel_id=1, replica_groups={{0,1,2,3,8,9,10,11,16,17,18,19,24,25,26,27,32,33,34,35,40,41,42,43,48,4..., dimensions={0} | all-to-all | bytes 262144 | tf_op jit(solution)/shard_map/all_to_all | solution.py:57
  110.4 1.4 %shard_map.46 = bf16[2,512,256]{2,1,0:T(8,128)(2,1)S(1)} custom-call(s32[3]{0:T(128)S(1)} %pad_add_fusion.place_ref.refs_0_, bf16[32,16,128]{2,1,0:T(8,128)(2,1)S(1)} %all_to_all.35.parts_ref, f32[16,128]{1,0:T(8,128)S(1)} %get-tuple-element.47.scale_ref, f32[8,128]{1,0:T(8,128)S(1)} %get-tuple-element.48.weight_ref, ...), custom_call_target="tpu_custom_call" | custom-call | flops 536870912 | bytes 8388608 | tf_op jit(solution)/shard_map/pallas_call | solution.py:318
  111.9 0.0 copy-start
  111.9 0.1 collective-permute-start.15
  112.0 1.4 %shard_map.45 = f32[2,512,256]{2,1,0:T(8,128)S(1)} custom-call(s32[3]{0:T(128)S(1)} %pad_add_fusion.place_ref.refs_0_, bf16[32,16,128]{2,1,0:T(8,128)(2,1)S(1)} %all_to_all.35.parts_ref, f32[16,128]{1,0:T(8,128)S(1)} %get-tuple-element.47.scale_ref, f32[8,128]{1,0:T(8,128)S(1)} %get-tuple-element.48.weight_ref, ...), custom_call_target="tpu_custom_call" | custom-call | flops 536870912 | bytes 8388608 | tf_op jit(solution)/shard_map/pallas_call | solution.py:318
  113.4 0.5 collective-permute-done.15
  113.9 0.1 convert_add_fusion
  114.0 0.1 fusion
  114.0 1.3 %collective-permute-start.17 = (bf16[512,256]{1,0:T(8,128)(2,1)S(1)}, bf16[512,256]{1,0:T(8,128)(2,1)S(1)}, u32[]{:S(2)}, u32[]{:S(2)}) collective-permute-start(bf16[512,256]{1,0:T(8,128)(2,1)S(1)} %get-tuple-element.51), channel_id=1, source_target_pairs={{128,4},{129,5},{130,6},{131,7},{132,64},{133,65},{134,66},{135,67... | collective-permute-start | bytes 786440 | tf_op jit(solution)/shard_map/ppermute | solution.py:70
  115.3 1.3 %collective-permute-start.18 = (bf16[512,256]{1,0:T(8,128)(2,1)S(1)}, bf16[512,256]{1,0:T(8,128)(2,1)S(1)}, u32[]{:S(2)}, u32[]{:S(2)}) collective-permute-start(bf16[512,256]{1,0:T(8,128)(2,1)S(1)} %get-tuple-element.52), channel_id=1, source_target_pairs={{128,68},{129,69},{130,70},{131,71},{132,0},{133,1},{134,2},{135,3... | collective-permute-start | bytes 786440 | tf_op jit(solution)/shard_map/ppermute | solution.py:70
  116.6 2.9 %collective-permute-start.16 = (bf16[512,256]{1,0:T(8,128)(2,1)S(1)}, bf16[512,256]{1,0:T(8,128)(2,1)S(1)}, u32[]{:S(2)}, u32[]{:S(2)}) collective-permute-start(bf16[512,256]{1,0:T(8,128)(2,1)S(1)} %get-tuple-element.52), channel_id=1, source_target_pairs={{0,64},{1,65},{2,66},{3,67},{4,68},{5,69},{6,70},{7,71},{8,72},{9,... | collective-permute-start | bytes 786440 | tf_op jit(solution)/shard_map/ppermute | solution.py:70
  119.5 2.2 %collective-permute-done.17 = bf16[512,256]{1,0:T(8,128)(2,1)S(1)} collective-permute-done((bf16[512,256]{1,0:T(8,128)(2,1)S(1)}, bf16[512,256]{1,0:T(8,128)(2,1)S(1)}, u32[]{:S(2)}, u32[]{:S(2)}) %collective-permute-start.17) | collective-permute-done | bytes 262176 | tf_op jit(solution)/shard_map/ppermute | solution.py:70
  121.7 1.3 %collective-permute-done.18 = bf16[512,256]{1,0:T(8,128)(2,1)S(1)} collective-permute-done((bf16[512,256]{1,0:T(8,128)(2,1)S(1)}, bf16[512,256]{1,0:T(8,128)(2,1)S(1)}, u32[]{:S(2)}, u32[]{:S(2)}) %collective-permute-start.18) | collective-permute-done | bytes 262176 | tf_op jit(solution)/shard_map/ppermute | solution.py:70
  123.0 4.2 %collective-permute-done.16 = bf16[512,256]{1,0:T(8,128)(2,1)S(1)} collective-permute-done((bf16[512,256]{1,0:T(8,128)(2,1)S(1)}, bf16[512,256]{1,0:T(8,128)(2,1)S(1)}, u32[]{:S(2)}, u32[]{:S(2)}) %collective-permute-start.16) | collective-permute-done | bytes 262176 | tf_op jit(solution)/shard_map/ppermute | solution.py:70
  127.2 1.0 select_bitcast_fusion
  (12 shorter events, 0.0 us)
Async XLA Ops:
  0.0 2.5 %collective-permute-start = (f32[512,256]{1,0:T(8,128)}, f32[512,256]{1,0:T(8,128)S(1)}, u32[]{:S(2)}, u32[]{:S(2)}) collective-permute-start(f32[512,256]{1,0:T(8,128)} %bitcast.17), channel_id=1, source_target_pairs={{0,128},{128,0},{1,129},{129,1},{2,130},{130,2},{3,131},{131,3},{4... | collective-permute-start | bytes 1572872 | tf_op jit(solution)/shard_map/ppermute | solution.py:61
  0.0 2.5 %collective-permute-start.1 = (bf16[512,256]{1,0:T(8,128)(2,1)}, bf16[512,256]{1,0:T(8,128)(2,1)S(1)}, u32[]{:S(2)}, u32[]{:S(2)}) collective-permute-start(bf16[512,256]{1,0:T(8,128)(2,1)} %bitcast.19), channel_id=1, source_target_pairs={{0,128},{128,0},{1,129},{129,1},{2,130},{130,2},{3,131},{131,3},{4... | collective-permute-start | bytes 786440 | tf_op jit(solution)/shard_map/ppermute | solution.py:61
  4.7 12.9 %collective-permute-start.9 = (bf16[512,256]{1,0:T(8,128)(2,1)S(1)}, bf16[512,256]{1,0:T(8,128)(2,1)S(1)}, u32[]{:S(2)}, u32[]{:S(2)}) collective-permute-start(bf16[512,256]{1,0:T(8,128)(2,1)S(1)} %get-tuple-element.29.refs_7_.refs_3_), channel_id=1, source_target_pairs={{0,68},{1,69},{2,70},{3,71},{4,0},{5,1},{6,2},{7,3},{8,76},{9,77},... | collective-permute-start | bytes 786440 | tf_op jit(solution)/shard_map/ppermute | solution.py:70
  7.0 6.9 %collective-permute-start.5 = (bf16[256,256]{1,0:T(8,128)(2,1)S(1)}, bf16[256,256]{1,0:T(8,128)(2,1)S(1)}, u32[]{:S(2)}, u32[]{:S(2)}) collective-permute-start(bf16[256,256]{1,0:T(8,128)(2,1)S(1)} %get-tuple-element.28.refs_1_), channel_id=1, source_target_pairs={{0,56},{1,57},{2,58},{3,59},{4,60},{5,61},{6,62},{7,63},{8,0},{9,1... | collective-permute-start | bytes 393224 | tf_op jit(solution)/shard_map/ppermute | solution.py:70
  11.2 6.5 %collective-permute-start.2 = (bf16[256,256]{1,0:T(8,128)(2,1)S(1)}, bf16[256,256]{1,0:T(8,128)(2,1)S(1)}, u32[]{:S(2)}, u32[]{:S(2)}) collective-permute-start(bf16[256,256]{1,0:T(8,128)(2,1)S(1)} %get-tuple-element.28.refs_1_), channel_id=1, source_target_pairs={{0,8},{1,9},{2,10},{3,11},{4,12},{5,13},{6,14},{7,15},{8,16},{9,17... | collective-permute-start | bytes 393224 | tf_op jit(solution)/shard_map/ppermute | solution.py:70
  11.2 12.7 %collective-permute-start.11 = (bf16[512,256]{1,0:T(8,128)(2,1)S(1)}, bf16[512,256]{1,0:T(8,128)(2,1)S(1)}, u32[]{:S(2)}, u32[]{:S(2)}) collective-permute-start(bf16[512,256]{1,0:T(8,128)(2,1)S(1)} %get-tuple-element.29.refs_7_.refs_3_), channel_id=1, source_target_pairs={{0,4},{1,5},{2,6},{3,7},{4,64},{5,65},{6,66},{7,67},{8,12},{9,13},... | collective-permute-start | bytes 786440 | tf_op jit(solution)/shard_map/ppermute | solution.py:70
  13.9 6.5 %collective-permute-start.6 = (bf16[256,256]{1,0:T(8,128)(2,1)S(1)}, bf16[256,256]{1,0:T(8,128)(2,1)S(1)}, u32[]{:S(2)}, u32[]{:S(2)}) collective-permute-start(bf16[256,256]{1,0:T(8,128)(2,1)S(1)} %collective-permute-done.5.refs_2_), channel_id=1, source_target_pairs={{0,56},{1,57},{2,58},{3,59},{4,60},{5,61},{6,62},{7,63},{8,0},{9,1... | collective-permute-start | bytes 393224 | tf_op jit(solution)/shard_map/ppermute | solution.py:70
  17.6 6.2 %collective-permute-start.3 = (bf16[256,256]{1,0:T(8,128)(2,1)S(1)}, bf16[256,256]{1,0:T(8,128)(2,1)S(1)}, u32[]{:S(2)}, u32[]{:S(2)}) collective-permute-start(bf16[256,256]{1,0:T(8,128)(2,1)S(1)} %collective-permute-done.2.refs_3_), channel_id=1, source_target_pairs={{0,8},{1,9},{2,10},{3,11},{4,12},{5,13},{6,14},{7,15},{8,16},{9,17... | collective-permute-start | bytes 393224 | tf_op jit(solution)/shard_map/ppermute | solution.py:70
  17.6 12.4 %collective-permute-start.10 = (bf16[512,256]{1,0:T(8,128)(2,1)S(1)}, bf16[512,256]{1,0:T(8,128)(2,1)S(1)}, u32[]{:S(2)}, u32[]{:S(2)}) collective-permute-start(bf16[512,256]{1,0:T(8,128)(2,1)S(1)} %collective-permute-done.9.refs_8_.refs_4_), channel_id=1, source_target_pairs={{0,68},{1,69},{2,70},{3,71},{4,0},{5,1},{6,2},{7,3},{8,76},{9,77},... | collective-permute-start | bytes 786440 | tf_op jit(solution)/shard_map/ppermute | solution.py:70
  20.5 5.8 %collective-permute-start.7 = (bf16[256,256]{1,0:T(8,128)(2,1)S(1)}, bf16[256,256]{1,0:T(8,128)(2,1)S(1)}, u32[]{:S(2)}, u32[]{:S(2)}) collective-permute-start(bf16[256,256]{1,0:T(8,128)(2,1)S(1)} %collective-permute-done.6.refs_4_), channel_id=1, source_target_pairs={{0,56},{1,57},{2,58},{3,59},{4,60},{5,61},{6,62},{7,63},{8,0},{9,1... | collective-permute-start | bytes 393224 | tf_op jit(solution)/shard_map/ppermute | solution.py:70
  23.8 6.2 %collective-permute-start.4 = (bf16[256,256]{1,0:T(8,128)(2,1)S(1)}, bf16[256,256]{1,0:T(8,128)(2,1)S(1)}, u32[]{:S(2)}, u32[]{:S(2)}) collective-permute-start(bf16[256,256]{1,0:T(8,128)(2,1)S(1)} %collective-permute-done.3.refs_5_), channel_id=1, source_target_pairs={{0,8},{1,9},{2,10},{3,11},{4,12},{5,13},{6,14},{7,15},{8,16},{9,17... | collective-permute-start | bytes 393224 | tf_op jit(solution)/shard_map/ppermute | solution.py:70
  30.0 1.5 %collective-permute-start.12 = (bf16[512,256]{1,0:T(8,128)(2,1)S(1)}, bf16[512,256]{1,0:T(8,128)(2,1)S(1)}, u32[]{:S(2)}, u32[]{:S(2)}) collective-permute-start(bf16[512,256]{1,0:T(8,128)(2,1)S(1)} %collective-permute-done.9.refs_8_.refs_4_), channel_id=1, source_target_pairs={{0,128},{128,0},{1,129},{129,1},{2,130},{130,2},{3,131},{131,3},{4... | collective-permute-start | bytes 786440 | tf_op jit(solution)/shard_map/ppermute | solution.py:61
  30.0 1.9 %collective-permute-start.13 = (bf16[512,256]{1,0:T(8,128)(2,1)S(1)}, bf16[512,256]{1,0:T(8,128)(2,1)S(1)}, u32[]{:S(2)}, u32[]{:S(2)}) collective-permute-start(bf16[512,256]{1,0:T(8,128)(2,1)S(1)} %collective-permute-done.10.refs_9_.refs_5_), channel_id=1, source_target_pairs={{0,128},{128,0},{1,129},{129,1},{2,130},{130,2},{3,131},{131,3},{4... | collective-permute-start | bytes 786440 | tf_op jit(solution)/shard_map/ppermute | solution.py:61
  30.5 1.8 %collective-permute-start.14 = (bf16[512,256]{1,0:T(8,128)(2,1)S(1)}, bf16[512,256]{1,0:T(8,128)(2,1)S(1)}, u32[]{:S(2)}, u32[]{:S(2)}) collective-permute-start(bf16[512,256]{1,0:T(8,128)(2,1)S(1)} %collective-permute-done.11.refs_10_.refs_6_), channel_id=1, source_target_pairs={{0,128},{128,0},{1,129},{129,1},{2,130},{130,2},{3,131},{131,3},{4... | collective-permute-start | bytes 786440 | tf_op jit(solution)/shard_map/ppermute | solution.py:61
  30.5 5.9 %collective-permute-start.8 = (bf16[256,256]{1,0:T(8,128)(2,1)S(1)}, bf16[256,256]{1,0:T(8,128)(2,1)S(1)}, u32[]{:S(2)}, u32[]{:S(2)}) collective-permute-start(bf16[256,256]{1,0:T(8,128)(2,1)S(1)} %collective-permute-done.7.refs_6_), channel_id=1, source_target_pairs={{0,56},{1,57},{2,58},{3,59},{4,60},{5,61},{6,62},{7,63},{8,0},{9,1... | collective-permute-start | bytes 393224 | tf_op jit(solution)/shard_map/ppermute | solution.py:70
  111.9 15.3 %copy-start = (f32[1,512,256]{2,1,0:T(8,128)S(1)}, f32[1,512,256]{2,1,0:T(8,128)}, u32[]{:S(2)}) copy-start(f32[1,512,256]{2,1,0:T(8,128)} %param.4) | copy-start | bytes 1572868
  111.9 2.0 %collective-permute-start.15 = (bf16[2,512,256]{2,1,0:T(8,128)(2,1)S(1)}, bf16[2,512,256]{2,1,0:T(8,128)(2,1)S(1)}, u32[]{:S(2)}, u32[]{:S(2)}) collective-permute-start(bf16[2,512,256]{2,1,0:T(8,128)(2,1)S(1)} %shard_map.46), channel_id=1, source_target_pairs={{0,128},{128,0},{1,129},{129,1},{2,130},{130,2},{3,131},{131,3},{4... | collective-permute-start | bytes 1572872 | tf_op jit(solution)/shard_map/ppermute | solution.py:61
  114.0 7.7 %collective-permute-start.17 = (bf16[512,256]{1,0:T(8,128)(2,1)S(1)}, bf16[512,256]{1,0:T(8,128)(2,1)S(1)}, u32[]{:S(2)}, u32[]{:S(2)}) collective-permute-start(bf16[512,256]{1,0:T(8,128)(2,1)S(1)} %get-tuple-element.51), channel_id=1, source_target_pairs={{128,4},{129,5},{130,6},{131,7},{132,64},{133,65},{134,66},{135,67... | collective-permute-start | bytes 786440 | tf_op jit(solution)/shard_map/ppermute | solution.py:70
  115.3 7.7 %collective-permute-start.18 = (bf16[512,256]{1,0:T(8,128)(2,1)S(1)}, bf16[512,256]{1,0:T(8,128)(2,1)S(1)}, u32[]{:S(2)}, u32[]{:S(2)}) collective-permute-start(bf16[512,256]{1,0:T(8,128)(2,1)S(1)} %get-tuple-element.52), channel_id=1, source_target_pairs={{128,68},{129,69},{130,70},{131,71},{132,0},{133,1},{134,2},{135,3... | collective-permute-start | bytes 786440 | tf_op jit(solution)/shard_map/ppermute | solution.py:70
  116.6 10.5 %collective-permute-start.16 = (bf16[512,256]{1,0:T(8,128)(2,1)S(1)}, bf16[512,256]{1,0:T(8,128)(2,1)S(1)}, u32[]{:S(2)}, u32[]{:S(2)}) collective-permute-start(bf16[512,256]{1,0:T(8,128)(2,1)S(1)} %get-tuple-element.52), channel_id=1, source_target_pairs={{0,64},{1,65},{2,66},{3,67},{4,68},{5,69},{6,70},{7,71},{8,72},{9,... | collective-permute-start | bytes 786440 | tf_op jit(solution)/shard_map/ppermute | solution.py:70

commit v9 on v8

--- a/solution.py
+++ b/solution.py
@@ -147,7 +147,7 @@
 
 
 def unit_call(place, features, other_features, mask, own_master, other_master):
-    rows = BLOCK // 2
+    rows = BLOCK
     picked = pl.BlockSpec((OWN_ROWS, 256), lambda i, place: (place[1] % 2 * 2 + place[0], 0))
     part = pl.BlockSpec((rows, 256), lambda i, place: (i, 0))
     return pl.pallas_call(
@@ -160,7 +160,7 @@
         ],
         grid_spec=pltpu.PrefetchScalarGridSpec(
             num_scalar_prefetch=1,
-            grid=(2,),
+            grid=(1,),
             in_specs=[
                 picked,
                 picked,
@@ -243,7 +243,7 @@
         parts_ref, exp_ref, extra_ref, out_ref, scale_ref = refs
     else:
         parts_ref, exp_ref, out_ref, scale_ref = refs
-    scale = 1.0 / jnp.sum(parts_ref[...], axis=0)
+    scale = 1.0 / jnp.sum(parts_ref[...].astype(jnp.float32), axis=0)
     scale_ref[...] = scale
     totals = [jnp.zeros((8, 128), jnp.float32) for _ in range(N_Z)]
     for j in range(COLS // 128):
@@ -272,7 +272,7 @@
         folded = sum(exp_ref[k, rows, :] * scale[k : k + 1, :] for k in range(N_Z))
         vector_ref[j : j + 1, :] = to_row(jnp.sum(folded, axis=1, keepdims=True))
     for k in range(N_COLGRP):
-        out_ref[k] = vector_ref[...]
+        out_ref[k] = vector_ref[...].astype(jnp.bfloat16)
 
 
 def grad_kernel(
@@ -410,7 +410,7 @@
         if not last:
             col_parts, *rest = call(
                 functools.partial(col_kernel, first),
-                [shape((N_COLGRP, 16, 128))] + [shape((8, 128))] * first,
+                [shape((N_COLGRP, 16, 128), jnp.bfloat16)] + [shape((8, 128))] * first,
                 [pltpu.VMEM((16, 128), jnp.float32)],
                 row_parts,
                 teacher_exp,

time: 129 us -> 128 us (level)
  no operation moved by 1% of the time
where the time goes in v9:
time: 128 us
  blocking collectives  68.3 us (53%)
  starting transfers between devices  24.7 us (19%)
  waiting for transfers between devices  20 us (16%)
  Pallas kernels  13.9 us (11%)
    all_to_all x6, blocking collectives, exchange(): lax.all_to_all(blocks, AXES, 0, 0, axis_index_groups=groups, tiled=True)  68.3 us
    ppermute x13, starting transfers between devices, permuted(): return lax.ppermute(block, AXES, route)  23.6 us
    ppermute x13, waiting for transfers between devices, permuted(): return lax.ppermute(block, AXES, route)  15.9 us
    pallas_call x9, Pallas kernels, call(): pl.pallas_call(kernel, out_shape=outs, in_specs=[smem if a.ndim == 1 else...  11.7 us
    ppermute x6, waiting for transfers between devices, swapped(): return lax.ppermute(block, 'grp', [(0, 1), (1, 0)])  4.08 us
  transfers between devices with their start and end apart: 19, of which 12 were waited for; matrix products, arithmetic and copies ran while one was open for 0% of the time, Pallas kernels for 4%

profile of v9, /device:TPU:2, one launch (start us, length us, event | category | flops | bytes accessed | tf_op | source)
XLA Modules:
  0.0 128.1 jit_solution(15150203999105448284)
XLA Ops:
  0.0 0.5 collective-permute-start.1
  0.5 0.1 pad_add_fusion.place_ref.refs_0_
  0.6 1.9 %collective-permute-done.1.other_features_ref = bf16[512,256]{1,0:T(8,128)(2,1)S(1)} collective-permute-done((bf16[512,256]{1,0:T(8,128)(2,1)}, bf16[512,256]{1,0:T(8,128)(2,1)S(1)}, u32[]{:S(2)}, u32[]{:S(2)}) %collective-permute-start.1) | collective-permute-done | bytes 262176 | tf_op jit(solution)/shard_map/ppermute | solution.py:61
  2.5 2.2 %shard_map.37 = (bf16[256,256]{1,0:T(8,128)(2,1)S(1)}, bf16[8,128]{1,0:T(8,128)(2,1)S(1)}, bf16[512,256]{1,0:T(8,128)(2,1)S(1)}, bf16[512,256]{1,0:T(8,128)(2,1)S(1)}) custom-call(s32[3]{0:T(128)S(1)} %pad_add_fusion.place_ref.refs_0_, bf16[512,256]{1,0:T(8,128)(2,1)} %bitcast.20, bf16[512,256]{1,0:T(8,128)(2,1)S(1)} %collective-permute-done.1.other_features_ref, ...), custom_call_target="tpu_custom_call" | custom-call | tf_op jit(solution)/shard_map/pallas_call | solution.py:153
  4.7 2.3 %collective-permute-start.9 = (bf16[512,256]{1,0:T(8,128)(2,1)S(1)}, bf16[512,256]{1,0:T(8,128)(2,1)S(1)}, u32[]{:S(2)}, u32[]{:S(2)}) collective-permute-start(bf16[512,256]{1,0:T(8,128)(2,1)S(1)} %get-tuple-element.29.refs_7_.refs_3_), channel_id=1, source_target_pairs={{0,68},{1,69},{2,70},{3,71},{4,0},{5,1},{6,2},{7,3},{8,76},{9,77},... | collective-permute-start | bytes 786440 | tf_op jit(solution)/shard_map/ppermute | solution.py:70
  7.0 4.1 %collective-permute-start.5 = (bf16[256,256]{1,0:T(8,128)(2,1)S(1)}, bf16[256,256]{1,0:T(8,128)(2,1)S(1)}, u32[]{:S(2)}, u32[]{:S(2)}) collective-permute-start(bf16[256,256]{1,0:T(8,128)(2,1)S(1)} %get-tuple-element.28.refs_1_), channel_id=1, source_target_pairs={{0,56},{1,57},{2,58},{3,59},{4,60},{5,61},{6,62},{7,63},{8,0},{9,1... | collective-permute-start | bytes 393224 | tf_op jit(solution)/shard_map/ppermute | solution.py:70
  11.1 1.5 %collective-permute-start.11 = (bf16[512,256]{1,0:T(8,128)(2,1)S(1)}, bf16[512,256]{1,0:T(8,128)(2,1)S(1)}, u32[]{:S(2)}, u32[]{:S(2)}) collective-permute-start(bf16[512,256]{1,0:T(8,128)(2,1)S(1)} %get-tuple-element.29.refs_7_.refs_3_), channel_id=1, source_target_pairs={{0,4},{1,5},{2,6},{3,7},{4,64},{5,65},{6,66},{7,67},{8,12},{9,13},... | collective-permute-start | bytes 786440 | tf_op jit(solution)/shard_map/ppermute | solution.py:70
  12.6 1.3 %collective-permute-done.5.refs_2_ = bf16[256,256]{1,0:T(8,128)(2,1)S(1)} collective-permute-done((bf16[256,256]{1,0:T(8,128)(2,1)S(1)}, bf16[256,256]{1,0:T(8,128)(2,1)S(1)}, u32[]{:S(2)}, u32[]{:S(2)}) %collective-permute-start.5) | collective-permute-done | bytes 131104 | tf_op jit(solution)/shard_map/ppermute | solution.py:70
  13.9 3.7 %collective-permute-start.6 = (bf16[256,256]{1,0:T(8,128)(2,1)S(1)}, bf16[256,256]{1,0:T(8,128)(2,1)S(1)}, u32[]{:S(2)}, u32[]{:S(2)}) collective-permute-start(bf16[256,256]{1,0:T(8,128)(2,1)S(1)} %collective-permute-done.5.refs_2_), channel_id=1, source_target_pairs={{0,56},{1,57},{2,58},{3,59},{4,60},{5,61},{6,62},{7,63},{8,0},{9,1... | collective-permute-start | bytes 393224 | tf_op jit(solution)/shard_map/ppermute | solution.py:70
  17.6 2.8 %collective-permute-start.10 = (bf16[512,256]{1,0:T(8,128)(2,1)S(1)}, bf16[512,256]{1,0:T(8,128)(2,1)S(1)}, u32[]{:S(2)}, u32[]{:S(2)}) collective-permute-start(bf16[512,256]{1,0:T(8,128)(2,1)S(1)} %collective-permute-done.9.refs_8_.refs_4_), channel_id=1, source_target_pairs={{0,68},{1,69},{2,70},{3,71},{4,0},{5,1},{6,2},{7,3},{8,76},{9,77},... | collective-permute-start | bytes 786440 | tf_op jit(solution)/shard_map/ppermute | solution.py:70
  20.5 3.3 %collective-permute-start.7 = (bf16[256,256]{1,0:T(8,128)(2,1)S(1)}, bf16[256,256]{1,0:T(8,128)(2,1)S(1)}, u32[]{:S(2)}, u32[]{:S(2)}) collective-permute-start(bf16[256,256]{1,0:T(8,128)(2,1)S(1)} %collective-permute-done.6.refs_4_), channel_id=1, source_target_pairs={{0,56},{1,57},{2,58},{3,59},{4,60},{5,61},{6,62},{7,63},{8,0},{9,1... | collective-permute-start | bytes 393224 | tf_op jit(solution)/shard_map/ppermute | solution.py:70
  23.8 0.0 collective-permute-done.3.refs_5_
  23.8 2.5 %collective-permute-done.7.refs_6_ = bf16[256,256]{1,0:T(8,128)(2,1)S(1)} collective-permute-done((bf16[256,256]{1,0:T(8,128)(2,1)S(1)}, bf16[256,256]{1,0:T(8,128)(2,1)S(1)}, u32[]{:S(2)}, u32[]{:S(2)}) %collective-permute-start.7) | collective-permute-done | bytes 131104 | tf_op jit(solution)/shard_map/ppermute | solution.py:70
  26.3 3.7 %collective-permute-done.4.refs_1_ = bf16[256,256]{1,0:T(8,128)(2,1)S(1)} collective-permute-done((bf16[256,256]{1,0:T(8,128)(2,1)S(1)}, bf16[256,256]{1,0:T(8,128)(2,1)S(1)}, u32[]{:S(2)}, u32[]{:S(2)}) %collective-permute-start.4) | collective-permute-done | bytes 131104 | tf_op jit(solution)/shard_map/ppermute | solution.py:70
  30.0 0.5 collective-permute-start.13
  30.5 0.0 collective-permute-start.14
  30.5 0.1 collective-permute-start.8
  30.6 0.9 collective-permute-done.12.refs_12_.refs_8_
  31.5 0.4 collective-permute-done.13.refs_13_.refs_9_
  31.9 0.4 collective-permute-done.14.refs_14_.refs_10_
  32.3 3.3 %shard_map.38 = (f32[16,128]{1,0:T(8,128)S(1)}, f32[8,2048,128]{2,1,0:T(8,128)S(1)}, f32[8,2048,128]{2,1,0:T(8,128)S(1)}, f32[8,128]{1,0:T(8,128)S(1)}, bf16[1024,256]{1,0:T(8,128)(2,1)S(1)}) custom-call(s32[3]{0:T(128)S(1)} %pad_add_fusion.place_ref.refs_0_, bf16[256,256]{1,0:T(8,128)(2,1)S(1)} %get-tuple-element.28.refs_1_, ...), custom_call_target="tpu_custom_call" | custom-call | flops 1610612736 | bytes 8388608 | tf_op jit(solution)/shard_map/pallas_call | solution.py:318
  35.5 0.9 collective-permute-done.8.refs_2_
  36.4 1.6 %shard_map.39 = (f32[8,16,128]{2,1,0:T(8,128)S(1)}, f32[8,2048,128]{2,1,0:T(8,128)S(1)}, f32[8,2048,128]{2,1,0:T(8,128)S(1)}, f32[8,128]{1,0:T(8,128)S(1)}, bf16[1024,256]{1,0:T(8,128)(2,1)S(1)}) custom-call(s32[3]{0:T(128)S(1)} %pad_add_fusion.place_ref.refs_0_, ...), custom_call_target="tpu_custom_call", output_to_operand_aliasing={{1}: (12, {}), {2}: (13, {}), {3}: (14, {}), {4}: (15, {})} | custom-call | flops 536870912 | bytes 8388608 | tf_op jit(solution)/shard_map/pallas_call | solution.py:318
  38.0 9.2 %all_to_all.30.refs_0_ = f32[8,16,128]{2,1,0:T(8,128)S(1)} all-to-all(f32[8,16,128]{2,1,0:T(8,128)S(1)} %get-tuple-element.39), channel_id=1, replica_groups={{0,4,64,68,128,132,192,196},{1,5,65,69,129,133,193,197},{2,6,66,70,130,..., dimensions={0} | all-to-all | bytes 131072 | tf_op jit(solution)/shard_map/all_to_all | solution.py:57
  47.2 0.8 shard_map.40
  48.1 16.5 %all_to_all.31.refs_0_ = bf16[32,16,128]{2,1,0:T(8,128)(2,1)S(1)} all-to-all(bf16[32,16,128]{2,1,0:T(8,128)(2,1)S(1)} %get-tuple-element.42), channel_id=1, replica_groups={{0,1,2,3,8,9,10,11,16,17,18,19,24,25,26,27,32,33,34,35,40,41,42,43,48,4..., dimensions={0} | all-to-all | bytes 262144 | tf_op jit(solution)/shard_map/all_to_all | solution.py:57
  64.5 0.7 shard_map.41
  65.3 7.6 %all_to_all.32.refs_0_ = bf16[8,16,128]{2,1,0:T(8,128)(2,1)S(1)} all-to-all(bf16[8,16,128]{2,1,0:T(8,128)(2,1)S(1)} %get-tuple-element.43), channel_id=1, replica_groups={{0,4,64,68,128,132,192,196},{1,5,65,69,129,133,193,197},{2,6,66,70,130,..., dimensions={0} | all-to-all | bytes 65536 | tf_op jit(solution)/shard_map/all_to_all | solution.py:57
  72.9 1.0 shard_map.42
  73.9 13.2 %all_to_all.33.refs_0_ = bf16[32,8,128]{2,1,0:T(8,128)(2,1)S(1)} all-to-all(bf16[32,8,128]{2,1,0:T(8,128)(2,1)S(1)} %get-tuple-element.44), channel_id=1, replica_groups={{0,1,2,3,8,9,10,11,16,17,18,19,24,25,26,27,32,33,34,35,40,41,42,43,48,4..., dimensions={0} | all-to-all | bytes 131072 | tf_op jit(solution)/shard_map/all_to_all | solution.py:57
  87.1 0.7 shard_map.43
  87.9 7.7 %all_to_all.34.refs_0_ = bf16[8,16,128]{2,1,0:T(8,128)(2,1)S(1)} all-to-all(bf16[8,16,128]{2,1,0:T(8,128)(2,1)S(1)} %shard_map.43), channel_id=1, replica_groups={{0,4,64,68,128,132,192,196},{1,5,65,69,129,133,193,197},{2,6,66,70,130,..., dimensions={0} | all-to-all | bytes 65536 | tf_op jit(solution)/shard_map/all_to_all | solution.py:57
  95.6 0.7 shard_map.44
  96.2 14.1 %all_to_all.35.parts_ref = bf16[32,16,128]{2,1,0:T(8,128)(2,1)S(1)} all-to-all(bf16[32,16,128]{2,1,0:T(8,128)(2,1)S(1)} %get-tuple-element.46), channel_id=1, replica_groups={{0,1,2,3,8,9,10,11,16,17,18,19,24,25,26,27,32,33,34,35,40,41,42,43,48,4..., dimensions={0} | all-to-all | bytes 262144 | tf_op jit(solution)/shard_map/all_to_all | solution.py:57
  110.3 1.4 %shard_map.46 = bf16[2,512,256]{2,1,0:T(8,128)(2,1)S(1)} custom-call(s32[3]{0:T(128)S(1)} %pad_add_fusion.place_ref.refs_0_, bf16[32,16,128]{2,1,0:T(8,128)(2,1)S(1)} %all_to_all.35.parts_ref, f32[16,128]{1,0:T(8,128)S(1)} %get-tuple-element.47.scale_ref, f32[8,128]{1,0:T(8,128)S(1)} %get-tuple-element.48.weight_ref, ...), custom_call_target="tpu_custom_call" | custom-call | flops 536870912 | bytes 8388608 | tf_op jit(solution)/shard_map/pallas_call | solution.py:318
  111.7 0.0 copy-start
  111.7 0.1 collective-permute-start.15
  111.8 1.4 %shard_map.45 = f32[2,512,256]{2,1,0:T(8,128)S(1)} custom-call(s32[3]{0:T(128)S(1)} %pad_add_fusion.place_ref.refs_0_, bf16[32,16,128]{2,1,0:T(8,128)(2,1)S(1)} %all_to_all.35.parts_ref, f32[16,128]{1,0:T(8,128)S(1)} %get-tuple-element.47.scale_ref, f32[8,128]{1,0:T(8,128)S(1)} %get-tuple-element.48.weight_ref, ...), custom_call_target="tpu_custom_call" | custom-call | flops 536870912 | bytes 8388608 | tf_op jit(solution)/shard_map/pallas_call | solution.py:318
  113.3 0.5 collective-permute-done.15
  113.7 0.1 convert_add_fusion
  113.9 0.1 fusion
  113.9 1.3 %collective-permute-start.17 = (bf16[512,256]{1,0:T(8,128)(2,1)S(1)}, bf16[512,256]{1,0:T(8,128)(2,1)S(1)}, u32[]{:S(2)}, u32[]{:S(2)}) collective-permute-start(bf16[512,256]{1,0:T(8,128)(2,1)S(1)} %get-tuple-element.51), channel_id=1, source_target_pairs={{128,4},{129,5},{130,6},{131,7},{132,64},{133,65},{134,66},{135,67... | collective-permute-start | bytes 786440 | tf_op jit(solution)/shard_map/ppermute | solution.py:70
  115.2 1.3 %collective-permute-start.18 = (bf16[512,256]{1,0:T(8,128)(2,1)S(1)}, bf16[512,256]{1,0:T(8,128)(2,1)S(1)}, u32[]{:S(2)}, u32[]{:S(2)}) collective-permute-start(bf16[512,256]{1,0:T(8,128)(2,1)S(1)} %get-tuple-element.52), channel_id=1, source_target_pairs={{128,68},{129,69},{130,70},{131,71},{132,0},{133,1},{134,2},{135,3... | collective-permute-start | bytes 786440 | tf_op jit(solution)/shard_map/ppermute | solution.py:70
  116.5 3.1 %collective-permute-start.16 = (bf16[512,256]{1,0:T(8,128)(2,1)S(1)}, bf16[512,256]{1,0:T(8,128)(2,1)S(1)}, u32[]{:S(2)}, u32[]{:S(2)}) collective-permute-start(bf16[512,256]{1,0:T(8,128)(2,1)S(1)} %get-tuple-element.52), channel_id=1, source_target_pairs={{0,64},{1,65},{2,66},{3,67},{4,68},{5,69},{6,70},{7,71},{8,72},{9,... | collective-permute-start | bytes 786440 | tf_op jit(solution)/shard_map/ppermute | solution.py:70
  119.6 2.0 %collective-permute-done.17 = bf16[512,256]{1,0:T(8,128)(2,1)S(1)} collective-permute-done((bf16[512,256]{1,0:T(8,128)(2,1)S(1)}, bf16[512,256]{1,0:T(8,128)(2,1)S(1)}, u32[]{:S(2)}, u32[]{:S(2)}) %collective-permute-start.17) | collective-permute-done | bytes 262176 | tf_op jit(solution)/shard_map/ppermute | solution.py:70
  121.6 1.3 %collective-permute-done.18 = bf16[512,256]{1,0:T(8,128)(2,1)S(1)} collective-permute-done((bf16[512,256]{1,0:T(8,128)(2,1)S(1)}, bf16[512,256]{1,0:T(8,128)(2,1)S(1)}, u32[]{:S(2)}, u32[]{:S(2)}) %collective-permute-start.18) | collective-permute-done | bytes 262176 | tf_op jit(solution)/shard_map/ppermute | solution.py:70
  122.9 4.2 %collective-permute-done.16 = bf16[512,256]{1,0:T(8,128)(2,1)S(1)} collective-permute-done((bf16[512,256]{1,0:T(8,128)(2,1)S(1)}, bf16[512,256]{1,0:T(8,128)(2,1)S(1)}, u32[]{:S(2)}, u32[]{:S(2)}) %collective-permute-start.16) | collective-permute-done | bytes 262176 | tf_op jit(solution)/shard_map/ppermute | solution.py:70
  127.2 1.0 select_bitcast_fusion
  (12 shorter events, 0.0 us)
Async XLA Ops:
  0.0 2.5 %collective-permute-start = (f32[512,256]{1,0:T(8,128)}, f32[512,256]{1,0:T(8,128)S(1)}, u32[]{:S(2)}, u32[]{:S(2)}) collective-permute-start(f32[512,256]{1,0:T(8,128)} %bitcast.17), channel_id=1, source_target_pairs={{0,128},{128,0},{1,129},{129,1},{2,130},{130,2},{3,131},{131,3},{4... | collective-permute-start | bytes 1572872 | tf_op jit(solution)/shard_map/ppermute | solution.py:61
  0.0 2.5 %collective-permute-start.1 = (bf16[512,256]{1,0:T(8,128)(2,1)}, bf16[512,256]{1,0:T(8,128)(2,1)S(1)}, u32[]{:S(2)}, u32[]{:S(2)}) collective-permute-start(bf16[512,256]{1,0:T(8,128)(2,1)} %bitcast.19), channel_id=1, source_target_pairs={{0,128},{128,0},{1,129},{129,1},{2,130},{130,2},{3,131},{131,3},{4... | collective-permute-start | bytes 786440 | tf_op jit(solution)/shard_map/ppermute | solution.py:61
  4.7 12.9 %collective-permute-start.9 = (bf16[512,256]{1,0:T(8,128)(2,1)S(1)}, bf16[512,256]{1,0:T(8,128)(2,1)S(1)}, u32[]{:S(2)}, u32[]{:S(2)}) collective-permute-start(bf16[512,256]{1,0:T(8,128)(2,1)S(1)} %get-tuple-element.29.refs_7_.refs_3_), channel_id=1, source_target_pairs={{0,68},{1,69},{2,70},{3,71},{4,0},{5,1},{6,2},{7,3},{8,76},{9,77},... | collective-permute-start | bytes 786440 | tf_op jit(solution)/shard_map/ppermute | solution.py:70
  7.0 6.9 %collective-permute-start.5 = (bf16[256,256]{1,0:T(8,128)(2,1)S(1)}, bf16[256,256]{1,0:T(8,128)(2,1)S(1)}, u32[]{:S(2)}, u32[]{:S(2)}) collective-permute-start(bf16[256,256]{1,0:T(8,128)(2,1)S(1)} %get-tuple-element.28.refs_1_), channel_id=1, source_target_pairs={{0,56},{1,57},{2,58},{3,59},{4,60},{5,61},{6,62},{7,63},{8,0},{9,1... | collective-permute-start | bytes 393224 | tf_op jit(solution)/shard_map/ppermute | solution.py:70
  11.1 6.5 %collective-permute-start.2 = (bf16[256,256]{1,0:T(8,128)(2,1)S(1)}, bf16[256,256]{1,0:T(8,128)(2,1)S(1)}, u32[]{:S(2)}, u32[]{:S(2)}) collective-permute-start(bf16[256,256]{1,0:T(8,128)(2,1)S(1)} %get-tuple-element.28.refs_1_), channel_id=1, source_target_pairs={{0,8},{1,9},{2,10},{3,11},{4,12},{5,13},{6,14},{7,15},{8,16},{9,17... | collective-permute-start | bytes 393224 | tf_op jit(solution)/shard_map/ppermute | solution.py:70
  11.1 12.7 %collective-permute-start.11 = (bf16[512,256]{1,0:T(8,128)(2,1)S(1)}, bf16[512,256]{1,0:T(8,128)(2,1)S(1)}, u32[]{:S(2)}, u32[]{:S(2)}) collective-permute-start(bf16[512,256]{1,0:T(8,128)(2,1)S(1)} %get-tuple-element.29.refs_7_.refs_3_), channel_id=1, source_target_pairs={{0,4},{1,5},{2,6},{3,7},{4,64},{5,65},{6,66},{7,67},{8,12},{9,13},... | collective-permute-start | bytes 786440 | tf_op jit(solution)/shard_map/ppermute | solution.py:70
  13.9 6.5 %collective-permute-start.6 = (bf16[256,256]{1,0:T(8,128)(2,1)S(1)}, bf16[256,256]{1,0:T(8,128)(2,1)S(1)}, u32[]{:S(2)}, u32[]{:S(2)}) collective-permute-start(bf16[256,256]{1,0:T(8,128)(2,1)S(1)} %collective-permute-done.5.refs_2_), channel_id=1, source_target_pairs={{0,56},{1,57},{2,58},{3,59},{4,60},{5,61},{6,62},{7,63},{8,0},{9,1... | collective-permute-start | bytes 393224 | tf_op jit(solution)/shard_map/ppermute | solution.py:70
  17.6 6.2 %collective-permute-start.3 = (bf16[256,256]{1,0:T(8,128)(2,1)S(1)}, bf16[256,256]{1,0:T(8,128)(2,1)S(1)}, u32[]{:S(2)}, u32[]{:S(2)}) collective-permute-start(bf16[256,256]{1,0:T(8,128)(2,1)S(1)} %collective-permute-done.2.refs_3_), channel_id=1, source_target_pairs={{0,8},{1,9},{2,10},{3,11},{4,12},{5,13},{6,14},{7,15},{8,16},{9,17... | collective-permute-start | bytes 393224 | tf_op jit(solution)/shard_map/ppermute | solution.py:70
  17.6 12.4 %collective-permute-start.10 = (bf16[512,256]{1,0:T(8,128)(2,1)S(1)}, bf16[512,256]{1,0:T(8,128)(2,1)S(1)}, u32[]{:S(2)}, u32[]{:S(2)}) collective-permute-start(bf16[512,256]{1,0:T(8,128)(2,1)S(1)} %collective-permute-done.9.refs_8_.refs_4_), channel_id=1, source_target_pairs={{0,68},{1,69},{2,70},{3,71},{4,0},{5,1},{6,2},{7,3},{8,76},{9,77},... | collective-permute-start | bytes 786440 | tf_op jit(solution)/shard_map/ppermute | solution.py:70
  20.5 5.8 %collective-permute-start.7 = (bf16[256,256]{1,0:T(8,128)(2,1)S(1)}, bf16[256,256]{1,0:T(8,128)(2,1)S(1)}, u32[]{:S(2)}, u32[]{:S(2)}) collective-permute-start(bf16[256,256]{1,0:T(8,128)(2,1)S(1)} %collective-permute-done.6.refs_4_), channel_id=1, source_target_pairs={{0,56},{1,57},{2,58},{3,59},{4,60},{5,61},{6,62},{7,63},{8,0},{9,1... | collective-permute-start | bytes 393224 | tf_op jit(solution)/shard_map/ppermute | solution.py:70
  23.8 6.2 %collective-permute-start.4 = (bf16[256,256]{1,0:T(8,128)(2,1)S(1)}, bf16[256,256]{1,0:T(8,128)(2,1)S(1)}, u32[]{:S(2)}, u32[]{:S(2)}) collective-permute-start(bf16[256,256]{1,0:T(8,128)(2,1)S(1)} %collective-permute-done.3.refs_5_), channel_id=1, source_target_pairs={{0,8},{1,9},{2,10},{3,11},{4,12},{5,13},{6,14},{7,15},{8,16},{9,17... | collective-permute-start | bytes 393224 | tf_op jit(solution)/shard_map/ppermute | solution.py:70
  30.0 1.5 %collective-permute-start.12 = (bf16[512,256]{1,0:T(8,128)(2,1)S(1)}, bf16[512,256]{1,0:T(8,128)(2,1)S(1)}, u32[]{:S(2)}, u32[]{:S(2)}) collective-permute-start(bf16[512,256]{1,0:T(8,128)(2,1)S(1)} %collective-permute-done.9.refs_8_.refs_4_), channel_id=1, source_target_pairs={{0,128},{128,0},{1,129},{129,1},{2,130},{130,2},{3,131},{131,3},{4... | collective-permute-start | bytes 786440 | tf_op jit(solution)/shard_map/ppermute | solution.py:61
  30.0 1.9 %collective-permute-start.13 = (bf16[512,256]{1,0:T(8,128)(2,1)S(1)}, bf16[512,256]{1,0:T(8,128)(2,1)S(1)}, u32[]{:S(2)}, u32[]{:S(2)}) collective-permute-start(bf16[512,256]{1,0:T(8,128)(2,1)S(1)} %collective-permute-done.10.refs_9_.refs_5_), channel_id=1, source_target_pairs={{0,128},{128,0},{1,129},{129,1},{2,130},{130,2},{3,131},{131,3},{4... | collective-permute-start | bytes 786440 | tf_op jit(solution)/shard_map/ppermute | solution.py:61
  30.5 1.8 %collective-permute-start.14 = (bf16[512,256]{1,0:T(8,128)(2,1)S(1)}, bf16[512,256]{1,0:T(8,128)(2,1)S(1)}, u32[]{:S(2)}, u32[]{:S(2)}) collective-permute-start(bf16[512,256]{1,0:T(8,128)(2,1)S(1)} %collective-permute-done.11.refs_10_.refs_6_), channel_id=1, source_target_pairs={{0,128},{128,0},{1,129},{129,1},{2,130},{130,2},{3,131},{131,3},{4... | collective-permute-start | bytes 786440 | tf_op jit(solution)/shard_map/ppermute | solution.py:61
  30.5 5.9 %collective-permute-start.8 = (bf16[256,256]{1,0:T(8,128)(2,1)S(1)}, bf16[256,256]{1,0:T(8,128)(2,1)S(1)}, u32[]{:S(2)}, u32[]{:S(2)}) collective-permute-start(bf16[256,256]{1,0:T(8,128)(2,1)S(1)} %collective-permute-done.7.refs_6_), channel_id=1, source_target_pairs={{0,56},{1,57},{2,58},{3,59},{4,60},{5,61},{6,62},{7,63},{8,0},{9,1... | collective-permute-start | bytes 393224 | tf_op jit(solution)/shard_map/ppermute | solution.py:70
  111.7 15.4 %copy-start = (f32[1,512,256]{2,1,0:T(8,128)S(1)}, f32[1,512,256]{2,1,0:T(8,128)}, u32[]{:S(2)}) copy-start(f32[1,512,256]{2,1,0:T(8,128)} %param.4) | copy-start | bytes 1572868
  111.7 2.0 %collective-permute-start.15 = (bf16[2,512,256]{2,1,0:T(8,128)(2,1)S(1)}, bf16[2,512,256]{2,1,0:T(8,128)(2,1)S(1)}, u32[]{:S(2)}, u32[]{:S(2)}) collective-permute-start(bf16[2,512,256]{2,1,0:T(8,128)(2,1)S(1)} %shard_map.46), channel_id=1, source_target_pairs={{0,128},{128,0},{1,129},{129,1},{2,130},{130,2},{3,131},{131,3},{4... | collective-permute-start | bytes 1572872 | tf_op jit(solution)/shard_map/ppermute | solution.py:61
  113.9 7.7 %collective-permute-start.17 = (bf16[512,256]{1,0:T(8,128)(2,1)S(1)}, bf16[512,256]{1,0:T(8,128)(2,1)S(1)}, u32[]{:S(2)}, u32[]{:S(2)}) collective-permute-start(bf16[512,256]{1,0:T(8,128)(2,1)S(1)} %get-tuple-element.51), channel_id=1, source_target_pairs={{128,4},{129,5},{130,6},{131,7},{132,64},{133,65},{134,66},{135,67... | collective-permute-start | bytes 786440 | tf_op jit(solution)/shard_map/ppermute | solution.py:70
  115.2 7.7 %collective-permute-start.18 = (bf16[512,256]{1,0:T(8,128)(2,1)S(1)}, bf16[512,256]{1,0:T(8,128)(2,1)S(1)}, u32[]{:S(2)}, u32[]{:S(2)}) collective-permute-start(bf16[512,256]{1,0:T(8,128)(2,1)S(1)} %get-tuple-element.52), channel_id=1, source_target_pairs={{128,68},{129,69},{130,70},{131,71},{132,0},{133,1},{134,2},{135,3... | collective-permute-start | bytes 786440 | tf_op jit(solution)/shard_map/ppermute | solution.py:70
  116.5 10.6 %collective-permute-start.16 = (bf16[512,256]{1,0:T(8,128)(2,1)S(1)}, bf16[512,256]{1,0:T(8,128)(2,1)S(1)}, u32[]{:S(2)}, u32[]{:S(2)}) collective-permute-start(bf16[512,256]{1,0:T(8,128)(2,1)S(1)} %get-tuple-element.52), channel_id=1, source_target_pairs={{0,64},{1,65},{2,66},{3,67},{4,68},{5,69},{6,70},{7,71},{8,72},{9,... | collective-permute-start | bytes 786440 | tf_op jit(solution)/shard_map/ppermute | solution.py:70
